TPU v7x, 128 devices: a whole 4x4x4 slice. The times are simulated.
128 devices in a mesh: head: 4 (over x), blk: 32 (over y, z, core).
Axes of the slice: x: 4, y: 4, z: 4, core: 2. Of those that a mesh axis runs over, the one named last changes fastest.
Arguments:
- tokens: bfloat16 [16384, 1024], P(('blk', 'head')), may hold values from -6 to 6
- gain_one: bfloat16 [1024], P(('head', 'blk')), may hold values from 0.5 to 1.5
- w_query: bfloat16 [1024, 1024], P(('head', 'blk')), may hold values from -0.25 to 0.25
- w_key: bfloat16 [1024, 512], P(('head', 'blk')), may hold values from -0.25 to 0.25
- w_value: bfloat16 [1024, 512], P(('head', 'blk')), may hold values from -0.1875 to 0.1875
- w_out: bfloat16 [1024, 1024], P(('head', 'blk')), may hold values from -1 to 1
- gain_two: bfloat16 [1024], P(('head', 'blk')), may hold values from 0.5 to 1.5
- w_router: bfloat16 [1024, 32], P(('head', 'blk')), may hold values from -0.09375 to 0.09375
- w_gate: bfloat16 [32, 1024, 512], P('blk'), may hold values from -0.1875 to 0.1875
- w_up: bfloat16 [32, 1024, 512], P('blk'), may hold values from -0.1875 to 0.1875
- w_down: bfloat16 [32, 512, 1024], P('blk'), may hold values from -1 to 1
- dealt_order: int32 [16384], replicated, may hold values from 0 to 16383, as said below
- lengths: int32 [5], replicated, may hold values from 1024 to 8192, as said below
- routes: int32 [16384, 8], P(('blk', 'head')), may hold values from 0 to 31, all different within a row; in each aligned block of 128 rows (0 to 127, 128 to 255, ...) at most 36 rows name the same one
- cotangent: bfloat16 [16384, 1024], P(('blk', 'head')), may hold values from -6 to 6
Outputs:
- mixed: bfloat16 [16384, 1024], P(('blk', 'head'))
- grad_tokens: float32 [16384, 1024], P(('blk', 'head'))
- grad_gain_one: float32 [1024], P(('head', 'blk'))
- grad_query: float32 [1024, 1024], P(('head', 'blk'))
- grad_key: float32 [1024, 512], P(('head', 'blk'))
- grad_value: float32 [1024, 512], P(('head', 'blk'))
- grad_out: float32 [1024, 1024], P(('head', 'blk'))
- grad_gain_two: float32 [1024], P(('head', 'blk'))
- grad_router: float32 [1024, 32], P(('head', 'blk'))
- grad_gate: float32 [32, 1024, 512], P('blk', 'head')
- grad_up: float32 [32, 1024, 512], P('blk', 'head')
- grad_down: float32 [32, 512, 1024], P('blk', 'head')
Inputs may be any that keep to these rules, and one draw needn't show every extreme that they name: `dealt_order`: A permutation. Cut the sequence order of the tokens into 64 runs of 256; each aligned block of 512 rows holds some run c < 32 in its first 256 rows and run 2 * 32 - 1 - c in the others, each in its own order; which c lies in which block varies. `lengths`: the sequences lie end to end and sum to 16384; the first or the last has 8192. `routes`: each row names 8 different experts; in the rows of one device (aligned blocks of 128) no expert is named more than 36 times.
All inputs are finite; a program needn't handle non-finite values.
Results may differ from a plain program's by a relative error of at most 0.028.
Values may be sent and summed in bfloat16 or wider, within the bound.
A program may use at most 192 MiB of HBM per device.

v0:
```python
import functools
import math

import jax
import jax.numpy as jnp
import ml_dtypes
import numpy as np
from jax import lax
from jax.experimental import pallas as pl
from jax.experimental.pallas import tpu as pltpu
from jax.sharding import Mesh
from jax.sharding import PartitionSpec as P

D = 1024
HEADS = 16
KV_HEADS = 8
HEAD_DIM = 64
EXPERTS = 32
FF = 512
CAP = 36
SLOT = 40
SLOTS = EXPERTS * SLOT
ROWS = 128
CHIP_ROWS = 1024
RUN = 256
TOKENS = 16384
NSEQ = 5
EPSILON = 1e-06
ROPE_BASE = 10000.0
FAR = float(2.0**100)
SIZE = {"x": 4, "y": 4, "z": 4, "c": 2}
AXES = ("x", "y", "z", "c")
MESH = pl.DeviceIdType.MESH
BF16 = jnp.bfloat16
F32 = jnp.float32
NN = (((1,), (0,)), ((), ()))
NT = (((1,), (1,)), ((), ()))
TN = (((0,), (0,)), ((), ()))
VMEM_BYTES = 56 * 1024 * 1024


def mm(a, b, dims=NN):
    return lax.dot_general(a, b, dims, preferred_element_type=F32)


def halves(value):
    high = value.astype(BF16)
    return high, (value - high.astype(F32)).astype(BF16)


def local_call(kernel, outs, scratch=(), grid=None, in_specs=None, out_specs=None):
    extra = {}
    if grid is not None:
        extra = {"grid": grid, "in_specs": in_specs, "out_specs": out_specs}
    elif in_specs is not None:
        extra = {"in_specs": in_specs}
    return pl.pallas_call(
        kernel,
        out_shape=outs,
        scratch_shapes=list(scratch),
        compiler_params=pltpu.CompilerParams(vmem_limit_bytes=VMEM_BYTES),
        **extra,
    )


def flat_index(coords, order):
    index = 0
    for axis in order:
        index = index * SIZE[axis] + coords[axis]
    return index


PLANE_ORDER = (
    (2, 2), (2, 3), (2, 1), (3, 2), (1, 2), (0, 2), (2, 0), (3, 1), (1, 3),
    (3, 3), (1, 1), (0, 3), (0, 1), (3, 0), (1, 0), (0, 0),
)
PLANE_OFFSETS = tuple({"y": dy, "z": dz} for dy, dz in PLANE_ORDER[:-1])
SPREAD_OFFSETS = tuple(
    {"y": dy, "z": dz, "c": (dc + i + 1) % 2}
    for i, (dy, dz) in enumerate(PLANE_ORDER)
    for dc in range(2)
    if (dy, dz, (dc + i + 1) % 2) != (0, 0, 0)
)
LINE_OFFSETS = tuple(
    {"x": dx, "c": dc} for dx, dc in ((2, 0), (2, 1), (1, 0), (3, 0), (1, 1), (3, 1), (0, 1))
)
OFFSETS = {("y", "z"): PLANE_OFFSETS, ("y", "z", "c"): SPREAD_OFFSETS, ("x", "c"): LINE_OFFSETS}


def position(axes):
    return {axis: lax.axis_index(axis) for axis in axes}


def moved(me, offset):
    return {axis: lax.rem(me[axis] + by, SIZE[axis]) if by else me[axis] for axis, by in offset.items()}


def greet(me, offsets):
    barrier = pltpu.get_barrier_semaphore()
    for offset in offsets:
        pl.semaphore_signal(barrier, inc=1, device_id=moved(me, offset), device_id_type=MESH)
    pl.semaphore_wait(barrier, len(offsets))


def remote(src, dst, send, recv, slot, to):
    return pltpu.make_async_remote_copy(
        src_ref=src,
        dst_ref=dst,
        send_sem=send.at[slot],
        recv_sem=recv.at[slot],
        device_id=to,
        device_id_type=MESH,
    )


def exchange_kernel(axes, dest_order, src_order, arrays, *refs):
    x_refs, o_refs = refs[:arrays], refs[arrays : 2 * arrays]
    send, recv, local = refs[2 * arrays :]
    me = position(axes)
    offsets = OFFSETS[axes]
    greet(me, offsets)
    here = flat_index(me, src_order)
    copies = []
    for offset in offsets:
        to = moved(me, offset)
        for x_ref, o_ref in zip(x_refs, o_refs):
            copies.append(
                remote(
                    x_ref.at[flat_index(to, dest_order)], o_ref.at[here], send, recv, len(copies), to
                )
            )
            copies[-1].start()
    kept = [
        pltpu.make_async_copy(
            x_ref.at[flat_index(me, dest_order)], o_ref.at[here], local.at[i]
        )
        for i, (x_ref, o_ref) in enumerate(zip(x_refs, o_refs))
    ]
    for item in kept:
        item.start()
    for item in kept + copies:
        item.wait()


def exchange(data, axes, cid, dest_order=None, src_order=None):
    single = not isinstance(data, (tuple, list))
    data = [data] if single else list(data)
    dest_order = dest_order or axes
    src_order = src_order or axes
    arrays = len(data)
    count = len(OFFSETS[axes]) * arrays
    out = pl.pallas_call(
        functools.partial(exchange_kernel, axes, dest_order, src_order, arrays),
        out_shape=[jax.ShapeDtypeStruct(item.shape, item.dtype) for item in data],
        in_specs=[pl.BlockSpec(memory_space=pl.ANY)] * arrays,
        out_specs=[pl.BlockSpec(memory_space=pl.ANY)] * arrays,
        scratch_shapes=[
            pltpu.SemaphoreType.DMA((count,)),
            pltpu.SemaphoreType.DMA((count,)),
            pltpu.SemaphoreType.DMA((arrays,)),
        ],
        compiler_params=pltpu.CompilerParams(collective_id=cid, has_side_effects=True),
    )(*data)
    return out[0] if single else out


def start_kernel(tok_ref, w_ref, o_tok, o_w, send, recv, local):
    me = position(AXES)
    x, y, z, c = (me[axis] for axis in AXES)
    offsets = LINE_OFFSETS + PLANE_OFFSETS
    greet(me, offsets)
    plus, minus, far = lax.rem(x + 1, 4), lax.rem(x + 3, 4), lax.rem(x + 2, 4)
    other = 1 - c
    lower, upper = pl.ds(0, 64), pl.ds(64, 64)
    used = [0]

    def go(src, dst, to):
        item = remote(src, dst, send, recv, used[0], to)
        used[0] += 1
        item.start()
        return item

    own_tok = pltpu.make_async_copy(tok_ref, o_tok.at[c, x], local.at[0])
    own_w = pltpu.make_async_copy(w_ref.at[x * 2 + c], o_w.at[x, y, z, c], local.at[1])
    own_tok.start()
    own_w.start()
    first_w = []
    for offset in LINE_OFFSETS:
        to = moved(me, offset)
        first_w.append(go(w_ref.at[to["x"] * 2 + to["c"]], o_w.at[x, y, z, c], to))
    to_plus = go(tok_ref, o_tok.at[c, x], {"x": plus})
    to_minus = go(tok_ref, o_tok.at[c, x], {"x": minus})
    sides = [go(tok_ref, o_tok.at[c, x], {"c": other})]
    own_w.wait()
    for item in first_w:
        item.wait()
    second_w = [
        go(o_w.at[:, y, z], o_w.at[:, y, z], moved(me, offset)) for offset in PLANE_OFFSETS
    ]
    to_plus.wait()
    next_plus = go(o_tok.at[c, minus, lower], o_tok.at[c, minus, lower], {"x": plus})
    sides.append(go(o_tok.at[c, minus], o_tok.at[c, minus], {"c": other}))
    to_minus.wait()
    next_minus = go(o_tok.at[c, plus, upper], o_tok.at[c, plus, upper], {"x": minus})
    sides.append(go(o_tok.at[c, plus], o_tok.at[c, plus], {"c": other}))
    next_plus.wait()
    next_minus.wait()
    sides.append(go(o_tok.at[c, far], o_tok.at[c, far], {"c": other}))
    for item in sides + second_w + [own_tok]:
        item.wait()


def start_rows(tokens, packed, cid):
    count = 3 + 7 + 15 + 2 + 3
    rows, weights = pl.pallas_call(
        start_kernel,
        out_shape=[
            jax.ShapeDtypeStruct((2, 4, ROWS, D), BF16),
            jax.ShapeDtypeStruct((4, 4, 4, 2, 8, 384), BF16),
        ],
        in_specs=[pl.BlockSpec(memory_space=pl.ANY)] * 2,
        out_specs=[pl.BlockSpec(memory_space=pl.ANY)] * 2,
        scratch_shapes=[
            pltpu.SemaphoreType.DMA((count,)),
            pltpu.SemaphoreType.DMA((count,)),
            pltpu.SemaphoreType.DMA((2,)),
        ],
        compiler_params=pltpu.CompilerParams(collective_id=cid, has_side_effects=True),
    )(tokens, packed)
    return rows.reshape(CHIP_ROWS, D), weights.reshape(D, 384)


AROUND = ({"y": 1, "z": 0}, {"y": 3, "z": 0}, {"y": 0, "z": 1}, {"y": 0, "z": 3})


def gather_plane_kernel(x_ref, o_ref, send, recv, local):
    me = position(("y", "z"))
    y, z = me["y"], me["z"]
    greet(me, AROUND)
    own = pltpu.make_async_copy(x_ref, o_ref.at[y, z], local)
    own.start()
    half = x_ref.shape[1] // 2
    lower, upper = pl.ds(0, half), pl.ds(half, half)
    used = [0]

    def go(src, dst, to):
        item = remote(src, dst, send, recv, used[0], to)
        used[0] += 1
        item.start()
        return item

    def place(t, a, b):
        return o_ref.at[a, b, 0] if t == 0 else o_ref.at[b, a, 1]

    axis = (("y", "z"), ("z", "y"))
    here = tuple((me[a], me[b]) for a, b in axis)
    step = {"plus": 1, "minus": 3, "far": 2, "own": 0}

    def at(t, which, name):
        return lax.rem(here[t][which] + step[name], 4)

    def send_second(t, src, name):
        dst = place(t, at(t, 0, name), here[t][1])
        src = dst if src is None else src
        return (
            go(src, dst, {axis[t][1]: at(t, 1, "plus")}),
            go(src, dst, {axis[t][1]: at(t, 1, "minus")}),
        )

    def pass_on(t, which, a_name, b_name, part, direction):
        ref = place(t, at(t, 0, a_name), at(t, 1, b_name)).at[part]
        return go(ref, ref, {axis[t][which]: at(t, which, direction)})

    def forward_second(t, name, pair):
        pair[0].wait()
        a = pass_on(t, 1, name, "minus", lower, "plus")
        pair[1].wait()
        b = pass_on(t, 1, name, "plus", upper, "minus")
        return [a, b]

    first, second, last = {}, {}, []
    for t in (0, 1):
        dst = place(t, *here[t])
        first[t] = (
            go(x_ref.at[t], dst, {axis[t][0]: at(t, 0, "plus")}),
            go(x_ref.at[t], dst, {axis[t][0]: at(t, 0, "minus")}),
        )
    for t in (0, 1):
        second[t, "own"] = send_second(t, x_ref.at[t], "own")
    far = {}
    for t in (0, 1):
        first[t][0].wait()
        a = pass_on(t, 0, "minus", "own", lower, "plus")
        second[t, "minus"] = send_second(t, None, "minus")
        first[t][1].wait()
        b = pass_on(t, 0, "plus", "own", upper, "minus")
        second[t, "plus"] = send_second(t, None, "plus")
        far[t] = (a, b)
    for t in (0, 1):
        last += forward_second(t, "own", second[t, "own"])
    for t in (0, 1):
        far[t][0].wait()
        far[t][1].wait()
        second[t, "far"] = send_second(t, None, "far")
    for name in ("minus", "plus", "far"):
        for t in (0, 1):
            last += forward_second(t, name, second[t, name])
    for item in last + [own]:
        item.wait()


def gather_plane(data, cid):
    rows = data.shape[0] // 2
    out = pl.pallas_call(
        gather_plane_kernel,
        out_shape=jax.ShapeDtypeStruct((4, 4, 2, rows, 128), data.dtype),
        in_specs=[pl.BlockSpec(memory_space=pl.ANY)],
        out_specs=pl.BlockSpec(memory_space=pl.ANY),
        scratch_shapes=[
            pltpu.SemaphoreType.DMA((40,)),
            pltpu.SemaphoreType.DMA((40,)),
            pltpu.SemaphoreType.DMA,
        ],
        compiler_params=pltpu.CompilerParams(collective_id=cid, has_side_effects=True),
    )(data.reshape(2, rows, 128))
    return out.reshape(32 * rows, 128)


def scatter_plane_kernel(p_ref, sent_ref, branch_ref, o_ref, grad_ref, far_a, near_a, out_a, sum_a, far_b, near_b, out_b, send, recv):
    me = position(("y", "z"))
    greet(me, AROUND)
    half = p_ref.shape[3] // 2
    lower, upper = pl.ds(0, half), pl.ds(half, half)
    axis = (("y", "z"), ("z", "y"))
    used = [0]

    def go(src, dst, t, which, by):
        to = {axis[t][which]: lax.rem(me[axis[t][which]] + by, 4)}
        item = remote(src, dst, send, recv, used[0], to)
        used[0] += 1
        item.start()
        return item

    def part(t, first, second):
        a = lax.rem(me[axis[t][0]] + first, 4)
        b = lax.rem(me[axis[t][1]] + second, 4)
        return p_ref.at[a, b, 0] if t == 0 else p_ref.at[b, a, 1]

    turns = (2, 1, 3, 0)
    both = (0, 1)
    far, near = {}, {}
    for k, by in enumerate(turns):
        for t in both:
            far[k, t] = (
                go(part(t, 2, by).at[lower], far_a.at[t, k, 0], t, 0, 1),
                go(part(t, 2, by).at[upper], far_a.at[t, k, 1], t, 0, 3),
            )
    grad_ref[...] = mm(sent_ref[...], branch_ref[...], TN)
    for k, by in enumerate(turns):
        for t in both:
            ahead, behind = part(t, 1, by), part(t, 3, by)
            far[k, t][0].wait()
            out_a[t, k, 0, 0:half] = (ahead[0:half].astype(F32) + far_a[t, k, 0].astype(F32)).astype(BF16)
            out_a[t, k, 0, half : 2 * half] = ahead[half : 2 * half]
            first = go(out_a.at[t, k, 0], near_a.at[t, k, 0], t, 0, 1)
            far[k, t][1].wait()
            out_a[t, k, 1, 0:half] = behind[0:half]
            out_a[t, k, 1, half : 2 * half] = (
                behind[half : 2 * half].astype(F32) + far_a[t, k, 1].astype(F32)
            ).astype(BF16)
            near[k, t] = (first, go(out_a.at[t, k, 1], near_a.at[t, k, 1], t, 0, 3))

    def summed(k, t):
        near[k, t][0].wait()
        near[k, t][1].wait()
        return (
            part(t, 0, turns[k])[...].astype(F32)
            + near_a[t, k, 0].astype(F32)
            + near_a[t, k, 1].astype(F32)
        )

    far_two, near_two = {}, {}
    for t in both:
        value = summed(0, t).astype(BF16)
        out_b[t, 0] = value
        far_two[t] = (
            go(out_b.at[t, 0, lower], far_b.at[t, 0], t, 1, 1),
            go(out_b.at[t, 0, upper], far_b.at[t, 1], t, 1, 3),
        )
    for k in (1, 2):
        for t in both:
            sum_a[t, k - 1] = summed(k, t)
    for t in both:
        far_two[t][0].wait()
        out_b[t, 1, 0:half] = (sum_a[t, 0, 0:half] + far_b[t, 0].astype(F32)).astype(BF16)
        out_b[t, 1, half : 2 * half] = sum_a[t, 0, half : 2 * half].astype(BF16)
        first = go(out_b.at[t, 1], near_b.at[t, 0], t, 1, 1)
        far_two[t][1].wait()
        out_b[t, 2, 0:half] = sum_a[t, 1, 0:half].astype(BF16)
        out_b[t, 2, half : 2 * half] = (
            sum_a[t, 1, half : 2 * half] + far_b[t, 1].astype(F32)
        ).astype(BF16)
        near_two[t] = (first, go(out_b.at[t, 2], near_b.at[t, 1], t, 1, 3))
    for t in both:
        value = summed(3, t)
        near_two[t][0].wait()
        near_two[t][1].wait()
        o_ref[t] = value + near_b[t, 0].astype(F32) + near_b[t, 1].astype(F32)


def scatter_plane(data, sent, branch_rows, cid):
    rows = data.shape[0] // 32
    whole = pl.BlockSpec(memory_space=pltpu.VMEM)
    out, grad_out = pl.pallas_call(
        scatter_plane_kernel,
        out_shape=[
            jax.ShapeDtypeStruct((2, rows, 128), F32),
            jax.ShapeDtypeStruct((ROWS, D), F32),
        ],
        in_specs=[whole] * 3,
        out_specs=[whole] * 2,
        scratch_shapes=[
            pltpu.VMEM((2, 4, 2, rows // 2, 128), BF16),
            pltpu.VMEM((2, 4, 2, rows, 128), BF16),
            pltpu.VMEM((2, 4, 2, rows, 128), BF16),
            pltpu.VMEM((2, 2, rows, 128), F32),
            pltpu.VMEM((2, 2, rows // 2, 128), BF16),
            pltpu.VMEM((2, 2, rows, 128), BF16),
            pltpu.VMEM((2, 3, rows, 128), BF16),
            pltpu.SemaphoreType.DMA((40,)),
            pltpu.SemaphoreType.DMA((40,)),
        ],
        compiler_params=pltpu.CompilerParams(
            collective_id=cid, has_side_effects=True, vmem_limit_bytes=VMEM_BYTES
        ),
    )(data.reshape(4, 4, 2, rows, 128), sent, branch_rows)
    return out.reshape(2 * rows, 128), grad_out


def lane_index(shape):
    return lax.broadcasted_iota(jnp.int32, shape, 1)


def turned(values):
    lane = lane_index(values.shape)
    up = pltpu.roll(values, 32, axis=1)
    down = pltpu.roll(values, 96, axis=1)
    return jnp.where(lane % 64 < 32, -down, up)


def project_kernel(tok_ref, w_ref, cos_ref, sin_ref, normed_ref, q_ref, kv_ref, gain_ref):
    gain = w_ref[:, 256:384].astype(F32).T[0:1, :]
    gain_ref[...] = gain
    for part in range(4):
        rows = pl.ds(part * 256, 256)
        tok = tok_ref[rows, :].astype(F32)
        scale = lax.rsqrt(jnp.mean(tok * tok, axis=-1, keepdims=True) + EPSILON)
        normed = (tok * scale * gain).astype(BF16)
        normed_ref[rows, :] = normed
        pre = mm(normed, w_ref[:, 0:256])
        cos, sin = cos_ref[rows, :], sin_ref[rows, :]
        low_lanes = lane_index((256, 128)) < 64
        q_pre, kv_pre = pre[:, :128], pre[:, 128:]
        query = (q_pre * cos + turned(q_pre) * sin).astype(BF16).astype(F32) * 0.125
        q_ref[0, rows, :] = jnp.where(low_lanes, query, 0.0).astype(BF16)
        q_ref[1, rows, :] = jnp.where(low_lanes, pltpu.roll(query, 64, axis=1), 0.0).astype(BF16)
        key = kv_pre * cos + turned(kv_pre) * sin
        kv_ref[rows, :] = jnp.where(low_lanes, key, kv_pre).astype(BF16)


def order_pair(order_ref, index):
    row = jnp.broadcast_to(order_ref[index : index + 1, :], (RUN, RUN))
    return row, row.T


def attend_kernel(
    first_ref, count_ref, kv_ref, aux_ref, own_kv_ref, own_aux_ref, q_ref, order_ref,
    att_ref, norm_ref, sent_ref, qx_ref, acc_ref,
):
    def largest(step, best):
        tile = kv_ref[pl.ds(pl.multiple_of(step * 512, 512), 512), :].astype(F32)
        square = jnp.sum(jnp.where(lane_index((512, 128)) < 64, tile * tile, 0.0), axis=1, keepdims=True)
        return jnp.maximum(best, square)

    best = lax.fori_loop(0, TOKENS // 512, largest, jnp.zeros((512, 1), F32))
    key_norm = jnp.sqrt(jnp.max(best, axis=0, keepdims=True))
    lane = lane_index((RUN, 128))
    lane_tall = lane_index((2 * RUN, 128))

    def weights(keys, aux, qx):
        return jnp.exp(mm(qx, jnp.concatenate([keys, aux], axis=1), NT))

    def right(keys):
        return jnp.where(lane_index(keys.shape) < 64, jnp.ones_like(keys), keys)

    for part in range(4):
        rows = pl.ds(part * RUN, RUN)
        own_aux = own_aux_ref[rows, :].astype(F32)
        for head in range(2):
            query = q_ref[head, rows, :]
            wide = query.astype(F32)
            shift = jnp.ceil(jnp.sqrt(jnp.sum(wide * wide, axis=1, keepdims=True)) * key_norm)
            top = shift.astype(BF16).astype(F32)
            middle = (shift - top).astype(BF16).astype(F32)
            rest = shift - top - middle
            ext = jnp.where(lane < 3 + NSEQ, (own_aux - 1.0) * FAR, 0.0)
            ext = jnp.where(lane == 0, -top, ext)
            ext = jnp.where(lane == 1, -middle, ext)
            ext = jnp.where(lane == 2, -rest, ext)
            here = pl.ds(head * RUN, RUN)
            qx_ref[part, here, 0:128] = query
            qx_ref[part, here, 128:256] = ext.astype(BF16)
        qx = qx_ref[part]
        order_key, order_query = order_pair(order_ref, part)
        allowed = order_key <= order_query
        keys = own_kv_ref[rows, :]
        e = weights(keys, own_aux_ref[rows, :], qx)
        e = jnp.where(jnp.concatenate([allowed, allowed], axis=0), e, 0.0)
        acc_ref[...] = mm(e.astype(BF16), right(keys))
        base = (part % 2) * 32

        def tiles(step):
            start = pl.multiple_of(first_ref[base + step], RUN)
            return kv_ref[pl.ds(start, RUN), :], aux_ref[pl.ds(start, RUN), :]

        def pair(step, carry):
            keys_a, aux_a = tiles(2 * step)
            keys_b, aux_b = tiles(2 * step + 1)
            keys = jnp.concatenate([keys_a, keys_b], axis=0)
            aux = jnp.concatenate([aux_a, aux_b], axis=0)
            acc_ref[...] += mm(weights(keys, aux, qx).astype(BF16), right(keys))
            return carry

        number = count_ref[part]
        lax.fori_loop(0, number // 2, pair, 0)

        @pl.when(number % 2 == 1)
        def _():
            keys, aux = tiles(number - 1)
            acc_ref[...] += mm(weights(keys, aux, qx).astype(BF16), right(keys))

        total = acc_ref[...]
        other = pltpu.roll(total, 64, axis=1)
        norm = jnp.where(lane_tall < 64, total, other)
        value = jnp.where(lane_tall < 64, other, total) / norm
        low_lanes = lane < 64
        att = jnp.where(low_lanes, value[:RUN], value[RUN:])
        att_ref[rows, :] = att
        norm_ref[rows, :] = jnp.where(low_lanes, norm[:RUN], norm[RUN:])
        sent_ref[rows, :] = att.astype(BF16)


def attend_back_kernel(
    first_ref, count_ref, base_ref, kv_ref, aux_ref, own_kv_ref, own_aux_ref, qx_ref, order_ref,
    gsent_ref, att_ref, norm_ref, dq_ref, dkv_ref, acc_ref, dq_acc, gx_ref, rhs_ref,
):
    def clear(step, carry):
        acc_ref[pl.ds(pl.multiple_of(step * 512, 512), 512), :] = jnp.zeros((512, 128), F32)
        return carry

    lax.fori_loop(0, TOKENS // 512, clear, 0)
    lane = lane_index((RUN, 128))
    low_lanes = lane < 64
    for part in range(4):
        rows = pl.ds(part * RUN, RUN)
        gsent = gsent_ref[rows, :].astype(F32)
        norm = norm_ref[rows, :]
        product = gsent * att_ref[rows, :] / norm
        scaled = (gsent / norm).astype(BF16).astype(F32)
        for head in range(2):
            mask = low_lanes if head == 0 else jnp.logical_not(low_lanes)
            delta = jnp.sum(jnp.where(mask, product, 0.0), axis=1, keepdims=True)
            top = delta.astype(BF16).astype(F32)
            middle = (delta - top).astype(BF16).astype(F32)
            rest = delta - top - middle
            ext = jnp.where(lane == 0, -top, 0.0)
            ext = jnp.where(lane == 1, -middle, ext)
            ext = jnp.where(lane == 2, -rest, ext)
            grad = pltpu.roll(scaled, 64, axis=1) if head == 0 else scaled
            grad = jnp.where(low_lanes, 0.0, grad).astype(BF16)
            here = pl.ds(head * RUN, RUN)
            gx_ref[here, 0:128] = grad
            gx_ref[here, 128:256] = ext.astype(BF16)
            rhs_ref[pl.ds(head * RUN, RUN), :] = qx_ref[part, here, 0:128]
            rhs_ref[pl.ds((2 + head) * RUN, RUN), :] = grad
        order_key, order_query = order_pair(order_ref, part)
        allowed = order_query <= order_key
        dq_acc[...] = jnp.zeros_like(dq_acc)

        def tile(start, keys, aux, mask):
            both = jnp.concatenate([keys, aux], axis=1)
            e = jnp.exp(mm(both, qx_ref[part], NT))
            if mask is not None:
                e = jnp.where(mask, e, 0.0)
            ds = (e * mm(both, gx_ref[...], NT)).astype(BF16)
            left = jnp.concatenate([ds, e.astype(BF16)], axis=1)
            acc_ref[pl.ds(start, RUN), :] += mm(left, rhs_ref[...])
            dq_acc[...] += mm(keys.T[:64], ds)

        tile(
            pl.multiple_of(base_ref[0] + part * RUN, RUN),
            own_kv_ref[rows, :],
            own_aux_ref[rows, :],
            jnp.concatenate([allowed, allowed], axis=1),
        )
        base = (part % 2) * 32

        def step_tile(step, carry):
            start = pl.multiple_of(first_ref[base + step], RUN)
            tile(start, kv_ref[pl.ds(start, RUN), :], aux_ref[pl.ds(start, RUN), :], None)
            return carry

        lax.fori_loop(0, count_ref[part], step_tile, 0)
        total = dq_acc[...] * 0.125
        dq_ref[rows, :] = jnp.concatenate([total[:, :RUN], total[:, RUN:]], axis=0).T

    def finish(step, carry):
        rows = pl.ds(pl.multiple_of(step * 512, 512), 512)
        dkv_ref[rows, :] = acc_ref[rows, :].astype(BF16)
        return carry

    lax.fori_loop(0, TOKENS // 512, finish, 0)


SLOT_EXPERT = np.arange(SLOTS) // SLOT
SLOT_PLACE = np.arange(SLOTS) % SLOT


def constant(array):
    return jnp.asarray(np.asarray(array).astype(ml_dtypes.bfloat16))


def expand_matrix():
    return constant(np.arange(128)[:, None] == SLOT_EXPERT[None, :])


def place_matrix():
    return constant(SLOT_PLACE[:, None] == np.arange(128)[None, :])


def pick_matrix(place):
    return constant((SLOT_EXPERT[:, None] == np.arange(128)[None, :]) & (SLOT_PLACE[:, None] == place))


def place_column():
    used = np.where(SLOT_PLACE < CAP, SLOT_PLACE, -5)
    return constant(np.broadcast_to(used[:, None], (SLOTS, 128)))


def place_row():
    used = np.where(SLOT_PLACE < CAP, SLOT_PLACE, -5)
    return jnp.asarray(used[None, :].astype(np.float32))


def prepare_kernel(routes_ref, cot_ref, expand_ref, expand_t_ref, col_ref, row_ref, member_ref, put_ref, take_ref, out_ref):
    lane = lane_index((ROWS, 128))
    routes = routes_ref[...]
    member = jnp.zeros((ROWS, 128), F32)
    for choice in range(8):
        member += jnp.where(routes[:, choice : choice + 1] == lane, 1.0, 0.0)
    below = lax.broadcasted_iota(jnp.int32, (ROWS, ROWS), 0) > lane_index((ROWS, ROWS))
    earlier = mm(jnp.where(below, 1.0, 0.0).astype(BF16), member.astype(BF16))
    slot = jnp.where(member > 0.5, earlier, -1.0).astype(BF16)
    member_ref[...] = member
    take = jnp.where(mm(slot, expand_ref[...]) == row_ref[...], 1.0, 0.0)
    take_ref[...] = take.astype(BF16)
    put = jnp.where(mm(expand_t_ref[...], slot, NT) == col_ref[...].astype(F32), 1.0, 0.0)
    put = put.astype(BF16)
    put_ref[...] = put
    for part in range(4):
        columns = pl.ds(part * 256, 256)
        out_ref[:, columns] = mm(put, cot_ref[:, columns]).astype(BF16)


BLOCK = 8 * SLOT
BLOCK_SOURCE = np.arange(BLOCK) // SLOT
BLOCK_PLACE = np.arange(BLOCK) % SLOT


def block_matrix(places):
    hit = np.isin(BLOCK_PLACE, places)[None, :] & (BLOCK_SOURCE[:, None] == BLOCK_SOURCE[None, :])
    return constant(hit)


def packed_pairs(values):
    total = sum(int(value) << (2 * i) for i, value in enumerate(values))
    return np.uint32(total).astype(np.int32)


STEP_Y = packed_pairs([dy for dy, _ in PLANE_ORDER])
STEP_Z = packed_pairs([dz for _, dz in PLANE_ORDER])


def moe_kernel(
    sent_ref, tok_ref, w_out_ref, router_ref, member_ref, put_ref, take_ref, expand_ref,
    expand_t_ref, place_ref, place_t_ref, pick_high_ref, pick_low_ref, pick_t_ref, cot_ref,
    select_ref, block_place_ref, high_ref, low_ref, g_hbm, gate_hbm, up_hbm, down_hbm,
    residual_ref, weigh_high_ref, weigh_low_ref, gmid_ref, branch_ref, gsent_in, side_in,
    y_hbm, grad_gate_hbm, grad_up_hbm, grad_down_hbm,
    sent_in, x_out, x_in, g_v, y_v, back_out, back_in, gate_v, up_v, down_v,
    sum_gate, sum_up, sum_down, grad_gate, grad_up, grad_down, mixed_v, gate_probs, gsent_out, side_out,
    x_send, x_recv, back_send, back_recv, line_send, line_recv, local,
):
    me = position(AXES)
    x_at, y_at, z_at, c_at = (me[axis] for axis in AXES)
    expert = (y_at * 4 + z_at) * 2 + c_at

    def offset(k):
        pair = lax.div(k, 2)
        dy = lax.shift_right_logical(jnp.int32(STEP_Y), 2 * pair) & 3
        dz = lax.shift_right_logical(jnp.int32(STEP_Z), 2 * pair) & 3
        return dy, dz, lax.rem(k + pair, 2)

    def toward(k):
        dy, dz, dc = offset(k)
        return {"y": lax.rem(y_at + dy, 4), "z": lax.rem(z_at + dz, 4), "c": lax.rem(c_at + dc, 2)}

    def source(k):
        dy, dz, dc = offset(k)
        return {
            "y": lax.rem(y_at + 4 - dy, 4),
            "z": lax.rem(z_at + 4 - dz, 4),
            "c": lax.rem(c_at + dc, 2),
        }

    def number(at):
        return (at["y"] * 4 + at["z"]) * 2 + at["c"]

    loads = [
        pltpu.make_async_copy(src, dst, local.at[i])
        for i, (src, dst) in enumerate(
            ((g_hbm, g_v), (gate_hbm, gate_v), (up_hbm, up_v), (down_hbm, down_v))
        )
    ]
    for item in loads:
        item.start()
    barrier = pltpu.get_barrier_semaphore()
    for by in LINE_OFFSETS:
        pl.semaphore_signal(barrier, inc=1, device_id=moved(me, by), device_id_type=MESH)

    def hello(k, carry):
        pl.semaphore_signal(barrier, inc=1, device_id=toward(k), device_id_type=MESH)
        return carry

    lax.fori_loop(0, 31, hello, 0)
    pl.semaphore_wait(barrier, 31 + len(LINE_OFFSETS))

    here_line = x_at * 2 + c_at
    moves = []
    for i, by in enumerate(LINE_OFFSETS):
        to = moved(me, by)
        moves.append(
            remote(sent_ref.at[to["c"] * 4 + to["x"]], sent_in.at[here_line], line_send, line_recv, i, to)
        )
        moves[-1].start()
    kept = pltpu.make_async_copy(sent_ref.at[c_at * 4 + x_at], sent_in.at[here_line], local.at[4])
    kept.start()
    for item in moves + [kept]:
        item.wait()
    sent = jnp.concatenate([sent_in[i] for i in range(8)], axis=1)
    residual = tok_ref[...].astype(F32) + mm(sent, w_out_ref[...])
    residual_ref[...] = residual
    gain = router_ref[...].astype(F32).T[EXPERTS : EXPERTS + 1, :]
    scale = lax.rsqrt(jnp.mean(residual * residual, axis=-1, keepdims=True) + EPSILON)
    mixed = (residual * scale * gain).astype(BF16)
    mixed_v[...] = mixed
    logits = mm(mixed, router_ref[...])
    member = member_ref[...]
    masked = jnp.where(member > 0.5, logits, -FAR)
    top = jnp.max(masked, axis=1, keepdims=True)
    power = jnp.where(member > 0.5, jnp.exp(masked - top), 0.0)
    gate = power / jnp.sum(power, axis=1, keepdims=True)
    gate_probs[...] = gate
    gate_high, gate_low = halves(gate)
    spread = mm(gate_high, expand_ref[...]) + mm(gate_low, expand_ref[...])
    weigh = take_ref[...].astype(F32) * spread
    weigh_high, weigh_low = halves(weigh)
    weigh_high_ref[...] = weigh_high
    weigh_low_ref[...] = weigh_low
    total = jnp.sum(weigh, axis=0, keepdims=True)
    rows_high, rows_low = halves(expand_ref[...].astype(F32) * total)
    rows_high = mm(rows_high, place_ref[...]).astype(BF16)
    rows_low = mm(rows_low, place_ref[...]).astype(BF16)
    gate_rows = mm(pick_high_ref[...], rows_high) + mm(pick_low_ref[...], rows_low)
    put = put_ref[...]

    def slots(value):
        return value.reshape(EXPERTS, SLOT, value.shape[1]).astype(BF16)

    x_out[:, :, 0:128] = slots(mm(put, mixed[:, 0:128]) + gate_rows)
    x_out[:, :, 128:512] = slots(mm(put, mixed[:, 128:512]))
    x_out[:, :, 512:1024] = slots(mm(put, mixed[:, 512:1024]))

    def x_copy(k):
        to = toward(k)
        return remote(x_out.at[number(to)], x_in.at[k], x_send, x_recv, k, to)

    def x_start(k, carry):
        x_copy(k).start()
        return carry

    lax.fori_loop(0, 31, x_start, 0)
    kept = pltpu.make_async_copy(x_out.at[expert], x_in.at[31], local.at[4])
    kept.start()
    kept.wait()
    sum_gate[...] = jnp.zeros_like(sum_gate)
    sum_up[...] = jnp.zeros_like(sum_up)
    sum_down[...] = jnp.zeros_like(sum_down)
    for item in loads:
        item.wait()

    def back_copy(k):
        to = source(k)
        return remote(back_out.at[k], back_in.at[expert], back_send, back_recv, k, to)

    def back_kept():
        return pltpu.make_async_copy(back_out.at[31], back_in.at[expert], local.at[4])

    def group(step, carry):
        first = step * 8
        for i in range(8):
            k = first + i

            @pl.when(k < 31)
            def _():
                x_copy(k).wait_recv()

        x = x_in[pl.ds(first, 8)].astype(F32).reshape(BLOCK, D).astype(BF16)
        g = jnp.concatenate([g_v[number(source(first + i))].astype(F32) for i in range(8)], axis=0)
        place = block_place_ref[...].astype(F32)
        share = jnp.sum(mm(select_ref[...], x[:, :128]) * place, axis=1, keepdims=True)
        a = mm(x, gate_v[...])
        b = mm(x, up_v[...])
        s = 1.0 / (1.0 + jnp.exp(-a))
        silu = a * s
        hidden = (silu * b).astype(BF16)
        y = mm(hidden, down_v[...]).astype(BF16).astype(F32)
        dgate = jnp.sum(y * g, axis=1, keepdims=True)
        y = y.reshape(8, SLOT, D)
        for i in range(8):
            y_v[number(source(first + i))] = y[i].astype(BF16)
        gy = (g * share).astype(BF16)
        dhidden = mm(gy, down_v[...], NT)
        da = (dhidden * b * (s * (1.0 + a * (1.0 - s)))).astype(BF16)
        db = (dhidden * silu).astype(BF16)
        back = mm(da, gate_v[...], NT) + mm(db, up_v[...], NT)
        dgate_high, dgate_low = halves(dgate * place)
        lead = back[:, 0:128] + mm(high_ref[...], dgate_high) + mm(low_ref[...], dgate_low)
        span = pl.ds(first, 8)
        back_out[span, :, 0:128] = lead.reshape(8, SLOT, 128).astype(BF16)
        back_out[span, :, 128:1024] = back[:, 128:1024].reshape(8, SLOT, 896).astype(BF16)
        for i in range(8):
            k = first + i

            @pl.when(k < 31)
            def _():
                back_copy(k).start()

            @pl.when(k == 31)
            def _():
                back_kept().start()

        sum_gate[...] += mm(x, da, TN)
        sum_up[...] += mm(x, db, TN)
        sum_down[...] += mm(hidden, gy, TN)
        return carry

    lax.fori_loop(0, 4, group, 0)
    grad_gate[...] = sum_gate[...].astype(BF16)
    grad_up[...] = sum_up[...].astype(BF16)
    grad_down[...] = sum_down[...].astype(BF16)
    stores = [
        pltpu.make_async_copy(src, dst, local.at[i])
        for i, (src, dst) in enumerate(
            ((y_v, y_hbm), (grad_gate, grad_gate_hbm), (grad_up, grad_up_hbm), (grad_down, grad_down_hbm))
        )
    ]
    for item in stores:
        item.start()

    def settle(k, carry):
        x_copy(k).wait_send()
        back_copy(k).wait()
        return carry

    lax.fori_loop(0, 31, settle, 0)
    back_kept().wait()

    take = take_ref[...]
    rows_high, rows_low = halves(
        sum(
            mm(
                pick_t_ref[:, i * 640 : (i + 1) * 640],
                back_in[i * 16 : (i + 1) * 16, :, 0:128].astype(F32).reshape(640, 128).astype(BF16),
            )
            for i in range(2)
        )
    )
    spread = mm(rows_high, place_t_ref[...]) + mm(rows_low, place_t_ref[...])
    along = jnp.sum(spread * expand_ref[...].astype(F32), axis=0, keepdims=True)
    found_high, found_low = halves(take.astype(F32) * along)
    dgate = mm(found_high, expand_t_ref[...]) + mm(found_low, expand_t_ref[...])
    gate = gate_probs[...]
    dlogits = gate * (dgate - jnp.sum(gate * dgate, axis=1, keepdims=True))
    dlogits = dlogits.astype(BF16)
    dmixed = mm(dlogits, router_ref[...], NT)
    for i in range(2):
        rows = back_in[i * 16 : (i + 1) * 16].astype(F32).reshape(640, D).astype(BF16)
        dmixed += mm(take[:, i * 640 : (i + 1) * 640], rows)
    residual = residual_ref[...]
    scale = lax.rsqrt(jnp.mean(residual * residual, axis=-1, keepdims=True) + EPSILON)
    gain = router_ref[...].astype(F32).T[EXPERTS : EXPERTS + 1, :]
    weighted = dmixed * gain
    inner = jnp.mean(weighted * residual, axis=-1, keepdims=True)
    gmid = cot_ref[...].astype(F32) + scale * weighted - residual * (scale * scale * scale) * inner
    gmid_ref[...] = gmid
    branch = gmid.astype(BF16)
    branch_ref[...] = branch
    gsent = mm(branch, w_out_ref[...], NT).astype(BF16)
    for i in range(8):
        gsent_out[i] = gsent[:, i * 128 : (i + 1) * 128]
    back_line = c_at * 4 + x_at
    moves = []
    for i, by in enumerate(LINE_OFFSETS):
        to = moved(me, by)
        moves.append(
            remote(
                gsent_out.at[to["x"] * 2 + to["c"]], gsent_in.at[back_line], line_send, line_recv, 7 + i, to
            )
        )
        moves[-1].start()
    kept = pltpu.make_async_copy(gsent_out.at[here_line], gsent_in.at[back_line], local.at[4])
    kept.start()
    moves.append(kept)
    gain_grad = jnp.sum(dmixed * residual * scale, axis=0, keepdims=True)
    grads = mm(dlogits, mixed_v[...], TN)
    row = lax.broadcasted_iota(jnp.int32, (128, D), 0)
    grads = jnp.where(row == EXPERTS, gain_grad, grads).T.reshape(4, 16, 2, 8, 128)
    for i in range(8):
        side_out[i] = grads[i // 2, :, i % 2].reshape(ROWS, 128).astype(BF16)
    for i, by in enumerate(LINE_OFFSETS):
        to = moved(me, by)
        moves.append(
            remote(
                side_out.at[to["x"] * 2 + to["c"]], side_in.at[back_line], line_send, line_recv, 14 + i, to
            )
        )
        moves[-1].start()
    kept = pltpu.make_async_copy(side_out.at[here_line], side_in.at[back_line], local.at[5])
    kept.start()
    for item in moves + [kept] + stores:
        item.wait()


def moe(inputs, cid):
    vmem = pl.BlockSpec(memory_space=pltpu.VMEM)
    hbm = pl.BlockSpec(memory_space=pl.ANY)
    slots = (EXPERTS, SLOT, D)
    up, down = (D, FF), (FF, D)
    dma = pltpu.SemaphoreType.DMA
    return pl.pallas_call(
        moe_kernel,
        grid=(1,),
        out_shape=[
            shape((ROWS, D), F32),
            shape((ROWS, SLOTS), BF16),
            shape((ROWS, SLOTS), BF16),
            shape((ROWS, D), F32),
            shape((ROWS, D), BF16),
            shape((8, ROWS, 128), BF16),
            shape((8, ROWS, 128), BF16),
            shape(slots, BF16),
            shape(up, BF16),
            shape(up, BF16),
            shape(down, BF16),
        ],
        in_specs=[vmem] * 2 + [OUT_BLOCK, SIDE_BLOCK] + [vmem] * 15 + [hbm] * 4,
        out_specs=[vmem] * 7 + [hbm] * 4,
        scratch_shapes=[
            pltpu.VMEM((8, ROWS, 128), BF16),
            pltpu.VMEM(slots, BF16),
            pltpu.VMEM(slots, BF16),
            pltpu.VMEM(slots, BF16),
            pltpu.VMEM(slots, BF16),
            pltpu.VMEM(slots, BF16),
            pltpu.VMEM(slots, BF16),
            pltpu.VMEM(up, BF16),
            pltpu.VMEM(up, BF16),
            pltpu.VMEM(down, BF16),
            pltpu.VMEM(up, F32),
            pltpu.VMEM(up, F32),
            pltpu.VMEM(down, F32),
            pltpu.VMEM(up, BF16),
            pltpu.VMEM(up, BF16),
            pltpu.VMEM(down, BF16),
            pltpu.VMEM((ROWS, D), BF16),
            pltpu.VMEM((ROWS, 128), F32),
            pltpu.VMEM((8, ROWS, 128), BF16),
            pltpu.VMEM((8, ROWS, 128), BF16),
            dma((31,)),
            dma((31,)),
            dma((31,)),
            dma((31,)),
            dma((21,)),
            dma((21,)),
            dma((6,)),
        ],
        compiler_params=pltpu.CompilerParams(
            collective_id=cid, has_side_effects=True, vmem_limit_bytes=VMEM_BYTES
        ),
    )(*inputs)


def finish_kernel(
    dq_ref, dkv_ref, cos_ref, sin_ref, normed_ref, w_ref,
    y_ref, weigh_high_ref, weigh_low_ref, residual_ref, out_ref, side_ref,
    dnormed_out, mixed_out, grads_out, early_out,
    dqkv, part_out, part_in, part_own, line_out, line_in, share_out, share_in, total,
    out_in, side_in, send, recv, local, out_recv,
):
    me = position(AXES)
    x, y, z, c = (me[axis] for axis in AXES)
    mine = y * 4 + z
    alone = jnp.where(c == lax.div(y, 2), 1, 0)
    barrier = pltpu.get_barrier_semaphore()

    def owner(k):
        at = lax.rem(lax.rem(y, 2) * 8 + z * 2 + c + k, 16)
        to = {"y": 2 * c + lax.div(at, 8), "z": lax.rem(lax.div(at, 2), 4), "c": lax.rem(at, 2)}
        return at, to

    def origin(k):
        at = lax.rem(mine + k, 16)
        return at, {"y": lax.div(at, 4), "z": lax.rem(at, 4), "c": lax.div(y, 2)}

    for k in range(1, 16):
        pl.semaphore_signal(barrier, inc=1, device_id=origin(k)[1], device_id_type=MESH)

    @pl.when(alone == 0)
    def _():
        pl.semaphore_signal(barrier, inc=1, device_id=origin(0)[1], device_id_type=MESH)

    offsets = LINE_OFFSETS + PLANE_OFFSETS
    for offset in offsets:
        pl.semaphore_signal(barrier, inc=1, device_id=moved(me, offset), device_id_type=MESH)
    pl.semaphore_wait(barrier, len(offsets) + 16 - alone)
    used = [0]

    def go(src, dst, to):
        item = remote(src, dst, send, recv, used[0], to)
        used[0] += 1
        item.start()
        return item

    other = 1 - c
    low_lanes = lane_index((256, 128)) < 64

    def out_copy(k):
        at, to = owner(k)
        return pltpu.make_async_remote_copy(
            src_ref=out_ref.at[at], dst_ref=out_in.at[mine], send_sem=send.at[used[0] + k],
            recv_sem=out_recv.at[mine], device_id=to, device_id_type=MESH,
        )

    def out_kept():
        return pltpu.make_async_copy(out_ref.at[owner(0)[0]], out_in.at[mine], local.at[1])

    out_copies = [out_copy(k) for k in range(16)]
    used[0] += 16
    out_arrivals = []
    for k in range(16):
        at, to = origin(k)
        out_arrivals.append(
            pltpu.make_async_remote_copy(
                src_ref=out_ref.at[0], dst_ref=out_in.at[at], send_sem=send.at[0],
                recv_sem=out_recv.at[at], device_id=to, device_id_type=MESH,
            )
        )

    @pl.when(alone == 0)
    def _():
        out_copies[0].start()

    @pl.when(alone == 1)
    def _():
        out_kept().start()

    for item in out_copies[1:]:
        item.start()
    early = []
    for offset in PLANE_OFFSETS:
        to = moved(me, offset)
        early.append(go(side_ref.at[to["y"] * 4 + to["z"]], side_in.at[mine], to))
    side_kept = pltpu.make_async_copy(side_ref.at[mine], side_in.at[mine], local.at[2])
    side_kept.start()
    early.append(side_kept)

    def turn_back(first):
        rows = pl.ds(pl.multiple_of(first, 256), 256)
        cos, sin = cos_ref[rows, :], sin_ref[rows, :]
        dq, dkv = dq_ref[rows, :], dkv_ref[rows, :]
        dq = (dq * cos - turned(dq) * sin).astype(BF16)
        dkv = jnp.where(low_lanes, dkv * cos - turned(dkv) * sin, dkv).astype(BF16)
        both = jnp.concatenate([dq, dkv], axis=1)
        dqkv[rows, :] = both
        return mm(both, w_ref[:, 0:256], NT)

    crossing = []
    for i in range(2):
        value = turn_back(other * 512 + i * 256).astype(BF16)
        part_out[2 * i] = value[:ROWS]
        part_out[2 * i + 1] = value[ROWS:]
        span = pl.ds(2 * i, 2)
        crossing.append(go(part_out.at[span], part_in.at[span], {"c": other}))
    for i in range(2):
        value = turn_back(c * 512 + i * 256)
        part_own[2 * i] = value[:ROWS]
        part_own[2 * i + 1] = value[ROWS:]
    for item in crossing:
        item.wait()
    along = []
    for i, by in enumerate((2, 1, 3)):
        to = lax.rem(x + by, 4)
        line_out[i] = (part_own[to] + part_in[to].astype(F32)).astype(BF16)
        along.append(go(line_out.at[i], line_in.at[i], {"x": to}))
    for i in range(4):
        columns = pl.ds(i * 256, 256)
        grad = mm(normed_ref[:, columns], dqkv[...], TN).astype(BF16)
        share_out[i] = grad.reshape(16, 16, 256)
    spread = []
    for offset in PLANE_OFFSETS:
        to = moved(me, offset)
        spread.append(go(share_out.at[:, to["y"] * 4 + to["z"]], share_in.at[mine], to))
    kept = pltpu.make_async_copy(share_out.at[:, mine], share_in.at[mine], local.at[0])
    kept.start()
    mixed = mm(weigh_high_ref[...], y_ref[...]) + mm(weigh_low_ref[...], y_ref[...])
    mixed_out[...] = (residual_ref[...] + mixed).astype(BF16)
    for item in spread + [kept]:
        item.wait()
    for i in range(4):
        value = share_in[0, i].astype(F32)
        for j in range(1, 16):
            value += share_in[j, i].astype(F32)
        total[i] = value.reshape(2, 8, 256)
    ends = []
    here = x * 2 + c
    for offset in LINE_OFFSETS:
        to = moved(me, offset)
        ends.append(go(total.at[to["x"], to["c"]], grads_out.at[here], to))
    kept = pltpu.make_async_copy(total.at[x, c], grads_out.at[here], local.at[0])
    kept.start()
    for item in out_copies[1:]:
        item.wait_send()
    for item in out_arrivals[1:]:
        item.wait_recv()

    @pl.when(alone == 0)
    def _():
        out_copies[0].wait_send()
        out_arrivals[0].wait_recv()

    @pl.when(alone == 1)
    def _():
        out_kept().wait()

    for item in early:
        item.wait()
    out_total, side_total = out_in[0], side_in[0]
    for j in range(1, 16):
        out_total += out_in[j]
        side_total += side_in[j]
    early_out[:, 0:D] = out_total
    early_out[:, D : D + 128] = side_total
    for item in along:
        item.wait()
    dnormed = part_own[x] + part_in[x].astype(F32)
    for i in range(3):
        dnormed += line_in[i].astype(F32)
    dnormed_out[...] = dnormed
    for item in ends + [kept]:
        item.wait()


def finish(inputs, cid):
    count = 2 + 3 + 15 + 7 + 16 + 15
    return pl.pallas_call(
        finish_kernel,
        out_shape=[
            jax.ShapeDtypeStruct((ROWS, D), F32),
            jax.ShapeDtypeStruct((ROWS, D), BF16),
            jax.ShapeDtypeStruct((8, 8, 256), F32),
            jax.ShapeDtypeStruct((8, D + 128), F32),
        ],
        in_specs=[pl.BlockSpec(memory_space=pltpu.VMEM)] * 12,
        out_specs=[pl.BlockSpec(memory_space=pltpu.VMEM)] * 4,
        scratch_shapes=[
            pltpu.VMEM((CHIP_ROWS, 256), BF16),
            pltpu.VMEM((4, ROWS, D), BF16),
            pltpu.VMEM((4, ROWS, D), BF16),
            pltpu.VMEM((4, ROWS, D), F32),
            pltpu.VMEM((3, ROWS, D), BF16),
            pltpu.VMEM((3, ROWS, D), BF16),
            pltpu.VMEM((4, 16, 16, 256), BF16),
            pltpu.VMEM((16, 4, 16, 256), BF16),
            pltpu.VMEM((4, 2, 8, 256), F32),
            pltpu.VMEM((16, 8, D), F32),
            pltpu.VMEM((16, 8, 128), F32),
            pltpu.SemaphoreType.DMA((count,)),
            pltpu.SemaphoreType.DMA((count,)),
            pltpu.SemaphoreType.DMA((3,)),
            pltpu.SemaphoreType.DMA((16,)),
        ],
        compiler_params=pltpu.CompilerParams(
            collective_id=cid, has_side_effects=True, vmem_limit_bytes=VMEM_BYTES
        ),
    )(*inputs)


def last_kernel(
    dnormed_ref, tok_ref, gain_ref, gmid_ref, mixed_ref, rows_ref, w_ref, own_gain_ref, early_ref,
    gate_ref, up_ref, down_ref,
    tokens_out, mixed_out, query_out, key_out, value_out, gains_out, grad_out, router_out,
    gate_out, up_out, down_out,
):
    tok = tok_ref[...].astype(F32)
    scale = lax.rsqrt(jnp.mean(tok * tok, axis=-1, keepdims=True) + EPSILON)
    weighted = dnormed_ref[...] * gain_ref[...]
    inner = jnp.mean(weighted * tok, axis=-1, keepdims=True)
    tokens_out[...] = gmid_ref[...] + scale * weighted - tok * (scale * scale * scale) * inner
    mixed_out[...] = mixed_ref[...]
    total = jnp.zeros((8, 256), F32)
    for i in range(8):
        rows = rows_ref[i]
        query_out[:, i * 128 : (i + 1) * 128] = rows[:, :128]
        total += rows * w_ref[:, i * 256 : (i + 1) * 256].astype(F32)
    lanes = lane_index((8, 128)) < 64
    for i in range(4):
        first, second = rows_ref[2 * i][:, 128:], rows_ref[2 * i + 1][:, 128:]
        key_out[:, i * 128 : (i + 1) * 128] = jnp.where(lanes, first, pltpu.roll(second, 64, axis=1))
        value_out[:, i * 128 : (i + 1) * 128] = jnp.where(lanes, pltpu.roll(first, 64, axis=1), second)
    gain_one = jnp.broadcast_to(jnp.sum(total, axis=1, keepdims=True), (8, 128)).T[0:1, :]
    side = early_ref[:, D : D + 128]
    gain_two = side.T[EXPERTS : EXPERTS + 1, :]
    gains_out[0:1, :] = gain_one[:, 0:8] / own_gain_ref[...]
    gains_out[1:2, :] = gain_two[:, 0:8]
    grad_out[...] = early_ref[:, 0:D]
    router_out[...] = side[:, 0:EXPERTS]
    gate_out[...] = gate_ref[...].astype(F32)
    up_out[...] = up_ref[...].astype(F32)
    down_out[...] = down_ref[...].astype(F32)


WHOLE = pl.BlockSpec(memory_space=pltpu.VMEM)
OUT_BLOCK = pl.BlockSpec((D, D), lambda i: (0, 0))
SIDE_BLOCK = pl.BlockSpec((D, 128), lambda i: (0, 8))


def shape(dims, dtype):
    return jax.ShapeDtypeStruct(dims, dtype)


def rotation_tables(order, lengths):
    ends = jnp.cumsum(lengths)
    passed = ends[None, :] <= order[:, None]
    position = order - jnp.sum(jnp.where(passed, lengths[None, :], 0), axis=1)
    frequency = ROPE_BASE ** (-jnp.arange(32, dtype=F32) / 32)
    angles = position.astype(F32)[:, None] * jnp.tile(frequency, 4)[None, :]
    return jnp.cos(angles), jnp.sin(angles)


def body(
    tokens,
    gain_one,
    w_query,
    w_key,
    w_value,
    w_out,
    gain_two,
    w_router,
    w_gate,
    w_up,
    w_down,
    dealt_order,
    lengths,
    routes,
    cotangent,
):
    x_at, y_at, z_at, c_at = (lax.axis_index(axis) for axis in AXES)
    chip = y_at * 4 + z_at
    first_row = chip * CHIP_ROWS

    grouped = jnp.concatenate(
        [
            w_query.reshape(8, 8, 128),
            w_key.reshape(8, 8, 64),
            w_value.reshape(8, 8, 64),
        ],
        axis=2,
    )
    gain_lane = jnp.where(jnp.arange(128)[None, :] == 0, gain_one[:, None], 0).astype(BF16)
    first_pack = jnp.concatenate(
        [grouped.transpose(1, 0, 2), jnp.broadcast_to(gain_lane[None], (8, 8, 128))], axis=2
    )
    token_rows, w_mine = start_rows(tokens, first_pack, 10)
    second_pack = jnp.concatenate(
        [w_out, w_router, gain_two[:, None], jnp.zeros((8, 95), BF16)], axis=1
    )
    second_pack, token_rows = lax.optimization_barrier((second_pack, token_rows))
    w_late = lax.all_gather(second_pack, AXES, axis=0, tiled=True)

    order_own = lax.dynamic_slice_in_dim(dealt_order, first_row, CHIP_ROWS)
    cos, sin = rotation_tables(order_own, lengths)
    ends = jnp.cumsum(lengths)
    within = (dealt_order[None, :] < ends[:, None]) & (
        dealt_order[None, :] >= (ends - lengths)[:, None]
    )
    aux_t = jnp.concatenate([jnp.ones((3, TOKENS), BF16), within.astype(BF16)], axis=0)
    aux = mm(aux_t, jnp.eye(8, 128, dtype=BF16), TN).astype(BF16)
    own_aux = lax.dynamic_slice_in_dim(aux, first_row, CHIP_ROWS)
    order_rows = order_own.astype(F32).reshape(4, RUN)
    run_of = dealt_order.reshape(32, 512)[:, 0] // RUN
    block_ids = jnp.arange(32, dtype=jnp.int32)
    block_of = jnp.sum(
        jnp.where(run_of[None, :] == block_ids[:, None], block_ids[None, :], 0), axis=1
    )
    first_rows = jnp.concatenate([block_of * 512, block_of[::-1] * 512 + RUN])
    mine = lax.dynamic_slice_in_dim(run_of, chip * 2, 2)
    counts = jnp.stack([mine[0], 31 - mine[0], mine[1], 31 - mine[1]])
    base = first_row.reshape(1).astype(jnp.int32)

    expand, expand_t = expand_matrix(), expand_matrix().T
    place, place_t = place_matrix(), place_matrix().T
    pick_high, pick_low = pick_matrix(CAP), pick_matrix(CAP + 1)
    member, put, take, g_out = local_call(
        prepare_kernel,
        (
            shape((ROWS, 128), F32),
            shape((SLOTS, ROWS), BF16),
            shape((ROWS, SLOTS), BF16),
            shape((SLOTS, D), BF16),
        ),
    )(routes, cotangent, expand, expand_t, place_column(), place_row())
    plane = ("y", "z", "c")

    normed, query, kv, gain_first = local_call(
        project_kernel,
        (
            shape((CHIP_ROWS, D), BF16),
            shape((2, CHIP_ROWS, 128), BF16),
            shape((CHIP_ROWS, 128), BF16),
            shape((1, D), F32),
        ),
    )(token_rows, w_mine, cos, sin)
    kv_all = gather_plane(kv, 1)
    g_out, kv_all = lax.optimization_barrier((g_out, kv_all))
    g_in = lax.all_to_all(
        g_out.reshape(EXPERTS, SLOT, D), plane, split_axis=0, concat_axis=0, tiled=True
    )
    smem = pl.BlockSpec(memory_space=pltpu.SMEM)
    vmem = pl.BlockSpec(memory_space=pltpu.VMEM)
    att, norm, sent, query_ext = local_call(
        attend_kernel,
        (
            shape((CHIP_ROWS, 128), F32),
            shape((CHIP_ROWS, 128), F32),
            shape((CHIP_ROWS, 128), BF16),
            shape((4, 2 * RUN, 256), BF16),
        ),
        scratch=[pltpu.VMEM((2 * RUN, 128), F32)],
        in_specs=[smem] * 2 + [vmem] * 6,
    )(first_rows, counts, kv_all, aux, kv, own_aux, query, order_rows)

    (
        residual, weigh_high, weigh_low, gmid, branch, gsent_own, side_rows, y_out,
        grad_gate, grad_up, grad_down,
    ) = moe(
        (
            sent.reshape(8, ROWS, 128), tokens, w_late, w_late, member, put, take, expand, expand_t,
            place, place_t, pick_high, pick_low, (pick_high + pick_low).T, cotangent,
            block_matrix((CAP, CAP + 1)),
            place[:BLOCK],
            block_matrix((CAP,)).T * constant(BLOCK_PLACE == CAP)[:, None],
            block_matrix((CAP + 1,)).T * constant(BLOCK_PLACE == CAP + 1)[:, None],
            g_in, w_gate[0], w_up[0], w_down[0],
        ),
        3,
    )
    y_in = lax.all_to_all(
        y_out, plane, split_axis=0, concat_axis=0, tiled=True
    ).reshape(SLOTS, D)
    grad_gate, grad_up, grad_down = (
        lax.psum_scatter(grad, "x", scatter_dimension=0, tiled=True)
        for grad in (grad_gate, grad_up, grad_down)
    )

    gsent_own = gsent_own.reshape(CHIP_ROWS, 128)
    branch_rows = lax.all_gather(branch, ("c", "x"), axis=0, tiled=True)
    side_sum = jnp.sum(side_rows.astype(F32), axis=0)

    dq, dkv = local_call(
        attend_back_kernel,
        (shape((CHIP_ROWS, 128), F32), shape((TOKENS, 128), BF16)),
        scratch=[
            pltpu.VMEM((TOKENS, 128), F32),
            pltpu.VMEM((64, 2 * RUN), F32),
            pltpu.VMEM((2 * RUN, 256), BF16),
            pltpu.VMEM((4 * RUN, 128), BF16),
        ],
        in_specs=[smem] * 3 + [vmem] * 9,
    )(
        first_rows, counts, base, kv_all, aux, kv, own_aux, query_ext, order_rows, gsent_own, att,
        norm,
    )
    dkv_own, grad_out = scatter_plane(dkv, sent, branch_rows, 6)

    dnormed, mixed, qkv_rows, early = finish(
        (
            dq, dkv_own, cos, sin, normed, w_mine, y_in, weigh_high, weigh_low, residual,
            grad_out.reshape(16, 8, D), side_sum.reshape(16, 8, 128),
        ),
        7,
    )
    (
        grad_tokens, mixed, grad_query, grad_key, grad_value, gains, grad_out_rows, grad_router,
        grad_gate, grad_up, grad_down,
    ) = local_call(
        last_kernel,
        (
            shape((ROWS, D), F32),
            shape((ROWS, D), BF16),
            shape((8, D), F32),
            shape((8, 512), F32),
            shape((8, 512), F32),
            shape((2, 8), F32),
            shape((8, D), F32),
            shape((8, EXPERTS), F32),
            shape((256, FF), F32),
            shape((256, FF), F32),
            shape((128, D), F32),
        ),
    )(
        dnormed, tokens, gain_first, gmid, mixed, qkv_rows, grouped.reshape(8, 2048),
        gain_one.astype(F32).reshape(1, 8), early, grad_gate, grad_up, grad_down,
    )
    grad_gain_one, grad_gain_two = gains[0], gains[1]
    grad_gate, grad_up, grad_down = grad_gate[None], grad_up[None], grad_down[None]
    return (
        mixed,
        grad_tokens,
        grad_gain_one,
        grad_query,
        grad_key,
        grad_value,
        grad_out_rows,
        grad_gain_two,
        grad_router,
        grad_gate,
        grad_up,
        grad_down,
    )


def solution(mesh):
    grid = Mesh(mesh.devices.reshape(4, 4, 4, 2), AXES)
    rows = P(("y", "z", "c", "x"), None)
    vector = P(AXES)
    matrix = P(AXES, None)
    expert = P(("y", "z", "c"), None, None)
    in_specs = (
        rows, vector, matrix, matrix, matrix, matrix, vector, matrix, expert, expert, expert,
        P(), P(), rows, rows,
    )
    grads = P(("y", "z", "c"), "x", None)
    out_specs = (
        rows, rows, vector, matrix, matrix, matrix, matrix, vector, matrix, grads, grads, grads,
    )
    return jax.shard_map(body, mesh=grid, in_specs=in_specs, out_specs=out_specs, check_vma=False)
```

profile of v0, /device:TPU:1, one launch (start us, length us, event | category | flops | bytes accessed | tf_op | source)
XLA Modules:
  0.0 393.5 jit_solution(16023560868050998896)
XLA Ops:
  7.2 0.8 reduce-window.8
  10.4 0.8 reshape.193
  12.6 0.8 fusion.4
  14.1 29.1 %shard_map.356 = (bf16[2,4,128,1024]{3,2,1,0:T(8,128)(2,1)}, bf16[4,4,4,2,8,384]{5,4,3,2,1,0:T(8,128)(2,1)}) custom-call(bf16[128,1024]{1,0:T(8,128)(2,1)} %tok_ref.5, bf16[8,8,384]{2,1,0:T(8,128)(2,1)} %pad_maximum_fusion.w_ref), custom_call_target="tpu_custom_call" | custom-call | tf_op jit(solution)/shard_map/pallas_call | solution.py:215
  43.2 1.4 concatenate.18
  44.6 3.0 multiply_sine_fusion
  47.7 5.0 %shard_map.357 = (bf16[1024,1024]{1,0:T(8,128)(2,1)}, bf16[2,1024,128]{2,1,0:T(8,128)(2,1)}, bf16[1024,128]{1,0:T(8,128)(2,1)}, f32[1,1024]{1,0:T(1,128)}) custom-call(bf16[1024,1024]{1,0:T(8,128)(2,1)} %bitcast.42, bf16[1024,384]{1,0:T(8,128)(2,1)} %bitcast.38, f32[1024,128]{1,0:T(8,128)} %get-tuple-element.111.cos_ref, f32[1024,128]{1,0:T(8,128)} %get-tuple-element.110.sin_ref), custom_call_target="tpu_custom_call" | custom-call | tf_op jit(solution)/shard_map/pallas_call | solution.py:1345
  52.7 25.2 %shard_map.358 = bf16[4,4,2,512,128]{4,3,2,1,0:T(8,128)(2,1)} custom-call(bf16[2,512,128]{2,1,0:T(8,128)(2,1)} %bitcast.41), custom_call_target="tpu_custom_call" | custom-call | tf_op jit(solution)/shard_map/pallas_call | solution.py:314
  78.6 4.3 %shard_map.355 = (f32[128,128]{1,0:T(8,128)}, bf16[1280,128]{1,0:T(8,128)(2,1)}, bf16[128,1280]{1,0:T(8,128)(2,1)}, bf16[1280,1024]{1,0:T(8,128)(2,1)}) custom-call(s32[128,8]{1,0:T(8,128)} %copy.50.routes_ref, bf16[128,1024]{1,0:T(8,128)(2,1)} %cot_ref.3, bf16[128,1280]{1,0:T(8,128)(2,1)} %constant.84.clone.expand_ref, ...), custom_call_target="tpu_custom_call" | custom-call | tf_op jit(solution)/shard_map/pallas_call | solution.py:1334
  82.9 8.6 %all-to-all-start = ((bf16[32,40,1024]{2,1,0:T(8,128)(2,1)}), bf16[32,40,1024]{2,1,0:T(8,128)(2,1)S(1)}, u32[]{:S(2)}, u32[]{:S(2)}) async-start(bf16[32,40,1024]{2,1,0:T(8,128)(2,1)} %bitcast.40), calls=%async_computation | async-start | bytes 5242880 | tf_op jit(solution)/shard_map/all_to_all | solution.py:1356
  95.2 1.9 pad_add_fusion.1.count_ref
  97.9 2.4 convolution_convert_fusion.aux_ref
  100.2 0.8 constant_dynamic-slice_fusion.own_aux_ref
  101.0 1.3 copy-done
  102.3 28.0 %shard_map.359 = (f32[1024,128]{1,0:T(8,128)}, f32[1024,128]{1,0:T(8,128)}, bf16[1024,128]{1,0:T(8,128)(2,1)}, bf16[4,512,256]{2,1,0:T(8,128)(2,1)}) custom-call(s32[64]{0:T(128)} %pad_add_fusion.first_ref, s32[4]{0:T(128)} %pad_add_fusion.1.count_ref, bf16[16384,128]{1,0:T(8,128)(2,1)} %bitcast.34, bf16[16384,128]{1,0:T(8,128)(2,1)} %copy-done, ...), custom_call_target="tpu_custom_call" | custom-call | tf_op jit(solution)/shard_map/pallas_call | solution.py:1361
  130.2 38.5 %all-gather.3.cloned.1.call-done.w_out_ref.router_ref = bf16[1024,1152]{1,0:T(8,128)(2,1)} async-done(((bf16[8,1152]{1,0:T(8,128)(2,1)}), bf16[1024,1152]{1,0:T(8,128)(2,1)}) %all-gather.3.cloned.1.call-update) | async-done | bytes 2359312 | tf_op jit(solution)/shard_map/all_gather | solution.py:1309
  168.8 94.1 %shard_map.360 = (f32[128,1024]{1,0:T(8,128)}, bf16[128,1280]{1,0:T(8,128)(2,1)}, bf16[128,1280]{1,0:T(8,128)(2,1)}, f32[128,1024]{1,0:T(8,128)}, bf16[128,1024]...) custom-call(bf16[8,128,128]{2,1,0:T(8,128)(2,1)} %bitcast.46, ...), custom_call_target="tpu_custom_call" | custom-call | tf_op jit(solution)/shard_map/pallas_call | solution.py:961
  264.3 6.1 %all-to-all-start.1 = ((bf16[32,40,1024]{2,1,0:T(8,128)(2,1)}), bf16[32,40,1024]{2,1,0:T(8,128)(2,1)S(1)}, u32[]{:S(2)}, u32[]{:S(2)}) async-start(bf16[32,40,1024]{2,1,0:T(8,128)(2,1)} %get-tuple-element.82), calls=%async_computation.1 | async-start | bytes 5242880 | tf_op jit(solution)/shard_map/all_to_all | solution.py:1388
  272.2 45.7 %shard_map.361 = (f32[1024,128]{1,0:T(8,128)}, bf16[16384,128]{1,0:T(8,128)(2,1)}) custom-call(s32[64]{0:T(128)} %pad_add_fusion.first_ref, s32[4]{0:T(128)} %pad_add_fusion.1.count_ref, s32[1]{0:T(128)} %bitcast.base_ref, bf16[16384,128]{1,0:T(8,128)(2,1)} %bitcast.35, bf16[16384,128]{1,0:T(8,128)(2,1)} %copy-done, ...), custom_call_target="tpu_custom_call" | custom-call | tf_op jit(solution)/shard_map/pallas_call | solution.py:1400
  318.5 31.7 %shard_map.362 = (f32[2,512,128]{2,1,0:T(8,128)}, f32[128,1024]{1,0:T(8,128)}) custom-call(bf16[4,4,2,512,128]{4,3,2,1,0:T(8,128)(2,1)} %bitcast.37, bf16[1024,128]{1,0:T(8,128)(2,1)} %get-tuple-element.68.sent_ref, bf16[1024,1024]{1,0:T(8,128)(2,1)} %all-gather.5.cloned.1.call-done.branch_ref), custom_call_target="tpu_custom_call" | custom-call | tf_op jit(solution)/shard_map/pallas_call | solution.py:414
  350.3 1.5 copy-done.2
  351.8 30.6 %shard_map.363 = (f32[128,1024]{1,0:T(8,128)}, bf16[128,1024]{1,0:T(8,128)(2,1)}, f32[8,8,256]{2,1,0:T(8,128)}, f32[8,1152]{1,0:T(8,128)}) custom-call(f32[1024,128]{1,0:T(8,128)} %get-tuple-element.77.dq_ref, f32[1024,128]{1,0:T(8,128)} %bitcast.47, f32[1024,128]{1,0:T(8,128)} %get-tuple-element.111.cos_ref, f32[1024,128]{1,0:T(8,128)} %get-tuple-element.110.sin_ref, ...), custom_call_target="tpu_custom_call" | custom-call | tf_op jit(solution)/shard_map/pallas_call | solution.py:1186
  382.5 3.3 shard_map.364
  385.8 1.2 slice_bitcast_fusion
  (63 shorter events, 12.2 us)
Async XLA Ops:
  52.6 25.2 %copy-start.6 = (s32[128,8]{0,1:T(8,128)S(1)}, s32[128,8]{0,1:T(8,128)}, u32[]{:S(2)}) copy-start(s32[128,8]{0,1:T(8,128)} %param.41) | copy-start | bytes 12292
  82.9 9.4 %copy-start.3 = (s32[16384]{0:T(1024)S(1)}, s32[16384]{0:T(1024)}, u32[]{:S(2)}) copy-start(s32[16384]{0:T(1024)} %param.39) | copy-start | bytes 196612
  82.9 14.8 %copy-start.7 = (s32[5]{0:T(128)S(1)}, s32[5]{0:T(128)}, u32[]{:S(2)}) copy-start(s32[5]{0:T(128)} %param.40) | copy-start | bytes 64
  82.9 47.4 %all-to-all-start = ((bf16[32,40,1024]{2,1,0:T(8,128)(2,1)}), bf16[32,40,1024]{2,1,0:T(8,128)(2,1)S(1)}, u32[]{:S(2)}, u32[]{:S(2)}) async-start(bf16[32,40,1024]{2,1,0:T(8,128)(2,1)} %bitcast.40), calls=%async_computation | async-start | bytes 5242880 | tf_op jit(solution)/shard_map/all_to_all | solution.py:1356
  91.5 77.3 %all-gather.3.cloned.1.call-start = ((), (), s32[]{:S(2)}) async-start(), calls=%async_computation.5 | async-start | bytes 2377728 | tf_op jit(solution)/shard_map/all_gather | solution.py:1309
  92.2 226.3 %all-gather.5.cloned.1.call-start = ((), (), s32[]{:S(2)}) async-start(), calls=%async_computation.6 | async-start | bytes 2359296 | tf_op jit(solution)/shard_map/all_gather | solution.py:1397
  100.2 2.1 copy-start
  130.2 38.5 %copy-start.1 = (bf16[32,40,1024]{2,1,0:T(8,128)(2,1)}, bf16[32,40,1024]{2,1,0:T(8,128)(2,1)S(1)}, u32[]{:S(2)}) copy-start(bf16[32,40,1024]{2,1,0:T(8,128)(2,1)S(1)} %all-to-all-done.g_hbm) | copy-start | bytes 7864324
  263.0 119.4 %reduce-scatter.4.cloned.1.call-start = ((), (), s32[]{:S(2)}) async-start(), calls=%async_computation.7 | async-start | bytes 1310720 | tf_op jit(solution)/shard_map/reduce_scatter | solution.py:1392
  263.7 118.7 %reduce-scatter.6.cloned.1.call-start = ((), (), s32[]{:S(2)}) async-start(), calls=%async_computation.8 | async-start | bytes 1310720 | tf_op jit(solution)/shard_map/reduce_scatter | solution.py:1392
  264.3 6.7 %copy-start.5 = (bf16[8,1024]{1,0:T(8,128)(2,1)S(1)}, bf16[8,1024]{1,0:T(8,128)(2,1)}, u32[]{:S(2)}) copy-start(bf16[8,1024]{1,0:T(8,128)(2,1)} %param.30) | copy-start | bytes 49156
  264.3 7.4 %copy-start.8 = (bf16[8]{0:T(256)(128)(2,1)S(1)}, bf16[8]{0:T(256)(128)(2,1)}, u32[]{:S(2)}) copy-start(bf16[8]{0:T(256)(128)(2,1)} %param.29) | copy-start | bytes 52
  264.3 86.0 %all-to-all-start.1 = ((bf16[32,40,1024]{2,1,0:T(8,128)(2,1)}), bf16[32,40,1024]{2,1,0:T(8,128)(2,1)S(1)}, u32[]{:S(2)}, u32[]{:S(2)}) async-start(bf16[32,40,1024]{2,1,0:T(8,128)(2,1)} %get-tuple-element.82), calls=%async_computation.1 | async-start | bytes 5242880 | tf_op jit(solution)/shard_map/all_to_all | solution.py:1388
  270.4 112.1 %reduce-scatter.8.cloned.1.call-start = ((), (), s32[]{:S(2)}) async-start(), calls=%async_computation.9 | async-start | bytes 1310720 | tf_op jit(solution)/shard_map/reduce_scatter | solution.py:1392
  272.2 45.7 %copy-start.4 = (bf16[8,128,128]{2,1,0:T(8,128)(2,1)S(1)}, bf16[8,128,128]{2,1,0:T(8,128)(2,1)}, u32[]{:S(2)}) copy-start(bf16[8,128,128]{2,1,0:T(8,128)(2,1)} %get-tuple-element.87) | copy-start | bytes 786436
  350.3 1.5 copy-start.2
Sparse Core Ops, SparseCore 0:
  95.9 72.8 all-gather.2
  263.1 24.0 all-gather.4
  289.6 22.0 reduce-scatter.3
  314.1 23.2 reduce-scatter.5
  339.6 23.2 reduce-scatter.7
where the time goes:
time: 394 us; the launch traced here: 393 us
  Pallas kernels  297 us (75%)
  waiting for transfers between devices  40.8 us (10%)
  between operations  15.3 us (4%)
  starting transfers between devices  15.1 us (4%)
  other arithmetic  12.1 us (3%)
  local copies, waits for them, and re-layouts  10.8 us (3%)
    pallas_call x1, Pallas kernels, moe(): pl.pallas_call(moe_kernel, grid=(1,), out_shape=[shape((ROWS, D), F32), s...  94.1 us
    pallas_call x1, Pallas kernels, body(): local_call(attend_back_kernel, (shape((CHIP_ROWS, 128), F32), shape((TOKE...  45.7 us
    all_gather x1, waiting for transfers between devices, body(): w_late = lax.all_gather(second_pack, AXES, axis=0, tiled=True)  38.5 us
    pallas_call x1, Pallas kernels, scatter_plane(): pl.pallas_call(scatter_plane_kernel, out_shape=[jax.ShapeDtypeStruct((2,...  31.7 us
    pallas_call x1, Pallas kernels, finish(): pl.pallas_call(finish_kernel, out_shape=[jax.ShapeDtypeStruct((ROWS, D),...  30.6 us
    pallas_call x1, Pallas kernels, start_rows(): pl.pallas_call(start_kernel, out_shape=[jax.ShapeDtypeStruct((2, 4, ROWS,...  29.1 us
    pallas_call x1, Pallas kernels, body(): local_call(attend_kernel, (shape((CHIP_ROWS, 128), F32), shape((CHIP_ROWS...  28 us
    pallas_call x1, Pallas kernels, gather_plane(): pl.pallas_call(gather_plane_kernel, out_shape=jax.ShapeDtypeStruct((4, 4,...  25.2 us
  transfers between devices with their start and end apart: 7, of which 1 were waited for; matrix products, arithmetic and copies ran while one was open for 2% of the time, Pallas kernels for 35%

commit v1 on v0

--- a/solution.py
+++ b/solution.py
@@ -164,166 +164,7 @@
     return out[0] if single else out
 
 
-def start_kernel(tok_ref, w_ref, o_tok, o_w, send, recv, local):
-    me = position(AXES)
-    x, y, z, c = (me[axis] for axis in AXES)
-    offsets = LINE_OFFSETS + PLANE_OFFSETS
-    greet(me, offsets)
-    plus, minus, far = lax.rem(x + 1, 4), lax.rem(x + 3, 4), lax.rem(x + 2, 4)
-    other = 1 - c
-    lower, upper = pl.ds(0, 64), pl.ds(64, 64)
-    used = [0]
-
-    def go(src, dst, to):
-        item = remote(src, dst, send, recv, used[0], to)
-        used[0] += 1
-        item.start()
-        return item
-
-    own_tok = pltpu.make_async_copy(tok_ref, o_tok.at[c, x], local.at[0])
-    own_w = pltpu.make_async_copy(w_ref.at[x * 2 + c], o_w.at[x, y, z, c], local.at[1])
-    own_tok.start()
-    own_w.start()
-    first_w = []
-    for offset in LINE_OFFSETS:
-        to = moved(me, offset)
-        first_w.append(go(w_ref.at[to["x"] * 2 + to["c"]], o_w.at[x, y, z, c], to))
-    to_plus = go(tok_ref, o_tok.at[c, x], {"x": plus})
-    to_minus = go(tok_ref, o_tok.at[c, x], {"x": minus})
-    sides = [go(tok_ref, o_tok.at[c, x], {"c": other})]
-    own_w.wait()
-    for item in first_w:
-        item.wait()
-    second_w = [
-        go(o_w.at[:, y, z], o_w.at[:, y, z], moved(me, offset)) for offset in PLANE_OFFSETS
-    ]
-    to_plus.wait()
-    next_plus = go(o_tok.at[c, minus, lower], o_tok.at[c, minus, lower], {"x": plus})
-    sides.append(go(o_tok.at[c, minus], o_tok.at[c, minus], {"c": other}))
-    to_minus.wait()
-    next_minus = go(o_tok.at[c, plus, upper], o_tok.at[c, plus, upper], {"x": minus})
-    sides.append(go(o_tok.at[c, plus], o_tok.at[c, plus], {"c": other}))
-    next_plus.wait()
-    next_minus.wait()
-    sides.append(go(o_tok.at[c, far], o_tok.at[c, far], {"c": other}))
-    for item in sides + second_w + [own_tok]:
-        item.wait()
-
-
-def start_rows(tokens, packed, cid):
-    count = 3 + 7 + 15 + 2 + 3
-    rows, weights = pl.pallas_call(
-        start_kernel,
-        out_shape=[
-            jax.ShapeDtypeStruct((2, 4, ROWS, D), BF16),
-            jax.ShapeDtypeStruct((4, 4, 4, 2, 8, 384), BF16),
-        ],
-        in_specs=[pl.BlockSpec(memory_space=pl.ANY)] * 2,
-        out_specs=[pl.BlockSpec(memory_space=pl.ANY)] * 2,
-        scratch_shapes=[
-            pltpu.SemaphoreType.DMA((count,)),
-            pltpu.SemaphoreType.DMA((count,)),
-            pltpu.SemaphoreType.DMA((2,)),
-        ],
-        compiler_params=pltpu.CompilerParams(collective_id=cid, has_side_effects=True),
-    )(tokens, packed)
-    return rows.reshape(CHIP_ROWS, D), weights.reshape(D, 384)
-
-
 AROUND = ({"y": 1, "z": 0}, {"y": 3, "z": 0}, {"y": 0, "z": 1}, {"y": 0, "z": 3})
-
-
-def gather_plane_kernel(x_ref, o_ref, send, recv, local):
-    me = position(("y", "z"))
-    y, z = me["y"], me["z"]
-    greet(me, AROUND)
-    own = pltpu.make_async_copy(x_ref, o_ref.at[y, z], local)
-    own.start()
-    half = x_ref.shape[1] // 2
-    lower, upper = pl.ds(0, half), pl.ds(half, half)
-    used = [0]
-
-    def go(src, dst, to):
-        item = remote(src, dst, send, recv, used[0], to)
-        used[0] += 1
-        item.start()
-        return item
-
-    def place(t, a, b):
-        return o_ref.at[a, b, 0] if t == 0 else o_ref.at[b, a, 1]
-
-    axis = (("y", "z"), ("z", "y"))
-    here = tuple((me[a], me[b]) for a, b in axis)
-    step = {"plus": 1, "minus": 3, "far": 2, "own": 0}
-
-    def at(t, which, name):
-        return lax.rem(here[t][which] + step[name], 4)
-
-    def send_second(t, src, name):
-        dst = place(t, at(t, 0, name), here[t][1])
-        src = dst if src is None else src
-        return (
-            go(src, dst, {axis[t][1]: at(t, 1, "plus")}),
-            go(src, dst, {axis[t][1]: at(t, 1, "minus")}),
-        )
-
-    def pass_on(t, which, a_name, b_name, part, direction):
-        ref = place(t, at(t, 0, a_name), at(t, 1, b_name)).at[part]
-        return go(ref, ref, {axis[t][which]: at(t, which, direction)})
-
-    def forward_second(t, name, pair):
-        pair[0].wait()
-        a = pass_on(t, 1, name, "minus", lower, "plus")
-        pair[1].wait()
-        b = pass_on(t, 1, name, "plus", upper, "minus")
-        return [a, b]
-
-    first, second, last = {}, {}, []
-    for t in (0, 1):
-        dst = place(t, *here[t])
-        first[t] = (
-            go(x_ref.at[t], dst, {axis[t][0]: at(t, 0, "plus")}),
-            go(x_ref.at[t], dst, {axis[t][0]: at(t, 0, "minus")}),
-        )
-    for t in (0, 1):
-        second[t, "own"] = send_second(t, x_ref.at[t], "own")
-    far = {}
-    for t in (0, 1):
-        first[t][0].wait()
-        a = pass_on(t, 0, "minus", "own", lower, "plus")
-        second[t, "minus"] = send_second(t, None, "minus")
-        first[t][1].wait()
-        b = pass_on(t, 0, "plus", "own", upper, "minus")
-        second[t, "plus"] = send_second(t, None, "plus")
-        far[t] = (a, b)
-    for t in (0, 1):
-        last += forward_second(t, "own", second[t, "own"])
-    for t in (0, 1):
-        far[t][0].wait()
-        far[t][1].wait()
-        second[t, "far"] = send_second(t, None, "far")
-    for name in ("minus", "plus", "far"):
-        for t in (0, 1):
-            last += forward_second(t, name, second[t, name])
-    for item in last + [own]:
-        item.wait()
-
-
-def gather_plane(data, cid):
-    rows = data.shape[0] // 2
-    out = pl.pallas_call(
-        gather_plane_kernel,
-        out_shape=jax.ShapeDtypeStruct((4, 4, 2, rows, 128), data.dtype),
-        in_specs=[pl.BlockSpec(memory_space=pl.ANY)],
-        out_specs=pl.BlockSpec(memory_space=pl.ANY),
-        scratch_shapes=[
-            pltpu.SemaphoreType.DMA((40,)),
-            pltpu.SemaphoreType.DMA((40,)),
-            pltpu.SemaphoreType.DMA,
-        ],
-        compiler_params=pltpu.CompilerParams(collective_id=cid, has_side_effects=True),
-    )(data.reshape(2, rows, 128))
-    return out.reshape(32 * rows, 128)
 
 
 def scatter_plane_kernel(p_ref, sent_ref, branch_ref, o_ref, grad_ref, far_a, near_a, out_a, sum_a, far_b, near_b, out_b, send, recv):
@@ -448,24 +289,293 @@
     return jnp.where(lane % 64 < 32, -down, up)
 
 
-def project_kernel(tok_ref, w_ref, cos_ref, sin_ref, normed_ref, q_ref, kv_ref, gain_ref):
-    gain = w_ref[:, 256:384].astype(F32).T[0:1, :]
+def gather_plane(kv_v, kv_hbm, go, me, own_sem, fillers):
+    own = pltpu.make_async_copy(kv_v, kv_hbm.at[me["y"], me["z"]], own_sem)
+    own.start()
+    half = kv_v.shape[1] // 2
+    lower, upper = pl.ds(0, half), pl.ds(half, half)
+    axis = (("y", "z"), ("z", "y"))
+    here = tuple((me[a], me[b]) for a, b in axis)
+    step = {"plus": 1, "minus": 3, "far": 2, "own": 0}
+
+    def place(t, a, b):
+        return kv_hbm.at[a, b, 0] if t == 0 else kv_hbm.at[b, a, 1]
+
+    def at(t, which, name):
+        return lax.rem(here[t][which] + step[name], 4)
+
+    def send_second(t, src, name):
+        dst = place(t, at(t, 0, name), here[t][1])
+        src = dst if src is None else src
+        return (
+            go(src, dst, {axis[t][1]: at(t, 1, "plus")}),
+            go(src, dst, {axis[t][1]: at(t, 1, "minus")}),
+        )
+
+    def pass_on(t, which, a_name, b_name, part, direction):
+        ref = place(t, at(t, 0, a_name), at(t, 1, b_name)).at[part]
+        return go(ref, ref, {axis[t][which]: at(t, which, direction)})
+
+    def forward_second(t, name, pair):
+        pair[0].wait()
+        a = pass_on(t, 1, name, "minus", lower, "plus")
+        pair[1].wait()
+        b = pass_on(t, 1, name, "plus", upper, "minus")
+        return [a, b]
+
+    first, second, last = {}, {}, []
+    for t in (0, 1):
+        dst = place(t, *here[t])
+        first[t] = (
+            go(kv_v.at[t], dst, {axis[t][0]: at(t, 0, "plus")}),
+            go(kv_v.at[t], dst, {axis[t][0]: at(t, 0, "minus")}),
+        )
+    for t in (0, 1):
+        second[t, "own"] = send_second(t, kv_v.at[t], "own")
+    fillers[0]()
+    far = {}
+    for t in (0, 1):
+        first[t][0].wait()
+        a = pass_on(t, 0, "minus", "own", lower, "plus")
+        second[t, "minus"] = send_second(t, None, "minus")
+        first[t][1].wait()
+        b = pass_on(t, 0, "plus", "own", upper, "minus")
+        second[t, "plus"] = send_second(t, None, "plus")
+        far[t] = (a, b)
+    fillers[1]()
+    for t in (0, 1):
+        last += forward_second(t, "own", second[t, "own"])
+    for t in (0, 1):
+        far[t][0].wait()
+        far[t][1].wait()
+        second[t, "far"] = send_second(t, None, "far")
+    fillers[2]()
+    for name in ("minus", "plus", "far"):
+        for t in (0, 1):
+            last += forward_second(t, name, second[t, name])
+    return last + [own]
+
+
+def front_kernel(
+    lengths_ref, tok_ref, w_ref, late_ref, order_ref, routes_ref, cot_ref, expand_ref, expand_t_ref,
+    col_ref, row_ref, turn_high_ref, turn_low_ref,
+    q_ref, kv_own_ref, gain_ref, cos_ref, sin_ref, w_out_ref, member_ref, put_ref, take_ref,
+    own_aux_ref, order_rows_ref, kv_hbm, late_hbm, normed_hbm, g_hbm, aux_hbm,
+    rows_v, w_v, normed_v, kv_v, g_v, aux_v, send, recv, local,
+):
+    me = position(AXES)
+    x, y, z, c = (me[axis] for axis in AXES)
+    greet(me, LINE_OFFSETS + PLANE_OFFSETS)
+    plus, minus, far = lax.rem(x + 1, 4), lax.rem(x + 3, 4), lax.rem(x + 2, 4)
+    other = 1 - c
+    lower, upper = pl.ds(0, 64), pl.ds(64, 64)
+    used = [0]
+
+    def go(src, dst, to):
+        item = remote(src, dst, send, recv, used[0], to)
+        used[0] += 1
+        item.start()
+        return item
+
+    def keep(src, dst, slot):
+        item = pltpu.make_async_copy(src, dst, local.at[slot])
+        item.start()
+        return item
+
+    own = [
+        keep(w_ref.at[x * 2 + c], w_v.at[x, y, z, c], 0),
+        keep(late_ref, late_hbm.at[x, y, z, c], 1),
+    ]
+    own_rows = keep(tok_ref, rows_v.at[c, x], 2)
+    first_w = []
+    for offset in LINE_OFFSETS:
+        to = moved(me, offset)
+        first_w.append(go(w_ref.at[to["x"] * 2 + to["c"]], w_v.at[x, y, z, c], to))
+    first_late = [go(late_ref, late_hbm.at[x, y, z, c], {"x": to}) for to in (far, plus, minus)]
+    to_plus = go(tok_ref, rows_v.at[c, x], {"x": plus})
+    to_minus = go(tok_ref, rows_v.at[c, x], {"x": minus})
+    sides = [go(tok_ref, rows_v.at[c, x], {"c": other})]
+
+    for item in own + first_w:
+        item.wait()
+    second_w = [go(w_v.at[:, y, z], w_v.at[:, y, z], moved(me, by)) for by in PLANE_OFFSETS]
+    for item in first_late:
+        item.wait()
+    second_late = [
+        go(late_hbm.at[:, y, z, c], late_hbm.at[:, y, z, c], moved(me, by)) for by in PLANE_OFFSETS
+    ]
+
+    chip = y * 4 + z
+    mine = order_ref[pl.ds(pl.multiple_of(chip * 8, 8), 8), :]
+    ends, total = [], jnp.int32(0)
+    for i in range(NSEQ):
+        total = total + lengths_ref[i]
+        ends.append(total)
+    place = mine
+    for i in range(NSEQ):
+        place = place - jnp.where(mine >= ends[i], lengths_ref[i], 0)
+    lane = lane_index((ROWS, 128))
+
+    def table(ref, picked):
+        return mm(picked, ref[0]) + mm(picked, ref[1]) + mm(picked, ref[2])
+
+    for i in range(8):
+        wide = jnp.broadcast_to(place[i : i + 1, :].astype(F32), (ROWS, 128)).T.astype(jnp.int32)
+        high = table(turn_high_ref, jnp.where(lane == lax.shift_right_logical(wide, 7), 1.0, 0.0).astype(BF16))
+        low = table(turn_low_ref, jnp.where(lane == (wide & 127), 1.0, 0.0).astype(BF16))
+        cos_ref[pl.ds(i * 128, 128), :] = high[:, :128] * low[:, :128] - high[:, 128:] * low[:, 128:]
+        sin_ref[pl.ds(i * 128, 128), :] = high[:, 128:] * low[:, :128] + high[:, :128] * low[:, 128:]
+    for i in range(4):
+        order_rows_ref[i : i + 1, 0:128] = mine[2 * i : 2 * i + 1, :].astype(F32)
+        order_rows_ref[i : i + 1, 128:256] = mine[2 * i + 1 : 2 * i + 2, :].astype(F32)
+
+    to_plus.wait()
+    next_plus = go(rows_v.at[c, minus, lower], rows_v.at[c, minus, lower], {"x": plus})
+    sides.append(go(rows_v.at[c, minus], rows_v.at[c, minus], {"c": other}))
+    to_minus.wait()
+    next_minus = go(rows_v.at[c, plus, upper], rows_v.at[c, plus, upper], {"x": minus})
+    sides.append(go(rows_v.at[c, plus], rows_v.at[c, plus], {"c": other}))
+    next_plus.wait()
+    next_minus.wait()
+    sides.append(go(rows_v.at[c, far], rows_v.at[c, far], {"c": other}))
+    own_rows.wait()
+    for item in second_w:
+        item.wait()
+    weights = w_v[...].astype(F32).reshape(D, 384)
+    w_out_ref[...] = weights.astype(BF16)
+    gain = weights[:, 256:384].T[0:1, :]
     gain_ref[...] = gain
-    for part in range(4):
-        rows = pl.ds(part * 256, 256)
-        tok = tok_ref[rows, :].astype(F32)
-        scale = lax.rsqrt(jnp.mean(tok * tok, axis=-1, keepdims=True) + EPSILON)
-        normed = (tok * scale * gain).astype(BF16)
-        normed_ref[rows, :] = normed
-        pre = mm(normed, w_ref[:, 0:256])
-        cos, sin = cos_ref[rows, :], sin_ref[rows, :]
-        low_lanes = lane_index((256, 128)) < 64
-        q_pre, kv_pre = pre[:, :128], pre[:, 128:]
-        query = (q_pre * cos + turned(q_pre) * sin).astype(BF16).astype(F32) * 0.125
-        q_ref[0, rows, :] = jnp.where(low_lanes, query, 0.0).astype(BF16)
-        q_ref[1, rows, :] = jnp.where(low_lanes, pltpu.roll(query, 64, axis=1), 0.0).astype(BF16)
-        key = kv_pre * cos + turned(kv_pre) * sin
-        kv_ref[rows, :] = jnp.where(low_lanes, key, kv_pre).astype(BF16)
+    low_lanes = lane_index((256, 128)) < 64
+
+    def project(block):
+        for i in range(2):
+            rows = pl.ds(pl.multiple_of(block * 512 + i * 256, 256), 256)
+            tok = rows_v[block, pl.ds(2 * i, 2)].astype(F32).reshape(256, D)
+            scale = lax.rsqrt(jnp.mean(tok * tok, axis=-1, keepdims=True) + EPSILON)
+            normed = (tok * scale * gain).astype(BF16)
+            normed_v[rows, :] = normed
+            pre = mm(normed, w_out_ref[:, 0:256])
+            cos, sin = cos_ref[rows, :], sin_ref[rows, :]
+            q_pre, kv_pre = pre[:, :128], pre[:, 128:]
+            query = (q_pre * cos + turned(q_pre) * sin).astype(BF16).astype(F32) * 0.125
+            q_ref[0, rows, :] = jnp.where(low_lanes, query, 0.0).astype(BF16)
+            q_ref[1, rows, :] = jnp.where(low_lanes, pltpu.roll(query, 64, axis=1), 0.0).astype(BF16)
+            key = kv_pre * cos + turned(kv_pre) * sin
+            kv = jnp.where(low_lanes, key, kv_pre).astype(BF16)
+            kv_own_ref[rows, :] = kv
+            kv_v[block, pl.ds(i * 256, 256), :] = kv
+
+    project(c)
+    for item in sides:
+        item.wait()
+    project(other)
+    stores = [keep(normed_v, normed_hbm, 2)]
+
+    def routing():
+        routes = routes_ref[...]
+        member = jnp.zeros((ROWS, 128), F32)
+        for choice in range(8):
+            member += jnp.where(routes[:, choice : choice + 1] == lane, 1.0, 0.0)
+        below = lax.broadcasted_iota(jnp.int32, (ROWS, ROWS), 0) > lane_index((ROWS, ROWS))
+        earlier = mm(jnp.where(below, 1.0, 0.0).astype(BF16), member.astype(BF16))
+        slot = jnp.where(member > 0.5, earlier, -1.0).astype(BF16)
+        member_ref[...] = member
+        take = jnp.where(mm(slot, expand_ref[...]) == row_ref[...], 1.0, 0.0)
+        take_ref[...] = take.astype(BF16)
+        put = jnp.where(mm(expand_t_ref[...], slot, NT) == col_ref[...].astype(F32), 1.0, 0.0)
+        put = put.astype(BF16)
+        put_ref[...] = put
+        for part in range(4):
+            columns = pl.ds(part * 256, 256)
+            g_v[:, :, columns] = mm(put, cot_ref[:, columns]).reshape(EXPERTS, SLOT, 256).astype(BF16)
+        stores.append(keep(g_v, g_hbm, 0))
+
+    def segments():
+        sub = lax.broadcasted_iota(jnp.int32, (8, 128), 0)
+        begin = jnp.zeros((8, 128), jnp.int32)
+        end = jnp.full((8, 128), TOKENS, jnp.int32)
+        for i in range(NSEQ):
+            begin = jnp.where(sub == 3 + i, ends[i] - lengths_ref[i], begin)
+            end = jnp.where(sub == 3 + i, ends[i], end)
+        spot = jnp.where(sub == lane_index((8, 128)), 1.0, 0.0).astype(BF16)
+
+        def block(step, carry):
+            rows = order_ref[pl.ds(pl.multiple_of(step * 8, 8), 8), :]
+            for i in range(8):
+                order = jnp.broadcast_to(rows[i : i + 1, :], (8, 128))
+                within = jnp.where((order >= begin) & (order < end), 1.0, 0.0).astype(BF16)
+                here = pl.ds(pl.multiple_of(step * 1024 + i * 128, 128), 128)
+                aux_v[here, :] = mm(within, spot, TN).astype(BF16)
+            return carry
+
+        lax.fori_loop(0, 16, block, 0)
+        stores.append(keep(aux_v, aux_hbm, 1))
+        own_aux_ref[...] = aux_v[pl.ds(pl.multiple_of(chip * CHIP_ROWS, CHIP_ROWS), CHIP_ROWS), :]
+
+    def late():
+        for item in second_late:
+            item.wait()
+        stores.append(go(late_hbm.at[:, :, :, c], late_hbm.at[:, :, :, c], {"c": other}))
+
+    last = gather_plane(kv_v, kv_hbm, go, me, local.at[3], (routing, segments, late))
+    for item in last + stores:
+        item.wait()
+
+
+def front(inputs, cid):
+    count = 7 + 3 + 3 + 15 + 15 + 2 + 3 + 40 + 1
+    vmem = pl.BlockSpec(memory_space=pltpu.VMEM)
+    smem = pl.BlockSpec(memory_space=pltpu.SMEM)
+    hbm = pl.BlockSpec(memory_space=pl.ANY)
+    return pl.pallas_call(
+        front_kernel,
+        out_shape=[
+            shape((2, CHIP_ROWS, 128), BF16),
+            shape((CHIP_ROWS, 128), BF16),
+            shape((1, D), F32),
+            shape((CHIP_ROWS, 128), F32),
+            shape((CHIP_ROWS, 128), F32),
+            shape((D, 384), BF16),
+            shape((ROWS, 128), F32),
+            shape((SLOTS, ROWS), BF16),
+            shape((ROWS, SLOTS), BF16),
+            shape((CHIP_ROWS, 128), BF16),
+            shape((4, RUN), F32),
+            shape((4, 4, 2, 512, 128), BF16),
+            shape((4, 4, 4, 2, 8, 1152), BF16),
+            shape((CHIP_ROWS, D), BF16),
+            shape((EXPERTS, SLOT, D), BF16),
+            shape((TOKENS, 128), BF16),
+        ],
+        in_specs=[smem, vmem, hbm, hbm] + [vmem] * 9,
+        out_specs=[vmem] * 11 + [hbm] * 5,
+        scratch_shapes=[
+            pltpu.VMEM((2, 4, ROWS, D), BF16),
+            pltpu.VMEM((4, 4, 4, 2, 8, 384), BF16),
+            pltpu.VMEM((CHIP_ROWS, D), BF16),
+            pltpu.VMEM((2, 512, 128), BF16),
+            pltpu.VMEM((EXPERTS, SLOT, D), BF16),
+            pltpu.VMEM((TOKENS, 128), BF16),
+            pltpu.SemaphoreType.DMA((count,)),
+            pltpu.SemaphoreType.DMA((count,)),
+            pltpu.SemaphoreType.DMA((4,)),
+        ],
+        compiler_params=pltpu.CompilerParams(
+            collective_id=cid, has_side_effects=True, vmem_limit_bytes=VMEM_BYTES
+        ),
+    )(*inputs)
+
+
+def turn_tables(step):
+    frequency = (np.float32(ROPE_BASE) ** (-np.arange(32, dtype=np.float32) / np.float32(32))).astype(np.float64)
+    angles = (np.arange(128) * step)[:, None] * np.tile(frequency, 4)[None, :]
+    rest = np.concatenate([np.cos(angles), np.sin(angles)], axis=1)
+    parts = []
+    for _ in range(3):
+        part = rest.astype(np.float32).astype(ml_dtypes.bfloat16)
+        parts.append(part)
+        rest = rest - part.astype(np.float64)
+    return jnp.asarray(np.stack(parts))
 
 
 def order_pair(order_ref, index):
@@ -650,26 +760,6 @@
 def place_row():
     used = np.where(SLOT_PLACE < CAP, SLOT_PLACE, -5)
     return jnp.asarray(used[None, :].astype(np.float32))
-
-
-def prepare_kernel(routes_ref, cot_ref, expand_ref, expand_t_ref, col_ref, row_ref, member_ref, put_ref, take_ref, out_ref):
-    lane = lane_index((ROWS, 128))
-    routes = routes_ref[...]
-    member = jnp.zeros((ROWS, 128), F32)
-    for choice in range(8):
-        member += jnp.where(routes[:, choice : choice + 1] == lane, 1.0, 0.0)
-    below = lax.broadcasted_iota(jnp.int32, (ROWS, ROWS), 0) > lane_index((ROWS, ROWS))
-    earlier = mm(jnp.where(below, 1.0, 0.0).astype(BF16), member.astype(BF16))
-    slot = jnp.where(member > 0.5, earlier, -1.0).astype(BF16)
-    member_ref[...] = member
-    take = jnp.where(mm(slot, expand_ref[...]) == row_ref[...], 1.0, 0.0)
-    take_ref[...] = take.astype(BF16)
-    put = jnp.where(mm(expand_t_ref[...], slot, NT) == col_ref[...].astype(F32), 1.0, 0.0)
-    put = put.astype(BF16)
-    put_ref[...] = put
-    for part in range(4):
-        columns = pl.ds(part * 256, 256)
-        out_ref[:, columns] = mm(put, cot_ref[:, columns]).astype(BF16)
 
 
 BLOCK = 8 * SLOT
@@ -1259,15 +1349,6 @@
     return jax.ShapeDtypeStruct(dims, dtype)
 
 
-def rotation_tables(order, lengths):
-    ends = jnp.cumsum(lengths)
-    passed = ends[None, :] <= order[:, None]
-    position = order - jnp.sum(jnp.where(passed, lengths[None, :], 0), axis=1)
-    frequency = ROPE_BASE ** (-jnp.arange(32, dtype=F32) / 32)
-    angles = position.astype(F32)[:, None] * jnp.tile(frequency, 4)[None, :]
-    return jnp.cos(angles), jnp.sin(angles)
-
-
 def body(
     tokens,
     gain_one,
@@ -1285,9 +1366,8 @@
     routes,
     cotangent,
 ):
-    x_at, y_at, z_at, c_at = (lax.axis_index(axis) for axis in AXES)
-    chip = y_at * 4 + z_at
-    first_row = chip * CHIP_ROWS
+    y_at, z_at = lax.axis_index("y"), lax.axis_index("z")
+    first_row = (y_at * 4 + z_at) * CHIP_ROWS
 
     grouped = jnp.concatenate(
         [
@@ -1301,61 +1381,36 @@
     first_pack = jnp.concatenate(
         [grouped.transpose(1, 0, 2), jnp.broadcast_to(gain_lane[None], (8, 8, 128))], axis=2
     )
-    token_rows, w_mine = start_rows(tokens, first_pack, 10)
     second_pack = jnp.concatenate(
         [w_out, w_router, gain_two[:, None], jnp.zeros((8, 95), BF16)], axis=1
     )
-    second_pack, token_rows = lax.optimization_barrier((second_pack, token_rows))
-    w_late = lax.all_gather(second_pack, AXES, axis=0, tiled=True)
-
-    order_own = lax.dynamic_slice_in_dim(dealt_order, first_row, CHIP_ROWS)
-    cos, sin = rotation_tables(order_own, lengths)
-    ends = jnp.cumsum(lengths)
-    within = (dealt_order[None, :] < ends[:, None]) & (
-        dealt_order[None, :] >= (ends - lengths)[:, None]
+    expand, expand_t = expand_matrix(), expand_matrix().T
+    place, place_t = place_matrix(), place_matrix().T
+    pick_high, pick_low = pick_matrix(CAP), pick_matrix(CAP + 1)
+    (
+        query, kv, gain_first, cos, sin, w_mine, member, put, take, own_aux, order_rows,
+        kv_all, w_late, normed, g_out, aux,
+    ) = front(
+        (
+            lengths, tokens, first_pack, second_pack, dealt_order.reshape(128, 128), routes, cotangent,
+            expand, expand_t, place_column(), place_row(), turn_tables(128), turn_tables(1),
+        ),
+        1,
     )
-    aux_t = jnp.concatenate([jnp.ones((3, TOKENS), BF16), within.astype(BF16)], axis=0)
-    aux = mm(aux_t, jnp.eye(8, 128, dtype=BF16), TN).astype(BF16)
-    own_aux = lax.dynamic_slice_in_dim(aux, first_row, CHIP_ROWS)
-    order_rows = order_own.astype(F32).reshape(4, RUN)
+    kv_all = kv_all.reshape(TOKENS, 128)
+    w_late = w_late.reshape(D, 1152)
+    plane = ("y", "z", "c")
+    g_in = lax.all_to_all(g_out, plane, split_axis=0, concat_axis=0, tiled=True)
+
     run_of = dealt_order.reshape(32, 512)[:, 0] // RUN
     block_ids = jnp.arange(32, dtype=jnp.int32)
     block_of = jnp.sum(
         jnp.where(run_of[None, :] == block_ids[:, None], block_ids[None, :], 0), axis=1
     )
     first_rows = jnp.concatenate([block_of * 512, block_of[::-1] * 512 + RUN])
-    mine = lax.dynamic_slice_in_dim(run_of, chip * 2, 2)
+    mine = lax.dynamic_slice_in_dim(run_of, (y_at * 4 + z_at) * 2, 2)
     counts = jnp.stack([mine[0], 31 - mine[0], mine[1], 31 - mine[1]])
     base = first_row.reshape(1).astype(jnp.int32)
-
-    expand, expand_t = expand_matrix(), expand_matrix().T
-    place, place_t = place_matrix(), place_matrix().T
-    pick_high, pick_low = pick_matrix(CAP), pick_matrix(CAP + 1)
-    member, put, take, g_out = local_call(
-        prepare_kernel,
-        (
-            shape((ROWS, 128), F32),
-            shape((SLOTS, ROWS), BF16),
-            shape((ROWS, SLOTS), BF16),
-            shape((SLOTS, D), BF16),
-        ),
-    )(routes, cotangent, expand, expand_t, place_column(), place_row())
-    plane = ("y", "z", "c")
-
-    normed, query, kv, gain_first = local_call(
-        project_kernel,
-        (
-            shape((CHIP_ROWS, D), BF16),
-            shape((2, CHIP_ROWS, 128), BF16),
-            shape((CHIP_ROWS, 128), BF16),
-            shape((1, D), F32),
-        ),
-    )(token_rows, w_mine, cos, sin)
-    kv_all = gather_plane(kv, 1)
-    g_out, kv_all = lax.optimization_barrier((g_out, kv_all))
-    g_in = lax.all_to_all(
-        g_out.reshape(EXPERTS, SLOT, D), plane, split_axis=0, concat_axis=0, tiled=True
-    )
     smem = pl.BlockSpec(memory_space=pltpu.SMEM)
     vmem = pl.BlockSpec(memory_space=pltpu.VMEM)
     att, norm, sent, query_ext = local_call(

time: 394 us -> 348 us (0.88)
  waiting for transfers between devices: 40.8 us -> 2.7 us
  other arithmetic: 12.1 us -> 6.65 us
    all_gather x1 -> x0, waiting for transfers between devices: 38.5 us -> none  [body(): w_late = lax.all_gather(second_pack, AXES, axis=0, tiled=True)]
    pallas_call x4 -> x1, Pallas kernels: 63.6 us -> 61.3 us  [front(): pl.pallas_call(front_kernel, out_shape=[shape((2, CHIP_ROWS, 128), BF16),...]
  transfers between devices with their start and end apart: 7 -> 6, of which waited for: 1 -> 1; matrix products, arithmetic and copies ran while one was open for 2% -> 2% of each run, Pallas kernels for 35% -> 39%
where the time goes in v1:
time: 348 us; the launch traced here: 347 us
  Pallas kernels  297 us (85%)
  between operations  17.1 us (5%)
  starting transfers between devices  13.2 us (4%)
  local copies, waits for them, and re-layouts  10.4 us (3%)
  other arithmetic  6.65 us (2%)
    pallas_call x1, Pallas kernels, moe(): pl.pallas_call(moe_kernel, grid=(1,), out_shape=[shape((ROWS, D), F32), s...  96.8 us
    pallas_call x1, Pallas kernels, front(): pl.pallas_call(front_kernel, out_shape=[shape((2, CHIP_ROWS, 128), BF16),...  61.3 us
    pallas_call x1, Pallas kernels, body(): local_call(attend_back_kernel, (shape((CHIP_ROWS, 128), F32), shape((TOKE...  46.1 us
    pallas_call x1, Pallas kernels, scatter_plane(): pl.pallas_call(scatter_plane_kernel, out_shape=[jax.ShapeDtypeStruct((2,...  31.9 us
    pallas_call x1, Pallas kernels, finish(): pl.pallas_call(finish_kernel, out_shape=[jax.ShapeDtypeStruct((ROWS, D),...  29.9 us
    pallas_call x1, Pallas kernels, body(): local_call(attend_kernel, (shape((CHIP_ROWS, 128), F32), shape((CHIP_ROWS...  28 us
    all_to_all x1, starting transfers between devices, body(): g_in = lax.all_to_all(g_out, plane, split_axis=0, concat_axis=0, tiled=True)  8.37 us
  transfers between devices with their start and end apart: 6, of which 1 were waited for; matrix products, arithmetic and copies ran while one was open for 2% of the time, Pallas kernels for 39%

profile of v1, /device:TPU:1, one launch (start us, length us, event | category | flops | bytes accessed | tf_op | source)
XLA Modules:
  0.0 347.2 jit_solution(10615125097671081838)
XLA Ops:
  8.0 0.8 reshape.147
  8.8 0.8 reshape.148
  9.6 1.4 copy.55.routes_ref
  11.0 0.7 copy.54
  11.8 0.7 broadcast_select_fusion
  12.5 0.8 fusion.1
  13.3 0.6 pad_maximum_fusion.w_ref
  13.9 1.4 concatenate.15.late_ref
  15.3 61.3 %shard_map.373 = (bf16[2,1024,128]{2,1,0:T(8,128)(2,1)}, bf16[1024,128]{1,0:T(8,128)(2,1)}, f32[1,1024]{1,0:T(1,128)}, f32[1024,128]{1,0:T(8,128)}, f32[1024,128...) custom-call(s32[5]{0:T(128)} %lengths_ref.1, ...), custom_call_target="tpu_custom_call" | custom-call | tf_op jit(solution)/shard_map/pallas_call | solution.py:530
  76.6 8.4 %all-to-all-start = ((bf16[32,40,1024]{2,1,0:T(8,128)(2,1)}), bf16[32,40,1024]{2,1,0:T(8,128)(2,1)S(1)}, u32[]{:S(2)}, u32[]{:S(2)}) async-start(bf16[32,40,1024]{2,1,0:T(8,128)(2,1)} %get-tuple-element.74), calls=%async_computation | async-start | bytes 5242880 | tf_op jit(solution)/shard_map/all_to_all | solution.py:1403
  87.4 1.9 pad_add_fusion.1.count_ref
  89.9 28.0 %shard_map.374 = (f32[1024,128]{1,0:T(8,128)}, f32[1024,128]{1,0:T(8,128)}, bf16[1024,128]{1,0:T(8,128)(2,1)}, bf16[4,512,256]{2,1,0:T(8,128)(2,1)}) custom-call(s32[64]{0:T(128)} %pad_add_fusion.first_ref, s32[4]{0:T(128)} %pad_add_fusion.1.count_ref, bf16[16384,128]{1,0:T(8,128)(2,1)} %bitcast.29, bf16[16384,128]{1,0:T(8,128)(2,1)} %get-tuple-element.63.aux_ref, ...), custom_call_target="tpu_custom_call" | custom-call | tf_op jit(solution)/shard_map/pallas_call | solution.py:1416
  117.8 1.0 all-to-all-done.g_hbm
  118.9 1.6 copy-done
  120.4 96.8 %shard_map.375 = (f32[128,1024]{1,0:T(8,128)}, bf16[128,1280]{1,0:T(8,128)(2,1)}, bf16[128,1280]{1,0:T(8,128)(2,1)}, f32[128,1024]{1,0:T(8,128)}, bf16[128,1024]...) custom-call(bf16[8,128,128]{2,1,0:T(8,128)(2,1)} %bitcast.38, ...), custom_call_target="tpu_custom_call" | custom-call | tf_op jit(solution)/shard_map/pallas_call | solution.py:1051
  218.5 4.6 %all-to-all-start.1 = ((bf16[32,40,1024]{2,1,0:T(8,128)(2,1)}), bf16[32,40,1024]{2,1,0:T(8,128)(2,1)S(1)}, u32[]{:S(2)}, u32[]{:S(2)}) async-start(bf16[32,40,1024]{2,1,0:T(8,128)(2,1)} %get-tuple-element.86), calls=%async_computation.1 | async-start | bytes 5242880 | tf_op jit(solution)/shard_map/all_to_all | solution.py:1443
  223.7 0.7 pad_maximum_fusion.1
  224.9 46.1 %shard_map.376 = (f32[1024,128]{1,0:T(8,128)}, bf16[16384,128]{1,0:T(8,128)(2,1)}) custom-call(s32[64]{0:T(128)} %pad_add_fusion.first_ref, s32[4]{0:T(128)} %pad_add_fusion.1.count_ref, s32[1]{0:T(128)} %bitcast.base_ref, bf16[16384,128]{1,0:T(8,128)(2,1)} %bitcast.30, bf16[16384,128]{1,0:T(8,128)(2,1)} %get-tuple-element.63.aux_ref, ...), custom_call_target="tpu_custom_call" | custom-call | tf_op jit(solution)/shard_map/pallas_call | solution.py:1455
  271.0 0.7 convert_reduce_fusion
  271.7 31.9 %shard_map.377 = (f32[2,512,128]{2,1,0:T(8,128)}, f32[128,1024]{1,0:T(8,128)}) custom-call(bf16[4,4,2,512,128]{4,3,2,1,0:T(8,128)(2,1)} %bitcast.34, bf16[1024,128]{1,0:T(8,128)(2,1)} %get-tuple-element.69.sent_ref, bf16[1024,1024]{1,0:T(8,128)(2,1)} %all-gather.2.cloned.1.call-done.branch_ref), custom_call_target="tpu_custom_call" | custom-call | tf_op jit(solution)/shard_map/pallas_call | solution.py:255
  303.6 1.5 copy-done.1
  305.1 29.9 %shard_map.378 = (f32[128,1024]{1,0:T(8,128)}, bf16[128,1024]{1,0:T(8,128)(2,1)}, f32[8,8,256]{2,1,0:T(8,128)}, f32[8,1152]{1,0:T(8,128)}) custom-call(f32[1024,128]{1,0:T(8,128)} %get-tuple-element.78.dq_ref, f32[1024,128]{1,0:T(8,128)} %bitcast.39, f32[1024,128]{1,0:T(8,128)} %get-tuple-element.82.cos_ref, f32[1024,128]{1,0:T(8,128)} %get-tuple-element.83.sin_ref, ...), custom_call_target="tpu_custom_call" | custom-call | tf_op jit(solution)/shard_map/pallas_call | solution.py:1276
  335.1 3.3 shard_map.379
  338.4 1.2 slice_bitcast_fusion
  (38 shorter events, 4.0 us)
Async XLA Ops:
  76.6 8.4 %copy-start.3 = (s32[16384]{0:T(1024)S(1)}, s32[16384]{0:T(1024)}, u32[]{:S(2)}) copy-start(s32[16384]{0:T(1024)} %param.41) | copy-start | bytes 196612
  76.6 42.3 %all-to-all-start = ((bf16[32,40,1024]{2,1,0:T(8,128)(2,1)}), bf16[32,40,1024]{2,1,0:T(8,128)(2,1)S(1)}, u32[]{:S(2)}, u32[]{:S(2)}) async-start(bf16[32,40,1024]{2,1,0:T(8,128)(2,1)} %get-tuple-element.74), calls=%async_computation | async-start | bytes 5242880 | tf_op jit(solution)/shard_map/all_to_all | solution.py:1403
  85.0 186.7 %all-gather.2.cloned.1.call-start = ((), (), s32[]{:S(2)}) async-start(), calls=%async_computation.5 | async-start | bytes 2359296 | tf_op jit(solution)/shard_map/all_gather | solution.py:1452
  118.9 1.6 copy-start
  217.3 117.7 %reduce-scatter.4.cloned.1.call-start = ((), (), s32[]{:S(2)}) async-start(), calls=%async_computation.6 | async-start | bytes 1310720 | tf_op jit(solution)/shard_map/reduce_scatter | solution.py:1447
  217.9 117.2 %reduce-scatter.6.cloned.1.call-start = ((), (), s32[]{:S(2)}) async-start(), calls=%async_computation.7 | async-start | bytes 1310720 | tf_op jit(solution)/shard_map/reduce_scatter | solution.py:1447
  218.5 5.2 %copy-start.4 = (bf16[8,1024]{1,0:T(8,128)(2,1)S(1)}, bf16[8,1024]{1,0:T(8,128)(2,1)}, u32[]{:S(2)}) copy-start(bf16[8,1024]{1,0:T(8,128)(2,1)} %param.32) | copy-start | bytes 49156
  218.5 5.9 %copy-start.5 = (bf16[8]{0:T(256)(128)(2,1)S(1)}, bf16[8]{0:T(256)(128)(2,1)}, u32[]{:S(2)}) copy-start(bf16[8]{0:T(256)(128)(2,1)} %param.31) | copy-start | bytes 52
  218.5 85.1 %all-to-all-start.1 = ((bf16[32,40,1024]{2,1,0:T(8,128)(2,1)}), bf16[32,40,1024]{2,1,0:T(8,128)(2,1)S(1)}, u32[]{:S(2)}, u32[]{:S(2)}) async-start(bf16[32,40,1024]{2,1,0:T(8,128)(2,1)} %get-tuple-element.86), calls=%async_computation.1 | async-start | bytes 5242880 | tf_op jit(solution)/shard_map/all_to_all | solution.py:1443
  223.1 112.0 %reduce-scatter.8.cloned.1.call-start = ((), (), s32[]{:S(2)}) async-start(), calls=%async_computation.8 | async-start | bytes 1310720 | tf_op jit(solution)/shard_map/reduce_scatter | solution.py:1447
  224.9 46.1 %copy-start.2 = (bf16[8,128,128]{2,1,0:T(8,128)(2,1)S(1)}, bf16[8,128,128]{2,1,0:T(8,128)(2,1)}, u32[]{:S(2)}) copy-start(bf16[8,128,128]{2,1,0:T(8,128)(2,1)} %get-tuple-element.91) | copy-start | bytes 786436
  303.6 1.5 copy-start.1
Sparse Core Ops, SparseCore 0:
  217.4 26.2 all-gather.1
Sparse Core Ops, SparseCore 1:
  220.2 25.0 reduce-scatter.3
  247.6 21.5 reduce-scatter.5
  271.4 23.3 reduce-scatter.7

commit v2 on v1

--- a/solution.py
+++ b/solution.py
@@ -43,6 +43,10 @@
     return lax.dot_general(a, b, dims, preferred_element_type=F32)
 
 
+def shape(dims, dtype):
+    return jax.ShapeDtypeStruct(dims, dtype)
+
+
 def halves(value):
     high = value.astype(BF16)
     return high, (value - high.astype(F32)).astype(BF16)
@@ -54,6 +58,8 @@
         extra = {"grid": grid, "in_specs": in_specs, "out_specs": out_specs}
     elif in_specs is not None:
         extra = {"in_specs": in_specs}
+        if out_specs is not None:
+            extra["out_specs"] = out_specs
     return pl.pallas_call(
         kernel,
         out_shape=outs,
@@ -61,6 +67,77 @@
         compiler_params=pltpu.CompilerParams(vmem_limit_bytes=VMEM_BYTES),
         **extra,
     )
+
+
+class Late:
+    def __init__(self, hbm, vmem, sem, columns):
+        self.hbm, self.vmem = hbm, vmem
+        source = hbm if columns is None else hbm.at[:, columns[0] : columns[1]]
+        self.copy, self.ready = pltpu.make_async_copy(source, vmem, sem), False
+        self.copy.start()
+
+    def get(self):
+        if not self.ready:
+            self.copy.wait()
+            self.ready = True
+        return self.vmem
+
+    def __getitem__(self, index):
+        return self.get()[index]
+
+
+class Early:
+    def __init__(self, hbm, vmem, sem):
+        self.vmem, self.copy = vmem, pltpu.make_async_copy(vmem, hbm, sem)
+
+    def __getitem__(self, index):
+        return self.vmem[index]
+
+    def __setitem__(self, index, value):
+        self.vmem[index] = value
+
+    def store(self):
+        self.copy.start()
+
+
+def remote_call(kernel, inputs, kinds, outs, out_kinds, scratch, cid):
+    spaces = {"s": pltpu.SMEM, "v": pltpu.VMEM}
+    late = [(i, kind) for i, kind in enumerate(kinds) if kind not in ("s", "v", "h")]
+    early = [i for i, kind in enumerate(out_kinds) if kind == "e"]
+
+    def late_shape(i, kind):
+        dims = inputs[i].shape if kind == "l" else (inputs[i].shape[0], kind[1] - kind[0])
+        return pltpu.VMEM(dims, inputs[i].dtype)
+
+    def wrapped(*refs):
+        ins, rest = list(refs[: len(inputs)]), list(refs[len(inputs) :])
+        results, rest = rest[: len(outs)], rest[len(outs) :]
+        own, rest = rest[: len(scratch)], rest[len(scratch) :]
+        late_v, rest = rest[: len(late)], rest[len(late) :]
+        early_v, (late_sem, early_sem) = rest[: len(early)], rest[len(early) :]
+        for n, (i, kind) in enumerate(late):
+            ins[i] = Late(ins[i], late_v[n], late_sem.at[n], None if kind == "l" else kind)
+        for n, i in enumerate(early):
+            results[i] = Early(results[i], early_v[n], early_sem.at[n])
+        kernel(*ins, *results, *own)
+        for i, _ in late:
+            ins[i].get()
+        for i in early:
+            results[i].copy.wait()
+
+    return pl.pallas_call(
+        wrapped,
+        out_shape=list(outs),
+        in_specs=[pl.BlockSpec(memory_space=spaces.get(kind, pl.ANY)) for kind in kinds],
+        out_specs=[pl.BlockSpec(memory_space=spaces.get(kind, pl.ANY)) for kind in out_kinds],
+        scratch_shapes=list(scratch)
+        + [late_shape(i, kind) for i, kind in late]
+        + [pltpu.VMEM(outs[i].shape, outs[i].dtype) for i in early]
+        + [pltpu.SemaphoreType.DMA((max(1, len(late)),)), pltpu.SemaphoreType.DMA((max(1, len(early)),))],
+        compiler_params=pltpu.CompilerParams(
+            collective_id=cid, has_side_effects=True, vmem_limit_bytes=VMEM_BYTES
+        ),
+    )(*inputs)
 
 
 def flat_index(coords, order):
@@ -170,7 +247,7 @@
 def scatter_plane_kernel(p_ref, sent_ref, branch_ref, o_ref, grad_ref, far_a, near_a, out_a, sum_a, far_b, near_b, out_b, send, recv):
     me = position(("y", "z"))
     greet(me, AROUND)
-    half = p_ref.shape[3] // 2
+    half = p_ref.vmem.shape[3] // 2
     lower, upper = pl.ds(0, half), pl.ds(half, half)
     axis = (("y", "z"), ("z", "y"))
     used = [0]
@@ -182,10 +259,11 @@
         item.start()
         return item
 
-    def part(t, first, second):
+    def part(t, first, second, hbm=False):
         a = lax.rem(me[axis[t][0]] + first, 4)
         b = lax.rem(me[axis[t][1]] + second, 4)
-        return p_ref.at[a, b, 0] if t == 0 else p_ref.at[b, a, 1]
+        ref = p_ref.hbm if hbm else p_ref.get()
+        return ref.at[a, b, 0] if t == 0 else ref.at[b, a, 1]
 
     turns = (2, 1, 3, 0)
     both = (0, 1)
@@ -193,8 +271,8 @@
     for k, by in enumerate(turns):
         for t in both:
             far[k, t] = (
-                go(part(t, 2, by).at[lower], far_a.at[t, k, 0], t, 0, 1),
-                go(part(t, 2, by).at[upper], far_a.at[t, k, 1], t, 0, 3),
+                go(part(t, 2, by, True).at[lower], far_a.at[t, k, 0], t, 0, 1),
+                go(part(t, 2, by, True).at[upper], far_a.at[t, k, 1], t, 0, 3),
             )
     grad_ref[...] = mm(sent_ref[...], branch_ref[...], TN)
     for k, by in enumerate(turns):
@@ -251,16 +329,13 @@
 
 def scatter_plane(data, sent, branch_rows, cid):
     rows = data.shape[0] // 32
-    whole = pl.BlockSpec(memory_space=pltpu.VMEM)
-    out, grad_out = pl.pallas_call(
+    out, grad_out = remote_call(
         scatter_plane_kernel,
-        out_shape=[
-            jax.ShapeDtypeStruct((2, rows, 128), F32),
-            jax.ShapeDtypeStruct((ROWS, D), F32),
-        ],
-        in_specs=[whole] * 3,
-        out_specs=[whole] * 2,
-        scratch_shapes=[
+        (data.reshape(4, 4, 2, rows, 128), sent, branch_rows),
+        ("l", "l", "l"),
+        [shape((2, rows, 128), F32), shape((ROWS, D), F32)],
+        ("v", "v"),
+        [
             pltpu.VMEM((2, 4, 2, rows // 2, 128), BF16),
             pltpu.VMEM((2, 4, 2, rows, 128), BF16),
             pltpu.VMEM((2, 4, 2, rows, 128), BF16),
@@ -271,10 +346,8 @@
             pltpu.SemaphoreType.DMA((40,)),
             pltpu.SemaphoreType.DMA((40,)),
         ],
-        compiler_params=pltpu.CompilerParams(
-            collective_id=cid, has_side_effects=True, vmem_limit_bytes=VMEM_BYTES
-        ),
-    )(data.reshape(4, 4, 2, rows, 128), sent, branch_rows)
+        cid,
+    )
     return out.reshape(2 * rows, 128), grad_out
 
 
@@ -357,14 +430,36 @@
 
 
 def front_kernel(
-    lengths_ref, tok_ref, w_ref, late_ref, order_ref, routes_ref, cot_ref, expand_ref, expand_t_ref,
-    col_ref, row_ref, turn_high_ref, turn_low_ref,
+    lengths_ref, tok_ref, wq_ref, wk_ref, wv_ref, wo_ref, router_ref, gain_one_ref, gain_two_ref,
+    order_ref, routes_ref, cot_ref, expand_ref, expand_t_ref, col_ref, row_ref, turn_high_ref, turn_low_ref,
     q_ref, kv_own_ref, gain_ref, cos_ref, sin_ref, w_out_ref, member_ref, put_ref, take_ref,
-    own_aux_ref, order_rows_ref, kv_hbm, late_hbm, normed_hbm, g_hbm, aux_hbm,
-    rows_v, w_v, normed_v, kv_v, g_v, aux_v, send, recv, local,
+    own_aux_ref, order_rows_ref, key_norm_ref, kv_hbm, late_hbm, normed_v, g_v, aux_v,
+    rows_v, w_v, kv_v, long_v, side_v, w_ref, late_ref, send, recv, local,
 ):
     me = position(AXES)
     x, y, z, c = (me[axis] for axis in AXES)
+    small = lane_index((8, 128))
+    diagonal = lax.broadcasted_iota(jnp.int32, (8, 8), 0) == lane_index((8, 8))
+
+    def column(ref):
+        row = jnp.broadcast_to(ref[...].astype(F32), (8, 8))
+        return jnp.sum(jnp.where(diagonal, row, 0.0), axis=1, keepdims=True)
+
+    gain_lane = jnp.where(small == 0, column(gain_one_ref), 0.0).astype(BF16)
+    for i in range(8):
+        span = slice((i // 2) * 128, (i // 2 + 1) * 128)
+        key, value = wk_ref[:, span].astype(F32), wv_ref[:, span].astype(F32)
+        if i % 2 == 0:
+            pair = jnp.where(small < 64, key, pltpu.roll(value, 64, axis=1))
+        else:
+            pair = jnp.where(small < 64, pltpu.roll(key, 64, axis=1), value)
+        w_ref[i, :, 0:128] = wq_ref[:, i * 128 : (i + 1) * 128]
+        w_ref[i, :, 128:256] = pair.astype(BF16)
+        w_ref[i, :, 256:384] = gain_lane
+    side_v[...] = jnp.zeros_like(side_v)
+    side_v[:, 0:EXPERTS] = router_ref[...].astype(F32)
+    late_ref[:, 0:D] = wo_ref[...]
+    late_ref[:, D : D + 128] = jnp.where(small == EXPERTS, column(gain_two_ref), side_v[...]).astype(BF16)
     greet(me, LINE_OFFSETS + PLANE_OFFSETS)
     plus, minus, far = lax.rem(x + 1, 4), lax.rem(x + 3, 4), lax.rem(x + 2, 4)
     other = 1 - c
@@ -391,7 +486,6 @@
     for offset in LINE_OFFSETS:
         to = moved(me, offset)
         first_w.append(go(w_ref.at[to["x"] * 2 + to["c"]], w_v.at[x, y, z, c], to))
-    first_late = [go(late_ref, late_hbm.at[x, y, z, c], {"x": to}) for to in (far, plus, minus)]
     to_plus = go(tok_ref, rows_v.at[c, x], {"x": plus})
     to_minus = go(tok_ref, rows_v.at[c, x], {"x": minus})
     sides = [go(tok_ref, rows_v.at[c, x], {"c": other})]
@@ -399,11 +493,7 @@
     for item in own + first_w:
         item.wait()
     second_w = [go(w_v.at[:, y, z], w_v.at[:, y, z], moved(me, by)) for by in PLANE_OFFSETS]
-    for item in first_late:
-        item.wait()
-    second_late = [
-        go(late_hbm.at[:, y, z, c], late_hbm.at[:, y, z, c], moved(me, by)) for by in PLANE_OFFSETS
-    ]
+    first_late = [go(late_ref, late_hbm.at[x, y, z, c], moved(me, by)) for by in PLANE_OFFSETS]
 
     chip = y * 4 + z
     mine = order_ref[pl.ds(pl.multiple_of(chip * 8, 8), 8), :]
@@ -448,6 +538,7 @@
     low_lanes = lane_index((256, 128)) < 64
 
     def project(block):
+        longest = jnp.zeros((256, 1), F32)
         for i in range(2):
             rows = pl.ds(pl.multiple_of(block * 512 + i * 256, 256), 256)
             tok = rows_v[block, pl.ds(2 * i, 2)].astype(F32).reshape(256, D)
@@ -464,18 +555,26 @@
             kv = jnp.where(low_lanes, key, kv_pre).astype(BF16)
             kv_own_ref[rows, :] = kv
             kv_v[block, pl.ds(i * 256, 256), :] = kv
-
-    project(c)
+            rounded = kv.astype(F32)
+            square = jnp.sum(jnp.where(low_lanes, rounded * rounded, 0.0), axis=1, keepdims=True)
+            longest = jnp.maximum(longest, square)
+        return jnp.max(longest, axis=0, keepdims=True)
+
+    longest = project(c)
     for item in sides:
         item.wait()
-    project(other)
-    stores = [keep(normed_v, normed_hbm, 2)]
+    longest = jnp.maximum(longest, project(other))
+    long_v[chip] = jnp.broadcast_to(longest, (8, 128))
+    longs = [go(long_v.at[chip], long_v.at[chip], moved(me, by)) for by in PLANE_OFFSETS]
+    stores = []
+    for item in (q_ref, kv_own_ref, cos_ref, sin_ref, w_out_ref, normed_v):
+        item.store()
 
     def routing():
-        routes = routes_ref[...]
+        routes = jnp.concatenate([routes_ref[...].astype(F32), jnp.full((120, 128), -1.0, F32)], axis=0).T
         member = jnp.zeros((ROWS, 128), F32)
         for choice in range(8):
-            member += jnp.where(routes[:, choice : choice + 1] == lane, 1.0, 0.0)
+            member += jnp.where(routes[:, choice : choice + 1].astype(jnp.int32) == lane, 1.0, 0.0)
         below = lax.broadcasted_iota(jnp.int32, (ROWS, ROWS), 0) > lane_index((ROWS, ROWS))
         earlier = mm(jnp.where(below, 1.0, 0.0).astype(BF16), member.astype(BF16))
         slot = jnp.where(member > 0.5, earlier, -1.0).astype(BF16)
@@ -488,7 +587,8 @@
         for part in range(4):
             columns = pl.ds(part * 256, 256)
             g_v[:, :, columns] = mm(put, cot_ref[:, columns]).reshape(EXPERTS, SLOT, 256).astype(BF16)
-        stores.append(keep(g_v, g_hbm, 0))
+        for item in (put_ref, take_ref, g_v):
+            item.store()
 
     def segments():
         sub = lax.broadcasted_iota(jnp.int32, (8, 128), 0)
@@ -509,27 +609,39 @@
             return carry
 
         lax.fori_loop(0, 16, block, 0)
-        stores.append(keep(aux_v, aux_hbm, 1))
+        aux_v.store()
         own_aux_ref[...] = aux_v[pl.ds(pl.multiple_of(chip * CHIP_ROWS, CHIP_ROWS), CHIP_ROWS), :]
+        own_aux_ref.store()
 
     def late():
         for item in second_late:
             item.wait()
         stores.append(go(late_hbm.at[:, :, :, c], late_hbm.at[:, :, :, c], {"c": other}))
 
+    for item in first_late:
+        item.wait()
+    second_late = [
+        go(late_hbm.at[x, :, :, c], late_hbm.at[x, :, :, c], {"x": to}) for to in (far, plus, minus)
+    ]
+
     last = gather_plane(kv_v, kv_hbm, go, me, local.at[3], (routing, segments, late))
+    for item in longs:
+        item.wait()
+    longest = long_v[0]
+    for i in range(1, 16):
+        longest = jnp.maximum(longest, long_v[i])
+    key_norm_ref[...] = jnp.sqrt(longest)
     for item in last + stores:
         item.wait()
 
 
 def front(inputs, cid):
-    count = 7 + 3 + 3 + 15 + 15 + 2 + 3 + 40 + 1
-    vmem = pl.BlockSpec(memory_space=pltpu.VMEM)
-    smem = pl.BlockSpec(memory_space=pltpu.SMEM)
-    hbm = pl.BlockSpec(memory_space=pl.ANY)
-    return pl.pallas_call(
+    count = 7 + 3 + 3 + 15 + 15 + 2 + 3 + 40 + 1 + 15
+    return remote_call(
         front_kernel,
-        out_shape=[
+        inputs,
+        ("s", "h") + ("v",) * 9 + ("l",) * 7,
+        [
             shape((2, CHIP_ROWS, 128), BF16),
             shape((CHIP_ROWS, 128), BF16),
             shape((1, D), F32),
@@ -541,29 +653,28 @@
             shape((ROWS, SLOTS), BF16),
             shape((CHIP_ROWS, 128), BF16),
             shape((4, RUN), F32),
+            shape((8, 128), F32),
             shape((4, 4, 2, 512, 128), BF16),
             shape((4, 4, 4, 2, 8, 1152), BF16),
             shape((CHIP_ROWS, D), BF16),
             shape((EXPERTS, SLOT, D), BF16),
             shape((TOKENS, 128), BF16),
         ],
-        in_specs=[smem, vmem, hbm, hbm] + [vmem] * 9,
-        out_specs=[vmem] * 11 + [hbm] * 5,
-        scratch_shapes=[
+        ("e", "e", "v", "e", "e", "e", "v", "e", "e", "e", "v", "v", "h", "h", "e", "e", "e"),
+        [
             pltpu.VMEM((2, 4, ROWS, D), BF16),
             pltpu.VMEM((4, 4, 4, 2, 8, 384), BF16),
-            pltpu.VMEM((CHIP_ROWS, D), BF16),
             pltpu.VMEM((2, 512, 128), BF16),
-            pltpu.VMEM((EXPERTS, SLOT, D), BF16),
-            pltpu.VMEM((TOKENS, 128), BF16),
+            pltpu.VMEM((16, 8, 128), F32),
+            pltpu.VMEM((8, 128), F32),
+            pltpu.VMEM((8, 8, 384), BF16),
+            pltpu.VMEM((8, 1152), BF16),
             pltpu.SemaphoreType.DMA((count,)),
             pltpu.SemaphoreType.DMA((count,)),
             pltpu.SemaphoreType.DMA((4,)),
         ],
-        compiler_params=pltpu.CompilerParams(
-            collective_id=cid, has_side_effects=True, vmem_limit_bytes=VMEM_BYTES
-        ),
-    )(*inputs)
+        cid,
+    )
 
 
 def turn_tables(step):
@@ -579,33 +690,61 @@
 
 
 def order_pair(order_ref, index):
-    row = jnp.broadcast_to(order_ref[index : index + 1, :], (RUN, RUN))
+    row = jnp.broadcast_to(order_ref[pl.ds(index, 1), :], (RUN, RUN))
     return row, row.T
 
 
+WIDE = 3
+
+
+def run_lists(order_ref, base, first_ref):
+    def note(block, carry):
+        run = lax.shift_right_logical(order_ref[block * 512], 8)
+        first_ref[run] = block * 512
+        first_ref[63 - run] = block * 512 + RUN
+        return carry
+
+    lax.fori_loop(0, 32, note, 0)
+
+    def count(part):
+        run = lax.shift_right_logical(order_ref[base + lax.div(part, 2) * 512], 8)
+        return jnp.where(lax.rem(part, 2) == 0, run, 31 - run)
+
+    return count
+
+
+def group_places(first_ref, number, half, step):
+    places = []
+    for i in range(WIDE):
+        index = step * WIDE + i
+        at = jnp.where(index < number, half + index, 32 - half)
+        places.append(pl.ds(pl.multiple_of(first_ref[at], RUN), RUN))
+    return places
+
+
 def attend_kernel(
-    first_ref, count_ref, kv_ref, aux_ref, own_kv_ref, own_aux_ref, q_ref, order_ref,
-    att_ref, norm_ref, sent_ref, qx_ref, acc_ref,
+    order_smem, base_ref, kv_hbm, aux_hbm, own_kv_ref, own_aux_ref, q_ref, order_ref, key_norm_ref,
+    att_ref, norm_ref, sent_ref, qx_ref, kv_ref, aux_ref, acc_ref, first_ref, loads,
 ):
-    def largest(step, best):
-        tile = kv_ref[pl.ds(pl.multiple_of(step * 512, 512), 512), :].astype(F32)
-        square = jnp.sum(jnp.where(lane_index((512, 128)) < 64, tile * tile, 0.0), axis=1, keepdims=True)
-        return jnp.maximum(best, square)
-
-    best = lax.fori_loop(0, TOKENS // 512, largest, jnp.zeros((512, 1), F32))
-    key_norm = jnp.sqrt(jnp.max(best, axis=0, keepdims=True))
+    copies = [
+        pltpu.make_async_copy(kv_hbm, kv_ref, loads.at[0]),
+        pltpu.make_async_copy(aux_hbm, aux_ref, loads.at[1]),
+    ]
+    for item in copies:
+        item.start()
+    count = run_lists(order_smem, base_ref[0], first_ref)
+    key_norm = key_norm_ref[0:1, 0:1]
     lane = lane_index((RUN, 128))
-    lane_tall = lane_index((2 * RUN, 128))
-
-    def weights(keys, aux, qx):
-        return jnp.exp(mm(qx, jnp.concatenate([keys, aux], axis=1), NT))
+    low_lanes = lane < 64
+    low_tall = lane_index((2 * RUN, 128)) < 64
 
     def right(keys):
         return jnp.where(lane_index(keys.shape) < 64, jnp.ones_like(keys), keys)
 
-    for part in range(4):
-        rows = pl.ds(part * RUN, RUN)
-        own_aux = own_aux_ref[rows, :].astype(F32)
+    def prepare(part, carry):
+        rows = pl.ds(pl.multiple_of(part * RUN, RUN), RUN)
+        own_aux = own_aux_ref[rows, :]
+        spread = jnp.where(lane < 3 + NSEQ, (own_aux.astype(F32) - 1.0) * FAR, 0.0)
         for head in range(2):
             query = q_ref[head, rows, :]
             wide = query.astype(F32)
@@ -613,57 +752,88 @@
             top = shift.astype(BF16).astype(F32)
             middle = (shift - top).astype(BF16).astype(F32)
             rest = shift - top - middle
-            ext = jnp.where(lane < 3 + NSEQ, (own_aux - 1.0) * FAR, 0.0)
-            ext = jnp.where(lane == 0, -top, ext)
+            ext = jnp.where(lane == 0, -top, spread)
             ext = jnp.where(lane == 1, -middle, ext)
             ext = jnp.where(lane == 2, -rest, ext)
             here = pl.ds(head * RUN, RUN)
             qx_ref[part, here, 0:128] = query
             qx_ref[part, here, 128:256] = ext.astype(BF16)
-        qx = qx_ref[part]
         order_key, order_query = order_pair(order_ref, part)
         allowed = order_key <= order_query
         keys = own_kv_ref[rows, :]
-        e = weights(keys, own_aux_ref[rows, :], qx)
+        e = jnp.exp(mm(qx_ref[part], jnp.concatenate([keys, own_aux], axis=1), NT))
         e = jnp.where(jnp.concatenate([allowed, allowed], axis=0), e, 0.0)
-        acc_ref[...] = mm(e.astype(BF16), right(keys))
-        base = (part % 2) * 32
-
-        def tiles(step):
-            start = pl.multiple_of(first_ref[base + step], RUN)
-            return kv_ref[pl.ds(start, RUN), :], aux_ref[pl.ds(start, RUN), :]
-
-        def pair(step, carry):
-            keys_a, aux_a = tiles(2 * step)
-            keys_b, aux_b = tiles(2 * step + 1)
-            keys = jnp.concatenate([keys_a, keys_b], axis=0)
-            aux = jnp.concatenate([aux_a, aux_b], axis=0)
-            acc_ref[...] += mm(weights(keys, aux, qx).astype(BF16), right(keys))
+        acc_ref[part] = mm(e.astype(BF16), right(keys))
+        return carry
+
+    lax.fori_loop(0, 4, prepare, 0)
+    for item in copies:
+        item.wait()
+
+    def part_step(part, carry):
+        number = count(part)
+        half = lax.rem(part, 2) * 32
+
+        def group(step, carry):
+            places = group_places(first_ref, number, half, step)
+            keys = jnp.concatenate([kv_ref[here, :] for here in places], axis=0)
+            aux = jnp.concatenate([aux_ref[here, :] for here in places], axis=0)
+            e = jnp.exp(mm(qx_ref[part], jnp.concatenate([keys, aux], axis=1), NT))
+            acc_ref[part] += mm(e.astype(BF16), right(keys))
             return carry
 
-        number = count_ref[part]
-        lax.fori_loop(0, number // 2, pair, 0)
-
-        @pl.when(number % 2 == 1)
-        def _():
-            keys, aux = tiles(number - 1)
-            acc_ref[...] += mm(weights(keys, aux, qx).astype(BF16), right(keys))
-
-        total = acc_ref[...]
+        lax.fori_loop(0, lax.div(number + WIDE - 1, WIDE), group, 0)
+        rows = pl.ds(pl.multiple_of(part * RUN, RUN), RUN)
+        total = acc_ref[part]
         other = pltpu.roll(total, 64, axis=1)
-        norm = jnp.where(lane_tall < 64, total, other)
-        value = jnp.where(lane_tall < 64, other, total) / norm
-        low_lanes = lane < 64
+        norm = jnp.where(low_tall, total, other)
+        value = jnp.where(low_tall, other, total) / norm
         att = jnp.where(low_lanes, value[:RUN], value[RUN:])
         att_ref[rows, :] = att
         norm_ref[rows, :] = jnp.where(low_lanes, norm[:RUN], norm[RUN:])
         sent_ref[rows, :] = att.astype(BF16)
+        return carry
+
+    lax.fori_loop(0, 4, part_step, 0)
+
+
+def attend(order, base, kv, aux, own_kv, own_aux, query, order_rows, key_norm):
+    smem = pl.BlockSpec(memory_space=pltpu.SMEM)
+    vmem = pl.BlockSpec(memory_space=pltpu.VMEM)
+    hbm = pl.BlockSpec(memory_space=pl.ANY)
+    return local_call(
+        attend_kernel,
+        (
+            shape((CHIP_ROWS, 128), F32),
+            shape((CHIP_ROWS, 128), F32),
+            shape((CHIP_ROWS, 128), BF16),
+            shape((4, 2 * RUN, 256), BF16),
+        ),
+        scratch=[
+            pltpu.VMEM((TOKENS, 128), BF16),
+            pltpu.VMEM((TOKENS, 128), BF16),
+            pltpu.VMEM((4, 2 * RUN, 128), F32),
+            pltpu.SMEM((64,), jnp.int32),
+            pltpu.SemaphoreType.DMA((2,)),
+        ],
+        in_specs=[smem] * 2 + [hbm] * 2 + [vmem] * 5,
+    )(order, base, kv, aux, own_kv, own_aux, query, order_rows, key_norm)
 
 
 def attend_back_kernel(
-    first_ref, count_ref, base_ref, kv_ref, aux_ref, own_kv_ref, own_aux_ref, qx_ref, order_ref,
-    gsent_ref, att_ref, norm_ref, dq_ref, dkv_ref, acc_ref, dq_acc, gx_ref, rhs_ref,
+    order_smem, base_ref, kv_hbm, aux_hbm, own_kv_ref, own_aux_ref, qx_ref, order_ref,
+    gsent_ref, att_ref, norm_ref, dq_ref, dkv_hbm,
+    kv_ref, aux_ref, acc_ref, dq_acc, gx_ref, rhs_ref, out_ref, first_ref, loads, stores,
 ):
+    copies = [
+        pltpu.make_async_copy(kv_hbm, kv_ref, loads.at[0]),
+        pltpu.make_async_copy(aux_hbm, aux_ref, loads.at[1]),
+    ]
+    for item in copies:
+        item.start()
+    own_base = base_ref[0]
+    count = run_lists(order_smem, own_base, first_ref)
+
     def clear(step, carry):
         acc_ref[pl.ds(pl.multiple_of(step * 512, 512), 512), :] = jnp.zeros((512, 128), F32)
         return carry
@@ -671,8 +841,19 @@
     lax.fori_loop(0, TOKENS // 512, clear, 0)
     lane = lane_index((RUN, 128))
     low_lanes = lane < 64
-    for part in range(4):
-        rows = pl.ds(part * RUN, RUN)
+
+    def apply(part, here, e, prob):
+        ds = (e * prob).astype(BF16)
+        left = jnp.concatenate([ds, e.astype(BF16)], axis=1)
+        acc_ref[here, :] += mm(left, rhs_ref[part])
+        return ds
+
+    def scores(part, keys, aux):
+        both = jnp.concatenate([keys, aux], axis=1)
+        return mm(both, qx_ref[part], NT), mm(both, gx_ref[part], NT)
+
+    def prepare(part, carry):
+        rows = pl.ds(pl.multiple_of(part * RUN, RUN), RUN)
         gsent = gsent_ref[rows, :].astype(F32)
         norm = norm_ref[rows, :]
         product = gsent * att_ref[rows, :] / norm
@@ -689,47 +870,86 @@
             grad = pltpu.roll(scaled, 64, axis=1) if head == 0 else scaled
             grad = jnp.where(low_lanes, 0.0, grad).astype(BF16)
             here = pl.ds(head * RUN, RUN)
-            gx_ref[here, 0:128] = grad
-            gx_ref[here, 128:256] = ext.astype(BF16)
-            rhs_ref[pl.ds(head * RUN, RUN), :] = qx_ref[part, here, 0:128]
-            rhs_ref[pl.ds((2 + head) * RUN, RUN), :] = grad
+            gx_ref[part, here, 0:128] = grad
+            gx_ref[part, here, 128:256] = ext.astype(BF16)
+            rhs_ref[part, pl.ds(head * RUN, RUN), :] = qx_ref[part, here, 0:128]
+            rhs_ref[part, pl.ds((2 + head) * RUN, RUN), :] = grad
         order_key, order_query = order_pair(order_ref, part)
         allowed = order_query <= order_key
-        dq_acc[...] = jnp.zeros_like(dq_acc)
-
-        def tile(start, keys, aux, mask):
-            both = jnp.concatenate([keys, aux], axis=1)
-            e = jnp.exp(mm(both, qx_ref[part], NT))
-            if mask is not None:
-                e = jnp.where(mask, e, 0.0)
-            ds = (e * mm(both, gx_ref[...], NT)).astype(BF16)
-            left = jnp.concatenate([ds, e.astype(BF16)], axis=1)
-            acc_ref[pl.ds(start, RUN), :] += mm(left, rhs_ref[...])
-            dq_acc[...] += mm(keys.T[:64], ds)
-
-        tile(
-            pl.multiple_of(base_ref[0] + part * RUN, RUN),
-            own_kv_ref[rows, :],
-            own_aux_ref[rows, :],
-            jnp.concatenate([allowed, allowed], axis=1),
-        )
-        base = (part % 2) * 32
-
-        def step_tile(step, carry):
-            start = pl.multiple_of(first_ref[base + step], RUN)
-            tile(start, kv_ref[pl.ds(start, RUN), :], aux_ref[pl.ds(start, RUN), :], None)
+        keys = own_kv_ref[rows, :]
+        score, prob = scores(part, keys, own_aux_ref[rows, :])
+        e = jnp.where(jnp.concatenate([allowed, allowed], axis=1), jnp.exp(score), 0.0)
+        own = pl.ds(pl.multiple_of(own_base + part * RUN, RUN), RUN)
+        dq_acc[part] = mm(keys.T[:64], apply(part, own, e, prob))
+        return carry
+
+    lax.fori_loop(0, 4, prepare, 0)
+    for item in copies:
+        item.wait()
+
+    def part_step(part, carry):
+        number = count(part)
+        half = lax.rem(part, 2) * 32
+
+        def group(step, carry):
+            places = group_places(first_ref, number, half, step)
+            parts = [scores(part, kv_ref[here, :], aux_ref[here, :]) for here in places]
+            ds = [
+                apply(part, here, jnp.exp(score), prob)
+                for here, (score, prob) in zip(places, parts)
+            ]
+            keys = jnp.concatenate([kv_ref[here, :] for here in places], axis=0)
+            dq_acc[part] += mm(keys.T[:64], jnp.concatenate(ds, axis=0))
             return carry
 
-        lax.fori_loop(0, count_ref[part], step_tile, 0)
-        total = dq_acc[...] * 0.125
+        lax.fori_loop(0, lax.div(number + WIDE - 1, WIDE), group, 0)
+        rows = pl.ds(pl.multiple_of(part * RUN, RUN), RUN)
+        total = dq_acc[part] * 0.125
         dq_ref[rows, :] = jnp.concatenate([total[:, :RUN], total[:, RUN:]], axis=0).T
-
-    def finish(step, carry):
-        rows = pl.ds(pl.multiple_of(step * 512, 512), 512)
-        dkv_ref[rows, :] = acc_ref[rows, :].astype(BF16)
         return carry
 
-    lax.fori_loop(0, TOKENS // 512, finish, 0)
+    lax.fori_loop(0, 4, part_step, 0)
+
+    def store(step):
+        rows = pl.ds(pl.multiple_of(step * 2048, 2048), 2048)
+        return pltpu.make_async_copy(out_ref.at[rows], dkv_hbm.at[rows], stores.at[step])
+
+    def narrow(step, carry):
+        rows = pl.ds(pl.multiple_of(step * 2048, 2048), 2048)
+        out_ref[rows, :] = acc_ref[rows, :].astype(BF16)
+        store(step).start()
+        return carry
+
+    def settle(step, carry):
+        store(step).wait()
+        return carry
+
+    lax.fori_loop(0, 8, narrow, 0)
+    lax.fori_loop(0, 8, settle, 0)
+
+
+def attend_back(order, base, kv, aux, own_kv, own_aux, query_ext, order_rows, gsent, att, norm):
+    smem = pl.BlockSpec(memory_space=pltpu.SMEM)
+    vmem = pl.BlockSpec(memory_space=pltpu.VMEM)
+    hbm = pl.BlockSpec(memory_space=pl.ANY)
+    return local_call(
+        attend_back_kernel,
+        (shape((CHIP_ROWS, 128), F32), shape((TOKENS, 128), BF16)),
+        scratch=[
+            pltpu.VMEM((TOKENS, 128), BF16),
+            pltpu.VMEM((TOKENS, 128), BF16),
+            pltpu.VMEM((TOKENS, 128), F32),
+            pltpu.VMEM((4, 64, 2 * RUN), F32),
+            pltpu.VMEM((4, 2 * RUN, 256), BF16),
+            pltpu.VMEM((4, 4 * RUN, 128), BF16),
+            pltpu.VMEM((TOKENS, 128), BF16),
+            pltpu.SMEM((64,), jnp.int32),
+            pltpu.SemaphoreType.DMA((2,)),
+            pltpu.SemaphoreType.DMA((8,)),
+        ],
+        in_specs=[smem] * 2 + [hbm] * 2 + [vmem] * 7,
+        out_specs=[vmem, hbm],
+    )(order, base, kv, aux, own_kv, own_aux, query_ext, order_rows, gsent, att, norm)
 
 
 SLOT_EXPERT = np.arange(SLOTS) // SLOT
@@ -850,6 +1070,7 @@
     sent = jnp.concatenate([sent_in[i] for i in range(8)], axis=1)
     residual = tok_ref[...].astype(F32) + mm(sent, w_out_ref[...])
     residual_ref[...] = residual
+    residual_ref.store()
     gain = router_ref[...].astype(F32).T[EXPERTS : EXPERTS + 1, :]
     scale = lax.rsqrt(jnp.mean(residual * residual, axis=-1, keepdims=True) + EPSILON)
     mixed = (residual * scale * gain).astype(BF16)
@@ -867,6 +1088,8 @@
     weigh_high, weigh_low = halves(weigh)
     weigh_high_ref[...] = weigh_high
     weigh_low_ref[...] = weigh_low
+    weigh_high_ref.store()
+    weigh_low_ref.store()
     total = jnp.sum(weigh, axis=0, keepdims=True)
     rows_high, rows_low = halves(expand_ref[...].astype(F32) * total)
     rows_high = mm(rows_high, place_ref[...]).astype(BF16)
@@ -898,6 +1121,8 @@
     sum_down[...] = jnp.zeros_like(sum_down)
     for item in loads:
         item.wait()
+    for item in (block_place_ref, select_ref, high_ref, low_ref):
+        item.get()
 
     def back_copy(k):
         to = source(k)
@@ -1004,8 +1229,10 @@
     inner = jnp.mean(weighted * residual, axis=-1, keepdims=True)
     gmid = cot_ref[...].astype(F32) + scale * weighted - residual * (scale * scale * scale) * inner
     gmid_ref[...] = gmid
+    gmid_ref.store()
     branch = gmid.astype(BF16)
     branch_ref[...] = branch
+    branch_ref.store()
     gsent = mm(branch, w_out_ref[...], NT).astype(BF16)
     for i in range(8):
         gsent_out[i] = gsent[:, i * 128 : (i + 1) * 128]
@@ -1043,15 +1270,14 @@
 
 
 def moe(inputs, cid):
-    vmem = pl.BlockSpec(memory_space=pltpu.VMEM)
-    hbm = pl.BlockSpec(memory_space=pl.ANY)
     slots = (EXPERTS, SLOT, D)
     up, down = (D, FF), (FF, D)
     dma = pltpu.SemaphoreType.DMA
-    return pl.pallas_call(
+    return remote_call(
         moe_kernel,
-        grid=(1,),
-        out_shape=[
+        inputs,
+        ("h", "l", (0, D), (D, D + 128)) + ("l",) * 15 + ("h",) * 4,
+        [
             shape((ROWS, D), F32),
             shape((ROWS, SLOTS), BF16),
             shape((ROWS, SLOTS), BF16),
@@ -1064,9 +1290,8 @@
             shape(up, BF16),
             shape(down, BF16),
         ],
-        in_specs=[vmem] * 2 + [OUT_BLOCK, SIDE_BLOCK] + [vmem] * 15 + [hbm] * 4,
-        out_specs=[vmem] * 7 + [hbm] * 4,
-        scratch_shapes=[
+        ("e", "e", "e", "e", "e", "v", "v", "h", "h", "h", "h"),
+        [
             pltpu.VMEM((8, ROWS, 128), BF16),
             pltpu.VMEM(slots, BF16),
             pltpu.VMEM(slots, BF16),
@@ -1095,10 +1320,8 @@
             dma((21,)),
             dma((6,)),
         ],
-        compiler_params=pltpu.CompilerParams(
-            collective_id=cid, has_side_effects=True, vmem_limit_bytes=VMEM_BYTES
-        ),
-    )(*inputs)
+        cid,
+    )
 
 
 def finish_kernel(
@@ -1193,7 +1416,7 @@
         dkv = jnp.where(low_lanes, dkv * cos - turned(dkv) * sin, dkv).astype(BF16)
         both = jnp.concatenate([dq, dkv], axis=1)
         dqkv[rows, :] = both
-        return mm(both, w_ref[:, 0:256], NT)
+        return mm(both, w_ref[...], NT)
 
     crossing = []
     for i in range(2):
@@ -1225,6 +1448,7 @@
     kept.start()
     mixed = mm(weigh_high_ref[...], y_ref[...]) + mm(weigh_low_ref[...], y_ref[...])
     mixed_out[...] = (residual_ref[...] + mixed).astype(BF16)
+    mixed_out.store()
     for item in spread + [kept]:
         item.wait()
     for i in range(4):
@@ -1273,17 +1497,18 @@
 
 def finish(inputs, cid):
     count = 2 + 3 + 15 + 7 + 16 + 15
-    return pl.pallas_call(
+    return remote_call(
         finish_kernel,
-        out_shape=[
-            jax.ShapeDtypeStruct((ROWS, D), F32),
-            jax.ShapeDtypeStruct((ROWS, D), BF16),
-            jax.ShapeDtypeStruct((8, 8, 256), F32),
-            jax.ShapeDtypeStruct((8, D + 128), F32),
+        inputs,
+        ("l", "l", "l", "l", "l", (0, 256), "l", "l", "l", "l", "h", "h"),
+        [
+            shape((ROWS, D), F32),
+            shape((ROWS, D), BF16),
+            shape((8, 8, 256), F32),
+            shape((8, D + 128), F32),
         ],
-        in_specs=[pl.BlockSpec(memory_space=pltpu.VMEM)] * 12,
-        out_specs=[pl.BlockSpec(memory_space=pltpu.VMEM)] * 4,
-        scratch_shapes=[
+        ("v", "e", "v", "v"),
+        [
             pltpu.VMEM((CHIP_ROWS, 256), BF16),
             pltpu.VMEM((4, ROWS, D), BF16),
             pltpu.VMEM((4, ROWS, D), BF16),
@@ -1300,14 +1525,12 @@
             pltpu.SemaphoreType.DMA((3,)),
             pltpu.SemaphoreType.DMA((16,)),
         ],
-        compiler_params=pltpu.CompilerParams(
-            collective_id=cid, has_side_effects=True, vmem_limit_bytes=VMEM_BYTES
-        ),
-    )(*inputs)
+        cid,
+    )
 
 
 def last_kernel(
-    dnormed_ref, tok_ref, gain_ref, gmid_ref, mixed_ref, rows_ref, w_ref, own_gain_ref, early_ref,
+    dnormed_ref, tok_ref, gain_ref, gmid_ref, mixed_ref, rows_ref, wq_ref, wk_ref, wv_ref, own_gain_ref, early_ref,
     gate_ref, up_ref, down_ref,
     tokens_out, mixed_out, query_out, key_out, value_out, gains_out, grad_out, router_out,
     gate_out, up_out, down_out,
@@ -1318,35 +1541,28 @@
     inner = jnp.mean(weighted * tok, axis=-1, keepdims=True)
     tokens_out[...] = gmid_ref[...] + scale * weighted - tok * (scale * scale * scale) * inner
     mixed_out[...] = mixed_ref[...]
-    total = jnp.zeros((8, 256), F32)
     for i in range(8):
-        rows = rows_ref[i]
-        query_out[:, i * 128 : (i + 1) * 128] = rows[:, :128]
-        total += rows * w_ref[:, i * 256 : (i + 1) * 256].astype(F32)
+        query_out[:, i * 128 : (i + 1) * 128] = rows_ref[i][:, :128]
     lanes = lane_index((8, 128)) < 64
     for i in range(4):
         first, second = rows_ref[2 * i][:, 128:], rows_ref[2 * i + 1][:, 128:]
         key_out[:, i * 128 : (i + 1) * 128] = jnp.where(lanes, first, pltpu.roll(second, 64, axis=1))
         value_out[:, i * 128 : (i + 1) * 128] = jnp.where(lanes, pltpu.roll(first, 64, axis=1), second)
-    gain_one = jnp.broadcast_to(jnp.sum(total, axis=1, keepdims=True), (8, 128)).T[0:1, :]
+    total = (
+        jnp.sum(query_out[...] * wq_ref[...].astype(F32), axis=1, keepdims=True)
+        + jnp.sum(key_out[...] * wk_ref[...].astype(F32), axis=1, keepdims=True)
+        + jnp.sum(value_out[...] * wv_ref[...].astype(F32), axis=1, keepdims=True)
+    )
+    gain_one = jnp.broadcast_to(total, (8, 128)).T[0:1, :]
     side = early_ref[:, D : D + 128]
     gain_two = side.T[EXPERTS : EXPERTS + 1, :]
-    gains_out[0:1, :] = gain_one[:, 0:8] / own_gain_ref[...]
+    gains_out[0:1, :] = gain_one[:, 0:8] / own_gain_ref[...].astype(F32)
     gains_out[1:2, :] = gain_two[:, 0:8]
     grad_out[...] = early_ref[:, 0:D]
     router_out[...] = side[:, 0:EXPERTS]
     gate_out[...] = gate_ref[...].astype(F32)
     up_out[...] = up_ref[...].astype(F32)
     down_out[...] = down_ref[...].astype(F32)
-
-
-WHOLE = pl.BlockSpec(memory_space=pltpu.VMEM)
-OUT_BLOCK = pl.BlockSpec((D, D), lambda i: (0, 0))
-SIDE_BLOCK = pl.BlockSpec((D, 128), lambda i: (0, 8))
-
-
-def shape(dims, dtype):
-    return jax.ShapeDtypeStruct(dims, dtype)
 
 
 def body(
@@ -1369,30 +1585,16 @@
     y_at, z_at = lax.axis_index("y"), lax.axis_index("z")
     first_row = (y_at * 4 + z_at) * CHIP_ROWS
 
-    grouped = jnp.concatenate(
-        [
-            w_query.reshape(8, 8, 128),
-            w_key.reshape(8, 8, 64),
-            w_value.reshape(8, 8, 64),
-        ],
-        axis=2,
-    )
-    gain_lane = jnp.where(jnp.arange(128)[None, :] == 0, gain_one[:, None], 0).astype(BF16)
-    first_pack = jnp.concatenate(
-        [grouped.transpose(1, 0, 2), jnp.broadcast_to(gain_lane[None], (8, 8, 128))], axis=2
-    )
-    second_pack = jnp.concatenate(
-        [w_out, w_router, gain_two[:, None], jnp.zeros((8, 95), BF16)], axis=1
-    )
     expand, expand_t = expand_matrix(), expand_matrix().T
     place, place_t = place_matrix(), place_matrix().T
     pick_high, pick_low = pick_matrix(CAP), pick_matrix(CAP + 1)
     (
-        query, kv, gain_first, cos, sin, w_mine, member, put, take, own_aux, order_rows,
+        query, kv, gain_first, cos, sin, w_mine, member, put, take, own_aux, order_rows, key_norm,
         kv_all, w_late, normed, g_out, aux,
     ) = front(
         (
-            lengths, tokens, first_pack, second_pack, dealt_order.reshape(128, 128), routes, cotangent,
+            lengths, tokens, w_query, w_key, w_value, w_out, w_router, gain_one.reshape(1, 8),
+            gain_two.reshape(1, 8), dealt_order.reshape(128, 128), routes.T, cotangent,
             expand, expand_t, place_column(), place_row(), turn_tables(128), turn_tables(1),
         ),
         1,
@@ -1402,28 +1604,10 @@
     plane = ("y", "z", "c")
     g_in = lax.all_to_all(g_out, plane, split_axis=0, concat_axis=0, tiled=True)
 
-    run_of = dealt_order.reshape(32, 512)[:, 0] // RUN
-    block_ids = jnp.arange(32, dtype=jnp.int32)
-    block_of = jnp.sum(
-        jnp.where(run_of[None, :] == block_ids[:, None], block_ids[None, :], 0), axis=1
+    base = first_row.reshape(1).astype(jnp.int32)
+    att, norm, sent, query_ext = attend(
+        dealt_order, base, kv_all, aux, kv, own_aux, query, order_rows, key_norm
     )
-    first_rows = jnp.concatenate([block_of * 512, block_of[::-1] * 512 + RUN])
-    mine = lax.dynamic_slice_in_dim(run_of, (y_at * 4 + z_at) * 2, 2)
-    counts = jnp.stack([mine[0], 31 - mine[0], mine[1], 31 - mine[1]])
-    base = first_row.reshape(1).astype(jnp.int32)
-    smem = pl.BlockSpec(memory_space=pltpu.SMEM)
-    vmem = pl.BlockSpec(memory_space=pltpu.VMEM)
-    att, norm, sent, query_ext = local_call(
-        attend_kernel,
-        (
-            shape((CHIP_ROWS, 128), F32),
-            shape((CHIP_ROWS, 128), F32),
-            shape((CHIP_ROWS, 128), BF16),
-            shape((4, 2 * RUN, 256), BF16),
-        ),
-        scratch=[pltpu.VMEM((2 * RUN, 128), F32)],
-        in_specs=[smem] * 2 + [vmem] * 6,
-    )(first_rows, counts, kv_all, aux, kv, own_aux, query, order_rows)
 
     (
         residual, weigh_high, weigh_low, gmid, branch, gsent_own, side_rows, y_out,
@@ -1452,19 +1636,8 @@
     branch_rows = lax.all_gather(branch, ("c", "x"), axis=0, tiled=True)
     side_sum = jnp.sum(side_rows.astype(F32), axis=0)
 
-    dq, dkv = local_call(
-        attend_back_kernel,
-        (shape((CHIP_ROWS, 128), F32), shape((TOKENS, 128), BF16)),
-        scratch=[
-            pltpu.VMEM((TOKENS, 128), F32),
-            pltpu.VMEM((64, 2 * RUN), F32),
-            pltpu.VMEM((2 * RUN, 256), BF16),
-            pltpu.VMEM((4 * RUN, 128), BF16),
-        ],
-        in_specs=[smem] * 3 + [vmem] * 9,
-    )(
-        first_rows, counts, base, kv_all, aux, kv, own_aux, query_ext, order_rows, gsent_own, att,
-        norm,
+    dq, dkv = attend_back(
+        dealt_order, base, kv_all, aux, kv, own_aux, query_ext, order_rows, gsent_own, att, norm
     )
     dkv_own, grad_out = scatter_plane(dkv, sent, branch_rows, 6)
 
@@ -1494,8 +1667,8 @@
             shape((128, D), F32),
         ),
     )(
-        dnormed, tokens, gain_first, gmid, mixed, qkv_rows, grouped.reshape(8, 2048),
-        gain_one.astype(F32).reshape(1, 8), early, grad_gate, grad_up, grad_down,
+        dnormed, tokens, gain_first, gmid, mixed, qkv_rows, w_query, w_key, w_value,
+        gain_one.reshape(1, 8), early, grad_gate, grad_up, grad_down,
     )
     grad_gain_one, grad_gain_two = gains[0], gains[1]
     grad_gate, grad_up, grad_down = grad_gate[None], grad_up[None], grad_down[None]

time: 348 us -> 312 us (0.90)
  Pallas kernels: 297 us -> 261 us
  waiting for transfers between devices: 2.7 us -> 14.1 us
  local copies, waits for them, and re-layouts: 10.4 us -> 4.3 us
  other arithmetic: 6.65 us -> 0.67 us
    pallas_call x6, Pallas kernels: 294 us -> 257 us  [the longest x4 202 us: remote_call(): pl.pallas_call(wrapped, out_shape=list(outs), in_specs=[pl.BlockSpec(memo...]
    all_to_all x1, waiting for transfers between devices: 1.05 us -> 12.7 us  [body(): g_in = lax.all_to_all(g_out, plane, split_axis=0, concat_axis=0, tiled=True)]
    all_to_all x1, starting transfers between devices: 4.61 us -> 8.11 us  [body(): lax.all_to_all(y_out, plane, split_axis=0, concat_axis=0, tiled=True)]
  transfers between devices with their start and end apart: 6 -> 6, of which waited for: 1 -> 1; matrix products, arithmetic and copies ran while one was open for 2% -> 0% of each run, Pallas kernels for 39% -> 36%
where the time goes in v2:
time: 312 us
  Pallas kernels  261 us (84%)
  starting transfers between devices  16.3 us (5%)
  between operations  15.8 us (5%)
  waiting for transfers between devices  14.1 us (5%)
  local copies, waits for them, and re-layouts  4.3 us (1%)
    pallas_call x4, Pallas kernels, remote_call(): pl.pallas_call(wrapped, out_shape=list(outs), in_specs=[pl.BlockSpec(memo...  202 us
    pallas_call x1, Pallas kernels, attend_back(): local_call(attend_back_kernel, (shape((CHIP_ROWS, 128), F32), shape((TOKE...  34.1 us
    pallas_call x1, Pallas kernels, attend(): local_call(attend_kernel, (shape((CHIP_ROWS, 128), F32), shape((CHIP_ROWS...  21 us
    all_to_all x1, waiting for transfers between devices, body(): g_in = lax.all_to_all(g_out, plane, split_axis=0, concat_axis=0, tiled=True)  12.7 us
    all_to_all x1, starting transfers between devices, body(): lax.all_to_all(y_out, plane, split_axis=0, concat_axis=0, tiled=True)  8.11 us
    all_to_all x1, starting transfers between devices, body(): g_in = lax.all_to_all(g_out, plane, split_axis=0, concat_axis=0, tiled=True)  7.66 us
  transfers between devices with their start and end apart: 6, of which 1 were waited for; matrix products, arithmetic and copies ran while one was open for 0% of the time, Pallas kernels for 36%

profile of v2, /device:TPU:1, one launch (start us, length us, event | category | flops | bytes accessed | tf_op | source)
XLA Modules:
  0.0 311.7 jit_solution(4463899930068234209)
XLA Ops:
  8.0 54.5 %shard_map.373 = (bf16[2,1024,128]{2,1,0:T(8,128)(2,1)}, bf16[1024,128]{1,0:T(8,128)(2,1)}, f32[1,1024]{1,0:T(1,128)}, f32[1024,128]{1,0:T(8,128)}, f32[1024,128...) custom-call(s32[5]{0:T(128)} %refs_0_.1, ...), custom_call_target="tpu_custom_call" | custom-call | tf_op jit(solution)/shard_map/pallas_call | solution.py:128
  62.5 7.7 %all-to-all-start = ((bf16[32,40,1024]{2,1,0:T(8,128)(2,1)}), bf16[32,40,1024]{2,1,0:T(8,128)(2,1)S(1)}, u32[]{:S(2)}, u32[]{:S(2)}) async-start(bf16[32,40,1024]{2,1,0:T(8,128)(2,1)} %get-tuple-element.76), calls=%async_computation | async-start | bytes 5242880 | tf_op jit(solution)/shard_map/all_to_all | solution.py:1605
  70.1 0.2 all-gather.2.cloned.1.call-start
  70.4 21.0 %shard_map.374 = (f32[1024,128]{1,0:T(8,128)}, f32[1024,128]{1,0:T(8,128)}, bf16[1024,128]{1,0:T(8,128)(2,1)}, bf16[4,512,256]{2,1,0:T(8,128)(2,1)}) custom-call(s32[16384]{0:T(1024)} %order_smem.3, s32[1]{0:T(128)} %bitcast.base_ref, bf16[16384,128]{1,0:T(8,128)(2,1)} %bitcast.24, bf16[16384,128]{1,0:T(8,128)(2,1)} %get-tuple-element.64.aux_hbm, ...), custom_call_target="tpu_custom_call" | custom-call | tf_op jit(solution)/shard_map/pallas_call | solution.py:804
  91.4 12.7 %all-to-all-done.refs_19_ = bf16[32,40,1024]{2,1,0:T(8,128)(2,1)S(1)} async-done(((bf16[32,40,1024]{2,1,0:T(8,128)(2,1)}), bf16[32,40,1024]{2,1,0:T(8,128)(2,1)S(1)}, u32[]{:S(2)}, u32[]{:S(2)}) %all-to-all-start) | async-done | bytes 2621472 | tf_op jit(solution)/shard_map/all_to_all | solution.py:1605
  104.0 1.5 copy-done
  105.6 91.8 %shard_map.375 = (f32[128,1024]{1,0:T(8,128)}, bf16[128,1280]{1,0:T(8,128)(2,1)}, bf16[128,1280]{1,0:T(8,128)(2,1)}, f32[128,1024]{1,0:T(8,128)}, bf16[128,1024]...) custom-call(bf16[8,128,128]{2,1,0:T(8,128)(2,1)} %bitcast.33, ...), custom_call_target="tpu_custom_call" | custom-call | tf_op jit(solution)/shard_map/pallas_call | solution.py:128
  197.4 0.0 reduce-scatter.4.cloned.1.call-start
  197.5 0.5 reduce-scatter.4.cloned.1.call-update
  198.0 0.0 reduce-scatter.6.cloned.1.call-start
  198.1 0.5 reduce-scatter.6.cloned.1.call-update
  198.6 8.1 %all-to-all-start.1 = ((bf16[32,40,1024]{2,1,0:T(8,128)(2,1)}), bf16[32,40,1024]{2,1,0:T(8,128)(2,1)S(1)}, u32[]{:S(2)}, u32[]{:S(2)}) async-start(bf16[32,40,1024]{2,1,0:T(8,128)(2,1)} %get-tuple-element.88), calls=%async_computation.1 | async-start | bytes 5242880 | tf_op jit(solution)/shard_map/all_to_all | solution.py:1627
  206.7 0.3 reduce-scatter.8.cloned.1.call-start
  207.0 0.3 reduce-scatter.8.cloned.1.call-update
  207.3 34.1 %shard_map.376 = (f32[1024,128]{1,0:T(8,128)}, bf16[16384,128]{1,0:T(8,128)(2,1)}) custom-call(s32[16384]{0:T(1024)} %order_smem.3, s32[1]{0:T(128)} %bitcast.base_ref, bf16[16384,128]{1,0:T(8,128)(2,1)} %bitcast.25, bf16[16384,128]{1,0:T(8,128)(2,1)} %get-tuple-element.64.aux_hbm, bf16[1024,128]{1,0:T(8,128)(2,1)} %get-tuple-element.65.own_kv_ref, ...), custom_call_target="tpu_custom_call" | custom-call | tf_op jit(solution)/shard_map/pallas_call | solution.py:935
  241.4 0.7 convert_reduce_fusion
  242.1 28.9 %shard_map.377 = (f32[2,512,128]{2,1,0:T(8,128)}, f32[128,1024]{1,0:T(8,128)}) custom-call(bf16[4,4,2,512,128]{4,3,2,1,0:T(8,128)(2,1)} %bitcast.29, bf16[1024,128]{1,0:T(8,128)(2,1)} %get-tuple-element.71.refs_1_, bf16[1024,1024]{1,0:T(8,128)(2,1)} %all-gather.2.cloned.1.call-done.refs_2_), custom_call_target="tpu_custom_call" | custom-call | tf_op jit(solution)/shard_map/pallas_call | solution.py:128
  271.0 1.5 copy-done.1
  272.5 27.0 %shard_map.378 = (f32[128,1024]{1,0:T(8,128)}, bf16[128,1024]{1,0:T(8,128)(2,1)}, f32[8,8,256]{2,1,0:T(8,128)}, f32[8,1152]{1,0:T(8,128)}) custom-call(f32[1024,128]{1,0:T(8,128)} %get-tuple-element.80.refs_0_, f32[1024,128]{1,0:T(8,128)} %bitcast.35, f32[1024,128]{1,0:T(8,128)} %get-tuple-element.84.refs_2_, f32[1024,128]{1,0:T(8,128)} %get-tuple-element.85.refs_3_, ...), custom_call_target="tpu_custom_call" | custom-call | tf_op jit(solution)/shard_map/pallas_call | solution.py:128
  299.5 0.0 reduce-scatter.4.cloned.1.call-done.gate_ref
  299.5 0.0 reduce-scatter.6.cloned.1.call-done.up_ref
  299.6 0.0 reduce-scatter.8.cloned.1.call-done.down_ref
  299.6 3.3 %shard_map.379 = (f32[128,1024]{1,0:T(8,128)}, bf16[128,1024]{1,0:T(8,128)(2,1)}, f32[8,1024]{1,0:T(8,128)}, f32[8,512]{1,0:T(8,128)}, f32[8,512]{1,0:T(8,128)},...) custom-call(f32[128,1024]{1,0:T(8,128)} %get-tuple-element.94.dnorme, ...), custom_call_target="tpu_custom_call" | custom-call | tf_op jit(solution)/shard_map/pallas_call | solution.py:1654
  302.9 1.3 slice_bitcast_fusion
  (7 shorter events, 0.0 us)
Async XLA Ops:
  62.5 41.6 %all-to-all-start = ((bf16[32,40,1024]{2,1,0:T(8,128)(2,1)}), bf16[32,40,1024]{2,1,0:T(8,128)(2,1)S(1)}, u32[]{:S(2)}, u32[]{:S(2)}) async-start(bf16[32,40,1024]{2,1,0:T(8,128)(2,1)} %get-tuple-element.76), calls=%async_computation | async-start | bytes 5242880 | tf_op jit(solution)/shard_map/all_to_all | solution.py:1605
  70.1 171.9 %all-gather.2.cloned.1.call-start = ((), (), s32[]{:S(2)}) async-start(), calls=%async_computation.5 | async-start | bytes 2359296 | tf_op jit(solution)/shard_map/all_gather | solution.py:1636
  104.0 1.6 copy-start
  197.4 102.1 %reduce-scatter.4.cloned.1.call-start = ((), (), s32[]{:S(2)}) async-start(), calls=%async_computation.6 | async-start | bytes 1310720 | tf_op jit(solution)/shard_map/reduce_scatter | solution.py:1631
  198.0 101.5 %reduce-scatter.6.cloned.1.call-start = ((), (), s32[]{:S(2)}) async-start(), calls=%async_computation.7 | async-start | bytes 1310720 | tf_op jit(solution)/shard_map/reduce_scatter | solution.py:1631
  198.6 72.3 %all-to-all-start.1 = ((bf16[32,40,1024]{2,1,0:T(8,128)(2,1)}), bf16[32,40,1024]{2,1,0:T(8,128)(2,1)S(1)}, u32[]{:S(2)}, u32[]{:S(2)}) async-start(bf16[32,40,1024]{2,1,0:T(8,128)(2,1)} %get-tuple-element.88), calls=%async_computation.1 | async-start | bytes 5242880 | tf_op jit(solution)/shard_map/all_to_all | solution.py:1627
  206.7 92.9 %reduce-scatter.8.cloned.1.call-start = ((), (), s32[]{:S(2)}) async-start(), calls=%async_computation.8 | async-start | bytes 1310720 | tf_op jit(solution)/shard_map/reduce_scatter | solution.py:1631
  207.3 34.1 %copy-start.2 = (bf16[8,128,128]{2,1,0:T(8,128)(2,1)S(1)}, bf16[8,128,128]{2,1,0:T(8,128)(2,1)}, u32[]{:S(2)}) copy-start(bf16[8,128,128]{2,1,0:T(8,128)(2,1)} %get-tuple-element.93) | copy-start | bytes 786436
  271.0 1.5 copy-start.1
Sparse Core Ops, SparseCore 0:
  197.6 30.3 all-gather.1
Sparse Core Ops, SparseCore 1:
  200.3 29.1 reduce-scatter.3
  231.8 21.6 reduce-scatter.5
  255.7 23.1 reduce-scatter.7

commit v3 on v2

--- a/solution.py
+++ b/solution.py
@@ -176,7 +176,7 @@
     barrier = pltpu.get_barrier_semaphore()
     for offset in offsets:
         pl.semaphore_signal(barrier, inc=1, device_id=moved(me, offset), device_id_type=MESH)
-    pl.semaphore_wait(barrier, len(offsets))
+    return lambda: pl.semaphore_wait(barrier, len(offsets))
 
 
 def remote(src, dst, send, recv, slot, to):
@@ -190,63 +190,7 @@
     )
 
 
-def exchange_kernel(axes, dest_order, src_order, arrays, *refs):
-    x_refs, o_refs = refs[:arrays], refs[arrays : 2 * arrays]
-    send, recv, local = refs[2 * arrays :]
-    me = position(axes)
-    offsets = OFFSETS[axes]
-    greet(me, offsets)
-    here = flat_index(me, src_order)
-    copies = []
-    for offset in offsets:
-        to = moved(me, offset)
-        for x_ref, o_ref in zip(x_refs, o_refs):
-            copies.append(
-                remote(
-                    x_ref.at[flat_index(to, dest_order)], o_ref.at[here], send, recv, len(copies), to
-                )
-            )
-            copies[-1].start()
-    kept = [
-        pltpu.make_async_copy(
-            x_ref.at[flat_index(me, dest_order)], o_ref.at[here], local.at[i]
-        )
-        for i, (x_ref, o_ref) in enumerate(zip(x_refs, o_refs))
-    ]
-    for item in kept:
-        item.start()
-    for item in kept + copies:
-        item.wait()
-
-
-def exchange(data, axes, cid, dest_order=None, src_order=None):
-    single = not isinstance(data, (tuple, list))
-    data = [data] if single else list(data)
-    dest_order = dest_order or axes
-    src_order = src_order or axes
-    arrays = len(data)
-    count = len(OFFSETS[axes]) * arrays
-    out = pl.pallas_call(
-        functools.partial(exchange_kernel, axes, dest_order, src_order, arrays),
-        out_shape=[jax.ShapeDtypeStruct(item.shape, item.dtype) for item in data],
-        in_specs=[pl.BlockSpec(memory_space=pl.ANY)] * arrays,
-        out_specs=[pl.BlockSpec(memory_space=pl.ANY)] * arrays,
-        scratch_shapes=[
-            pltpu.SemaphoreType.DMA((count,)),
-            pltpu.SemaphoreType.DMA((count,)),
-            pltpu.SemaphoreType.DMA((arrays,)),
-        ],
-        compiler_params=pltpu.CompilerParams(collective_id=cid, has_side_effects=True),
-    )(*data)
-    return out[0] if single else out
-
-
-AROUND = ({"y": 1, "z": 0}, {"y": 3, "z": 0}, {"y": 0, "z": 1}, {"y": 0, "z": 3})
-
-
-def scatter_plane_kernel(p_ref, sent_ref, branch_ref, o_ref, grad_ref, far_a, near_a, out_a, sum_a, far_b, near_b, out_b, send, recv):
-    me = position(("y", "z"))
-    greet(me, AROUND)
+def scatter_plane(me, p_ref, o_ref, far_a, near_a, out_a, sum_a, far_b, near_b, out_b, send, recv):
     half = p_ref.vmem.shape[3] // 2
     lower, upper = pl.ds(0, half), pl.ds(half, half)
     axis = (("y", "z"), ("z", "y"))
@@ -274,7 +218,6 @@
                 go(part(t, 2, by, True).at[lower], far_a.at[t, k, 0], t, 0, 1),
                 go(part(t, 2, by, True).at[upper], far_a.at[t, k, 1], t, 0, 3),
             )
-    grad_ref[...] = mm(sent_ref[...], branch_ref[...], TN)
     for k, by in enumerate(turns):
         for t in both:
             ahead, behind = part(t, 1, by), part(t, 3, by)
@@ -325,30 +268,6 @@
         near_two[t][0].wait()
         near_two[t][1].wait()
         o_ref[t] = value + near_b[t, 0].astype(F32) + near_b[t, 1].astype(F32)
-
-
-def scatter_plane(data, sent, branch_rows, cid):
-    rows = data.shape[0] // 32
-    out, grad_out = remote_call(
-        scatter_plane_kernel,
-        (data.reshape(4, 4, 2, rows, 128), sent, branch_rows),
-        ("l", "l", "l"),
-        [shape((2, rows, 128), F32), shape((ROWS, D), F32)],
-        ("v", "v"),
-        [
-            pltpu.VMEM((2, 4, 2, rows // 2, 128), BF16),
-            pltpu.VMEM((2, 4, 2, rows, 128), BF16),
-            pltpu.VMEM((2, 4, 2, rows, 128), BF16),
-            pltpu.VMEM((2, 2, rows, 128), F32),
-            pltpu.VMEM((2, 2, rows // 2, 128), BF16),
-            pltpu.VMEM((2, 2, rows, 128), BF16),
-            pltpu.VMEM((2, 3, rows, 128), BF16),
-            pltpu.SemaphoreType.DMA((40,)),
-            pltpu.SemaphoreType.DMA((40,)),
-        ],
-        cid,
-    )
-    return out.reshape(2 * rows, 128), grad_out
 
 
 def lane_index(shape):
@@ -431,13 +350,14 @@
 
 def front_kernel(
     lengths_ref, tok_ref, wq_ref, wk_ref, wv_ref, wo_ref, router_ref, gain_one_ref, gain_two_ref,
-    order_ref, routes_ref, cot_ref, expand_ref, expand_t_ref, col_ref, row_ref, turn_high_ref, turn_low_ref,
+    order_ref, routes_ref, expand_ref, expand_t_ref, col_ref, row_ref, turn_high_ref, turn_low_ref,
     q_ref, kv_own_ref, gain_ref, cos_ref, sin_ref, w_out_ref, member_ref, put_ref, take_ref,
-    own_aux_ref, order_rows_ref, key_norm_ref, kv_hbm, late_hbm, normed_v, g_v, aux_v,
+    own_aux_ref, order_rows_ref, key_norm_ref, kv_hbm, late_hbm, normed_v, aux_v,
     rows_v, w_v, kv_v, long_v, side_v, w_ref, late_ref, send, recv, local,
 ):
     me = position(AXES)
     x, y, z, c = (me[axis] for axis in AXES)
+    arrived = greet(me, LINE_OFFSETS + PLANE_OFFSETS)
     small = lane_index((8, 128))
     diagonal = lax.broadcasted_iota(jnp.int32, (8, 8), 0) == lane_index((8, 8))
 
@@ -460,7 +380,7 @@
     side_v[:, 0:EXPERTS] = router_ref[...].astype(F32)
     late_ref[:, 0:D] = wo_ref[...]
     late_ref[:, D : D + 128] = jnp.where(small == EXPERTS, column(gain_two_ref), side_v[...]).astype(BF16)
-    greet(me, LINE_OFFSETS + PLANE_OFFSETS)
+    arrived()
     plus, minus, far = lax.rem(x + 1, 4), lax.rem(x + 3, 4), lax.rem(x + 2, 4)
     other = 1 - c
     lower, upper = pl.ds(0, 64), pl.ds(64, 64)
@@ -584,10 +504,7 @@
         put = jnp.where(mm(expand_t_ref[...], slot, NT) == col_ref[...].astype(F32), 1.0, 0.0)
         put = put.astype(BF16)
         put_ref[...] = put
-        for part in range(4):
-            columns = pl.ds(part * 256, 256)
-            g_v[:, :, columns] = mm(put, cot_ref[:, columns]).reshape(EXPERTS, SLOT, 256).astype(BF16)
-        for item in (put_ref, take_ref, g_v):
+        for item in (put_ref, take_ref):
             item.store()
 
     def segments():
@@ -640,7 +557,7 @@
     return remote_call(
         front_kernel,
         inputs,
-        ("s", "h") + ("v",) * 9 + ("l",) * 7,
+        ("s", "h") + ("v",) * 9 + ("l",) * 6,
         [
             shape((2, CHIP_ROWS, 128), BF16),
             shape((CHIP_ROWS, 128), BF16),
@@ -657,10 +574,9 @@
             shape((4, 4, 2, 512, 128), BF16),
             shape((4, 4, 4, 2, 8, 1152), BF16),
             shape((CHIP_ROWS, D), BF16),
-            shape((EXPERTS, SLOT, D), BF16),
             shape((TOKENS, 128), BF16),
         ],
-        ("e", "e", "v", "e", "e", "e", "v", "e", "e", "e", "v", "v", "h", "h", "e", "e", "e"),
+        ("e", "e", "v", "e", "e", "e", "v", "e", "e", "e", "v", "v", "h", "h", "e", "e"),
         [
             pltpu.VMEM((2, 4, ROWS, D), BF16),
             pltpu.VMEM((4, 4, 4, 2, 8, 384), BF16),
@@ -694,7 +610,8 @@
     return row, row.T
 
 
-WIDE = 3
+WIDE = 6
+WIDE_BACK = 3
 
 
 def run_lists(order_ref, base, first_ref):
@@ -713,10 +630,10 @@
     return count
 
 
-def group_places(first_ref, number, half, step):
+def group_places(first_ref, number, half, step, wide):
     places = []
-    for i in range(WIDE):
-        index = step * WIDE + i
+    for i in range(wide):
+        index = step * wide + i
         at = jnp.where(index < number, half + index, 32 - half)
         places.append(pl.ds(pl.multiple_of(first_ref[at], RUN), RUN))
     return places
@@ -735,11 +652,11 @@
     count = run_lists(order_smem, base_ref[0], first_ref)
     key_norm = key_norm_ref[0:1, 0:1]
     lane = lane_index((RUN, 128))
-    low_lanes = lane < 64
-    low_tall = lane_index((2 * RUN, 128)) < 64
 
     def right(keys):
-        return jnp.where(lane_index(keys.shape) < 64, jnp.ones_like(keys), keys)
+        turned_keys = keys.T
+        row = lax.broadcasted_iota(jnp.int32, turned_keys.shape, 0)
+        return jnp.where(row < 64, jnp.ones_like(turned_keys), turned_keys)[56:]
 
     def prepare(part, carry):
         rows = pl.ds(pl.multiple_of(part * RUN, RUN), RUN)
@@ -759,11 +676,11 @@
             qx_ref[part, here, 0:128] = query
             qx_ref[part, here, 128:256] = ext.astype(BF16)
         order_key, order_query = order_pair(order_ref, part)
-        allowed = order_key <= order_query
+        allowed = order_query <= order_key
         keys = own_kv_ref[rows, :]
-        e = jnp.exp(mm(qx_ref[part], jnp.concatenate([keys, own_aux], axis=1), NT))
-        e = jnp.where(jnp.concatenate([allowed, allowed], axis=0), e, 0.0)
-        acc_ref[part] = mm(e.astype(BF16), right(keys))
+        e = jnp.exp(mm(jnp.concatenate([keys, own_aux], axis=1), qx_ref[part], NT))
+        e = jnp.where(jnp.concatenate([allowed, allowed], axis=1), e, 0.0)
+        acc_ref[part] = mm(right(keys), e.astype(BF16))
         return carry
 
     lax.fori_loop(0, 4, prepare, 0)
@@ -775,22 +692,22 @@
         half = lax.rem(part, 2) * 32
 
         def group(step, carry):
-            places = group_places(first_ref, number, half, step)
+            places = group_places(first_ref, number, half, step, WIDE)
             keys = jnp.concatenate([kv_ref[here, :] for here in places], axis=0)
             aux = jnp.concatenate([aux_ref[here, :] for here in places], axis=0)
-            e = jnp.exp(mm(qx_ref[part], jnp.concatenate([keys, aux], axis=1), NT))
-            acc_ref[part] += mm(e.astype(BF16), right(keys))
+            e = jnp.exp(mm(jnp.concatenate([keys, aux], axis=1), qx_ref[part], NT))
+            acc_ref[part] += mm(right(keys), e.astype(BF16))
             return carry
 
         lax.fori_loop(0, lax.div(number + WIDE - 1, WIDE), group, 0)
         rows = pl.ds(pl.multiple_of(part * RUN, RUN), RUN)
         total = acc_ref[part]
-        other = pltpu.roll(total, 64, axis=1)
-        norm = jnp.where(low_tall, total, other)
-        value = jnp.where(low_tall, other, total) / norm
-        att = jnp.where(low_lanes, value[:RUN], value[RUN:])
+        value = total[8:72] / total[0:1]
+        att = jnp.concatenate([value[:, :RUN], value[:, RUN:]], axis=0).T
+        norm = jnp.broadcast_to(total[0:1], (64, 2 * RUN))
+        norm = jnp.concatenate([norm[:, :RUN], norm[:, RUN:]], axis=0).T
         att_ref[rows, :] = att
-        norm_ref[rows, :] = jnp.where(low_lanes, norm[:RUN], norm[RUN:])
+        norm_ref[rows, :] = norm
         sent_ref[rows, :] = att.astype(BF16)
         return carry
 
@@ -812,7 +729,7 @@
         scratch=[
             pltpu.VMEM((TOKENS, 128), BF16),
             pltpu.VMEM((TOKENS, 128), BF16),
-            pltpu.VMEM((4, 2 * RUN, 128), F32),
+            pltpu.VMEM((4, 72, 2 * RUN), F32),
             pltpu.SMEM((64,), jnp.int32),
             pltpu.SemaphoreType.DMA((2,)),
         ],
@@ -892,7 +809,7 @@
         half = lax.rem(part, 2) * 32
 
         def group(step, carry):
-            places = group_places(first_ref, number, half, step)
+            places = group_places(first_ref, number, half, step, WIDE_BACK)
             parts = [scores(part, kv_ref[here, :], aux_ref[here, :]) for here in places]
             ds = [
                 apply(part, here, jnp.exp(score), prob)
@@ -902,7 +819,7 @@
             dq_acc[part] += mm(keys.T[:64], jnp.concatenate(ds, axis=0))
             return carry
 
-        lax.fori_loop(0, lax.div(number + WIDE - 1, WIDE), group, 0)
+        lax.fori_loop(0, lax.div(number + WIDE_BACK - 1, WIDE_BACK), group, 0)
         rows = pl.ds(pl.multiple_of(part * RUN, RUN), RUN)
         total = dq_acc[part] * 0.125
         dq_ref[rows, :] = jnp.concatenate([total[:, :RUN], total[:, RUN:]], axis=0).T
@@ -1003,13 +920,14 @@
 
 def moe_kernel(
     sent_ref, tok_ref, w_out_ref, router_ref, member_ref, put_ref, take_ref, expand_ref,
-    expand_t_ref, place_ref, place_t_ref, pick_high_ref, pick_low_ref, pick_t_ref, cot_ref,
-    select_ref, block_place_ref, high_ref, low_ref, g_hbm, gate_hbm, up_hbm, down_hbm,
+    expand_t_ref, place_ref, place_t_ref, cot_ref, cots_hbm, gate_hbm, up_hbm, down_hbm,
     residual_ref, weigh_high_ref, weigh_low_ref, gmid_ref, branch_ref, gsent_in, side_in,
-    y_hbm, grad_gate_hbm, grad_up_hbm, grad_down_hbm,
-    sent_in, x_out, x_in, g_v, y_v, back_out, back_in, gate_v, up_v, down_v,
-    sum_gate, sum_up, sum_down, grad_gate, grad_up, grad_down, mixed_v, gate_probs, gsent_out, side_out,
-    x_send, x_recv, back_send, back_recv, line_send, line_recv, local,
+    y_hbm, grads_hbm,
+    sent_in, x_out, x_in, y_v, back_out, back_in, gate_v, up_v, down_v,
+    sum_gate, sum_up, sum_down, grads_v, mixed_v, gate_probs, gsent_out, side_out, cots_v,
+    note_out, note_in, answer_out, answer_in,
+    x_send, x_recv, back_send, back_recv, note_send, note_recv, answer_send, answer_recv,
+    line_send, line_recv, local,
 ):
     me = position(AXES)
     x_at, y_at, z_at, c_at = (me[axis] for axis in AXES)
@@ -1039,7 +957,7 @@
     loads = [
         pltpu.make_async_copy(src, dst, local.at[i])
         for i, (src, dst) in enumerate(
-            ((g_hbm, g_v), (gate_hbm, gate_v), (up_hbm, up_v), (down_hbm, down_v))
+            ((cots_hbm, cots_v), (gate_hbm, gate_v), (up_hbm, up_v), (down_hbm, down_v))
         )
     ]
     for item in loads:
@@ -1053,6 +971,9 @@
         return carry
 
     lax.fori_loop(0, 31, hello, 0)
+    sum_gate[...] = jnp.zeros_like(sum_gate)
+    sum_up[...] = jnp.zeros_like(sum_up)
+    sum_down[...] = jnp.zeros_like(sum_down)
     pl.semaphore_wait(barrier, 31 + len(LINE_OFFSETS))
 
     here_line = x_at * 2 + c_at
@@ -1075,6 +996,29 @@
     scale = lax.rsqrt(jnp.mean(residual * residual, axis=-1, keepdims=True) + EPSILON)
     mixed = (residual * scale * gain).astype(BF16)
     mixed_v[...] = mixed
+    put = put_ref[...]
+
+    def slots(value):
+        return value.reshape(EXPERTS, SLOT, value.shape[1]).astype(BF16)
+
+    x_out[:, :, 0:512] = slots(mm(put, mixed[:, 0:512]))
+    x_out[:, :, 512:1024] = slots(mm(put, mixed[:, 512:1024]))
+
+    def x_copy(k):
+        to = toward(k)
+        return remote(x_out.at[number(to)], x_in.at[k], x_send, x_recv, k, to)
+
+    def note_copy(k):
+        to = toward(k)
+        return remote(note_out.at[number(to)], note_in.at[k], note_send, note_recv, k, to)
+
+    def x_start(k, carry):
+        x_copy(k).start()
+        return carry
+
+    lax.fori_loop(0, 8, x_start, 0)
+    kept = pltpu.make_async_copy(x_out.at[expert], x_in.at[31], local.at[4])
+    kept.start()
     logits = mm(mixed, router_ref[...])
     member = member_ref[...]
     masked = jnp.where(member > 0.5, logits, -FAR)
@@ -1090,39 +1034,39 @@
     weigh_low_ref[...] = weigh_low
     weigh_high_ref.store()
     weigh_low_ref.store()
-    total = jnp.sum(weigh, axis=0, keepdims=True)
-    rows_high, rows_low = halves(expand_ref[...].astype(F32) * total)
-    rows_high = mm(rows_high, place_ref[...]).astype(BF16)
-    rows_low = mm(rows_low, place_ref[...]).astype(BF16)
-    gate_rows = mm(pick_high_ref[...], rows_high) + mm(pick_low_ref[...], rows_low)
-    put = put_ref[...]
-
-    def slots(value):
-        return value.reshape(EXPERTS, SLOT, value.shape[1]).astype(BF16)
-
-    x_out[:, :, 0:128] = slots(mm(put, mixed[:, 0:128]) + gate_rows)
-    x_out[:, :, 128:512] = slots(mm(put, mixed[:, 128:512]))
-    x_out[:, :, 512:1024] = slots(mm(put, mixed[:, 512:1024]))
-
-    def x_copy(k):
-        to = toward(k)
-        return remote(x_out.at[number(to)], x_in.at[k], x_send, x_recv, k, to)
-
-    def x_start(k, carry):
-        x_copy(k).start()
+    wide_expand = expand_ref[...].astype(F32)
+    rows_high, rows_low = halves(wide_expand * jnp.sum(weigh, axis=0, keepdims=True))
+    gates = mm(rows_high, place_ref[...]) + mm(rows_low, place_ref[...])
+    token = lax.broadcasted_iota(jnp.int32, (ROWS, SLOTS), 0).astype(F32)
+    token = jnp.sum(take_ref[...].astype(F32) * token, axis=0, keepdims=True)
+    token = mm((wide_expand * token).astype(BF16), place_ref[...])
+    top_row = lax.broadcasted_iota(jnp.int32, (8, 128), 0) == 0
+    for i in range(EXPERTS):
+        note_out[i] = jnp.where(
+            top_row,
+            jnp.broadcast_to(gates[i : i + 1], (8, 128)),
+            jnp.broadcast_to(token[i : i + 1], (8, 128)),
+        )
+
+    def note_start(k, carry):
+        note_copy(k).start()
         return carry
 
-    lax.fori_loop(0, 31, x_start, 0)
-    kept = pltpu.make_async_copy(x_out.at[expert], x_in.at[31], local.at[4])
-    kept.start()
+    lax.fori_loop(0, 31, note_start, 0)
+    lax.fori_loop(8, 31, x_start, 0)
+    note_in[31] = note_out[expert]
     kept.wait()
-    sum_gate[...] = jnp.zeros_like(sum_gate)
-    sum_up[...] = jnp.zeros_like(sum_up)
-    sum_down[...] = jnp.zeros_like(sum_down)
     for item in loads:
         item.wait()
-    for item in (block_place_ref, select_ref, high_ref, low_ref):
-        item.get()
+
+    def cot_of(at):
+        return cots_v[number(at)]
+
+    slot_lane = lane_index((SLOT, 128))
+    own_lane = slot_lane == lax.broadcasted_iota(jnp.int32, (SLOT, 128), 0)
+
+    def answer_copy(k):
+        return remote(answer_out.at[k], answer_in.at[expert], answer_send, answer_recv, k, source(k))
 
     def back_copy(k):
         to = source(k)
@@ -1139,11 +1083,17 @@
             @pl.when(k < 31)
             def _():
                 x_copy(k).wait_recv()
+                note_copy(k).wait_recv()
 
         x = x_in[pl.ds(first, 8)].astype(F32).reshape(BLOCK, D).astype(BF16)
-        g = jnp.concatenate([g_v[number(source(first + i))].astype(F32) for i in range(8)], axis=0)
-        place = block_place_ref[...].astype(F32)
-        share = jnp.sum(mm(select_ref[...], x[:, :128]) * place, axis=1, keepdims=True)
+        share, chosen = [], []
+        for i in range(8):
+            note = note_in[first + i]
+            share.append(jnp.sum(jnp.where(own_lane, note[0:1], 0.0), axis=1, keepdims=True))
+            row = jnp.sum(jnp.where(own_lane, note[1:2], 0.0), axis=1, keepdims=True)
+            chosen.append(jnp.where(slot_lane.astype(F32) == row, 1.0, 0.0).astype(BF16))
+        share = jnp.concatenate(share, axis=0)
+        g = jnp.concatenate([mm(chosen[i], cot_of(source(first + i))) for i in range(8)], axis=0)
         a = mm(x, gate_v[...])
         b = mm(x, up_v[...])
         s = 1.0 / (1.0 + jnp.exp(-a))
@@ -1151,6 +1101,16 @@
         hidden = (silu * b).astype(BF16)
         y = mm(hidden, down_v[...]).astype(BF16).astype(F32)
         dgate = jnp.sum(y * g, axis=1, keepdims=True)
+        for i in range(8):
+            k = first + i
+            own = dgate[i * SLOT : (i + 1) * SLOT]
+            row = jnp.sum(jnp.where(own_lane, own, 0.0), axis=0, keepdims=True)
+            answer_out[k] = jnp.broadcast_to(row, (8, 128))
+
+            @pl.when(k < 31)
+            def _():
+                answer_copy(k).start()
+
         y = y.reshape(8, SLOT, D)
         for i in range(8):
             y_v[number(source(first + i))] = y[i].astype(BF16)
@@ -1159,11 +1119,7 @@
         da = (dhidden * b * (s * (1.0 + a * (1.0 - s)))).astype(BF16)
         db = (dhidden * silu).astype(BF16)
         back = mm(da, gate_v[...], NT) + mm(db, up_v[...], NT)
-        dgate_high, dgate_low = halves(dgate * place)
-        lead = back[:, 0:128] + mm(high_ref[...], dgate_high) + mm(low_ref[...], dgate_low)
-        span = pl.ds(first, 8)
-        back_out[span, :, 0:128] = lead.reshape(8, SLOT, 128).astype(BF16)
-        back_out[span, :, 128:1024] = back[:, 128:1024].reshape(8, SLOT, 896).astype(BF16)
+        back_out[pl.ds(first, 8)] = back.reshape(8, SLOT, D).astype(BF16)
         for i in range(8):
             k = first + i
 
@@ -1181,35 +1137,28 @@
         return carry
 
     lax.fori_loop(0, 4, group, 0)
-    grad_gate[...] = sum_gate[...].astype(BF16)
-    grad_up[...] = sum_up[...].astype(BF16)
-    grad_down[...] = sum_down[...].astype(BF16)
+    answer_in[expert] = answer_out[31]
+    for i in range(4):
+        grads_v[i * 768 : i * 768 + 256] = sum_gate[i * 256 : (i + 1) * 256].astype(BF16)
+        grads_v[i * 768 + 256 : i * 768 + 512] = sum_up[i * 256 : (i + 1) * 256].astype(BF16)
+        down = sum_down[i * 128 : (i + 1) * 128].astype(BF16)
+        grads_v[i * 768 + 512 : i * 768 + 640] = down[:, 0:FF]
+        grads_v[i * 768 + 640 : i * 768 + 768] = down[:, FF:D]
     stores = [
         pltpu.make_async_copy(src, dst, local.at[i])
-        for i, (src, dst) in enumerate(
-            ((y_v, y_hbm), (grad_gate, grad_gate_hbm), (grad_up, grad_up_hbm), (grad_down, grad_down_hbm))
-        )
+        for i, (src, dst) in enumerate(((y_v, y_hbm), (grads_v, grads_hbm)))
     ]
     for item in stores:
         item.start()
 
-    def settle(k, carry):
-        x_copy(k).wait_send()
-        back_copy(k).wait()
+    def answers(k, carry):
+        answer_copy(k).wait()
         return carry
 
-    lax.fori_loop(0, 31, settle, 0)
-    back_kept().wait()
-
+    lax.fori_loop(0, 31, answers, 0)
     take = take_ref[...]
     rows_high, rows_low = halves(
-        sum(
-            mm(
-                pick_t_ref[:, i * 640 : (i + 1) * 640],
-                back_in[i * 16 : (i + 1) * 16, :, 0:128].astype(F32).reshape(640, 128).astype(BF16),
-            )
-            for i in range(2)
-        )
+        jnp.concatenate([answer_in[i][0:1] for i in range(EXPERTS)] + [jnp.zeros((96, 128), F32)], axis=0)
     )
     spread = mm(rows_high, place_t_ref[...]) + mm(rows_low, place_t_ref[...])
     along = jnp.sum(spread * expand_ref[...].astype(F32), axis=0, keepdims=True)
@@ -1219,6 +1168,16 @@
     dlogits = gate * (dgate - jnp.sum(gate * dgate, axis=1, keepdims=True))
     dlogits = dlogits.astype(BF16)
     dmixed = mm(dlogits, router_ref[...], NT)
+
+    def settle(k, carry):
+        x_copy(k).wait_send()
+        note_copy(k).wait_send()
+        back_copy(k).wait()
+        return carry
+
+    lax.fori_loop(0, 31, settle, 0)
+    back_kept().wait()
+
     for i in range(2):
         rows = back_in[i * 16 : (i + 1) * 16].astype(F32).reshape(640, D).astype(BF16)
         dmixed += mm(take[:, i * 640 : (i + 1) * 640], rows)
@@ -1276,7 +1235,7 @@
     return remote_call(
         moe_kernel,
         inputs,
-        ("h", "l", (0, D), (D, D + 128)) + ("l",) * 15 + ("h",) * 4,
+        ("h", "l", (0, D), (D, D + 128)) + ("l",) * 8 + ("h",) * 4,
         [
             shape((ROWS, D), F32),
             shape((ROWS, SLOTS), BF16),
@@ -1286,14 +1245,11 @@
             shape((8, ROWS, 128), BF16),
             shape((8, ROWS, 128), BF16),
             shape(slots, BF16),
-            shape(up, BF16),
-            shape(up, BF16),
-            shape(down, BF16),
+            shape((3 * D, FF), BF16),
         ],
-        ("e", "e", "e", "e", "e", "v", "v", "h", "h", "h", "h"),
+        ("e", "e", "e", "e", "e", "v", "v", "h", "h"),
         [
             pltpu.VMEM((8, ROWS, 128), BF16),
-            pltpu.VMEM(slots, BF16),
             pltpu.VMEM(slots, BF16),
             pltpu.VMEM(slots, BF16),
             pltpu.VMEM(slots, BF16),
@@ -1305,17 +1261,19 @@
             pltpu.VMEM(up, F32),
             pltpu.VMEM(up, F32),
             pltpu.VMEM(down, F32),
-            pltpu.VMEM(up, BF16),
-            pltpu.VMEM(up, BF16),
-            pltpu.VMEM(down, BF16),
+            pltpu.VMEM((3 * D, FF), BF16),
             pltpu.VMEM((ROWS, D), BF16),
             pltpu.VMEM((ROWS, 128), F32),
             pltpu.VMEM((8, ROWS, 128), BF16),
             pltpu.VMEM((8, ROWS, 128), BF16),
-            dma((31,)),
-            dma((31,)),
-            dma((31,)),
-            dma((31,)),
+            pltpu.VMEM((EXPERTS, ROWS, D), BF16),
+            pltpu.VMEM((EXPERTS, 8, 128), F32),
+            pltpu.VMEM((EXPERTS, 8, 128), F32),
+            pltpu.VMEM((EXPERTS, 8, 128), F32),
+            pltpu.VMEM((EXPERTS, 8, 128), F32),
+        ]
+        + [dma((31,))] * 8
+        + [
             dma((21,)),
             dma((21,)),
             dma((6,)),
@@ -1324,12 +1282,13 @@
     )
 
 
-def finish_kernel(
-    dq_ref, dkv_ref, cos_ref, sin_ref, normed_ref, w_ref,
-    y_ref, weigh_high_ref, weigh_low_ref, residual_ref, out_ref, side_ref,
+def tail_kernel(
+    partial_ref, sent_ref, branch_ref, side_rows_ref, dq_ref, cos_ref, sin_ref, normed_ref, w_ref,
+    y_ref, weigh_high_ref, weigh_low_ref, residual_ref,
     dnormed_out, mixed_out, grads_out, early_out,
     dqkv, part_out, part_in, part_own, line_out, line_in, share_out, share_in, total,
-    out_in, side_in, send, recv, local, out_recv,
+    out_in, side_in, dkv_ref, out_ref, side_ref, far_a, near_a, out_a, sum_a, far_b, near_b, out_b,
+    plane_send, plane_recv, send, recv, local, out_recv,
 ):
     me = position(AXES)
     x, y, z, c = (me[axis] for axis in AXES)
@@ -1356,7 +1315,17 @@
     offsets = LINE_OFFSETS + PLANE_OFFSETS
     for offset in offsets:
         pl.semaphore_signal(barrier, inc=1, device_id=moved(me, offset), device_id_type=MESH)
+    grad_out = mm(sent_ref[...], branch_ref[...], TN)
+    for j in range(16):
+        out_ref[j] = grad_out[j * 8 : (j + 1) * 8]
+    side = side_rows_ref[0].astype(F32)
+    for i in range(1, 8):
+        side += side_rows_ref[i].astype(F32)
+    side_ref[...] = side.reshape(16, 8, 128)
     pl.semaphore_wait(barrier, len(offsets) + 16 - alone)
+    scatter_plane(
+        me, partial_ref, dkv_ref, far_a, near_a, out_a, sum_a, far_b, near_b, out_b, plane_send, plane_recv
+    )
     used = [0]
 
     def go(src, dst, to):
@@ -1411,7 +1380,7 @@
     def turn_back(first):
         rows = pl.ds(pl.multiple_of(first, 256), 256)
         cos, sin = cos_ref[rows, :], sin_ref[rows, :]
-        dq, dkv = dq_ref[rows, :], dkv_ref[rows, :]
+        dq, dkv = dq_ref[rows, :], dkv_ref[lax.div(first, 512), pl.ds(lax.rem(first, 512), 256), :]
         dq = (dq * cos - turned(dq) * sin).astype(BF16)
         dkv = jnp.where(low_lanes, dkv * cos - turned(dkv) * sin, dkv).astype(BF16)
         both = jnp.concatenate([dq, dkv], axis=1)
@@ -1495,12 +1464,12 @@
         item.wait()
 
 
-def finish(inputs, cid):
+def tail(inputs, cid):
     count = 2 + 3 + 15 + 7 + 16 + 15
     return remote_call(
-        finish_kernel,
+        tail_kernel,
         inputs,
-        ("l", "l", "l", "l", "l", (0, 256), "l", "l", "l", "l", "h", "h"),
+        ("l",) * 8 + ((0, 256), "v", "l", "l", "l"),
         [
             shape((ROWS, D), F32),
             shape((ROWS, D), BF16),
@@ -1520,6 +1489,18 @@
             pltpu.VMEM((4, 2, 8, 256), F32),
             pltpu.VMEM((16, 8, D), F32),
             pltpu.VMEM((16, 8, 128), F32),
+            pltpu.VMEM((2, 512, 128), F32),
+            pltpu.VMEM((16, 8, D), F32),
+            pltpu.VMEM((16, 8, 128), F32),
+            pltpu.VMEM((2, 4, 2, 256, 128), BF16),
+            pltpu.VMEM((2, 4, 2, 512, 128), BF16),
+            pltpu.VMEM((2, 4, 2, 512, 128), BF16),
+            pltpu.VMEM((2, 2, 512, 128), F32),
+            pltpu.VMEM((2, 2, 256, 128), BF16),
+            pltpu.VMEM((2, 2, 512, 128), BF16),
+            pltpu.VMEM((2, 3, 512, 128), BF16),
+            pltpu.SemaphoreType.DMA((40,)),
+            pltpu.SemaphoreType.DMA((40,)),
             pltpu.SemaphoreType.DMA((count,)),
             pltpu.SemaphoreType.DMA((count,)),
             pltpu.SemaphoreType.DMA((3,)),
@@ -1531,7 +1512,7 @@
 
 def last_kernel(
     dnormed_ref, tok_ref, gain_ref, gmid_ref, mixed_ref, rows_ref, wq_ref, wk_ref, wv_ref, own_gain_ref, early_ref,
-    gate_ref, up_ref, down_ref,
+    grads_ref,
     tokens_out, mixed_out, query_out, key_out, value_out, gains_out, grad_out, router_out,
     gate_out, up_out, down_out,
 ):
@@ -1560,9 +1541,10 @@
     gains_out[1:2, :] = gain_two[:, 0:8]
     grad_out[...] = early_ref[:, 0:D]
     router_out[...] = side[:, 0:EXPERTS]
-    gate_out[...] = gate_ref[...].astype(F32)
-    up_out[...] = up_ref[...].astype(F32)
-    down_out[...] = down_ref[...].astype(F32)
+    gate_out[...] = grads_ref[0:256].astype(F32)
+    up_out[...] = grads_ref[256:512].astype(F32)
+    down_out[:, 0:FF] = grads_ref[512:640].astype(F32)
+    down_out[:, FF:D] = grads_ref[640:768].astype(F32)
 
 
 def body(
@@ -1585,16 +1567,17 @@
     y_at, z_at = lax.axis_index("y"), lax.axis_index("z")
     first_row = (y_at * 4 + z_at) * CHIP_ROWS
 
+    cot_rows = lax.all_gather(cotangent, ("y", "z", "c"), axis=0, tiled=True)
+
     expand, expand_t = expand_matrix(), expand_matrix().T
     place, place_t = place_matrix(), place_matrix().T
-    pick_high, pick_low = pick_matrix(CAP), pick_matrix(CAP + 1)
     (
         query, kv, gain_first, cos, sin, w_mine, member, put, take, own_aux, order_rows, key_norm,
-        kv_all, w_late, normed, g_out, aux,
+        kv_all, w_late, normed, aux,
     ) = front(
         (
             lengths, tokens, w_query, w_key, w_value, w_out, w_router, gain_one.reshape(1, 8),
-            gain_two.reshape(1, 8), dealt_order.reshape(128, 128), routes.T, cotangent,
+            gain_two.reshape(1, 8), dealt_order.reshape(128, 128), routes.T,
             expand, expand_t, place_column(), place_row(), turn_tables(128), turn_tables(1),
         ),
         1,
@@ -1602,7 +1585,6 @@
     kv_all = kv_all.reshape(TOKENS, 128)
     w_late = w_late.reshape(D, 1152)
     plane = ("y", "z", "c")
-    g_in = lax.all_to_all(g_out, plane, split_axis=0, concat_axis=0, tiled=True)
 
     base = first_row.reshape(1).astype(jnp.int32)
     att, norm, sent, query_ext = attend(
@@ -1610,41 +1592,31 @@
     )
 
     (
-        residual, weigh_high, weigh_low, gmid, branch, gsent_own, side_rows, y_out,
-        grad_gate, grad_up, grad_down,
+        residual, weigh_high, weigh_low, gmid, branch, gsent_own, side_rows, y_out, expert_grads,
     ) = moe(
         (
             sent.reshape(8, ROWS, 128), tokens, w_late, w_late, member, put, take, expand, expand_t,
-            place, place_t, pick_high, pick_low, (pick_high + pick_low).T, cotangent,
-            block_matrix((CAP, CAP + 1)),
-            place[:BLOCK],
-            block_matrix((CAP,)).T * constant(BLOCK_PLACE == CAP)[:, None],
-            block_matrix((CAP + 1,)).T * constant(BLOCK_PLACE == CAP + 1)[:, None],
-            g_in, w_gate[0], w_up[0], w_down[0],
+            place, place_t, cotangent,
+            cot_rows.reshape(EXPERTS, ROWS, D), w_gate[0], w_up[0], w_down[0],
         ),
         3,
     )
     y_in = lax.all_to_all(
         y_out, plane, split_axis=0, concat_axis=0, tiled=True
     ).reshape(SLOTS, D)
-    grad_gate, grad_up, grad_down = (
-        lax.psum_scatter(grad, "x", scatter_dimension=0, tiled=True)
-        for grad in (grad_gate, grad_up, grad_down)
-    )
+    expert_grads = lax.psum_scatter(expert_grads, "x", scatter_dimension=0, tiled=True)
 
     gsent_own = gsent_own.reshape(CHIP_ROWS, 128)
     branch_rows = lax.all_gather(branch, ("c", "x"), axis=0, tiled=True)
-    side_sum = jnp.sum(side_rows.astype(F32), axis=0)
 
     dq, dkv = attend_back(
         dealt_order, base, kv_all, aux, kv, own_aux, query_ext, order_rows, gsent_own, att, norm
     )
-    dkv_own, grad_out = scatter_plane(dkv, sent, branch_rows, 6)
-
-    dnormed, mixed, qkv_rows, early = finish(
+
+    dnormed, mixed, qkv_rows, early = tail(
         (
-            dq, dkv_own, cos, sin, normed, w_mine, y_in, weigh_high, weigh_low, residual,
-            grad_out.reshape(16, 8, D), side_sum.reshape(16, 8, 128),
+            dkv.reshape(4, 4, 2, 512, 128), sent, branch_rows, side_rows, dq, cos, sin, normed, w_mine,
+            y_in, weigh_high, weigh_low, residual,
         ),
         7,
     )
@@ -1668,7 +1640,7 @@
         ),
     )(
         dnormed, tokens, gain_first, gmid, mixed, qkv_rows, w_query, w_key, w_value,
-        gain_one.reshape(1, 8), early, grad_gate, grad_up, grad_down,
+        gain_one.reshape(1, 8), early, expert_grads,
     )
     grad_gain_one, grad_gain_two = gains[0], gains[1]
     grad_gate, grad_up, grad_down = grad_gate[None], grad_up[None], grad_down[None]

time: 312 us -> 302 us (0.968)
  Pallas kernels: 261 us -> 276 us
  waiting for transfers between devices: 14.1 us -> 1.44 us
  starting transfers between devices: 16.3 us -> 8.01 us
    pallas_call x4 -> x3, Pallas kernels: 202 us -> 221 us  [remote_call(): pl.pallas_call(wrapped, out_shape=list(outs), in_specs=[pl.BlockSpec(memo...]
    all_to_all x1 -> x0, waiting for transfers between devices: 12.7 us -> none  [body(): g_in = lax.all_to_all(g_out, plane, split_axis=0, concat_axis=0, tiled=True)]
    all_to_all x1 -> x0, starting transfers between devices: 7.66 us -> none  [body(): g_in = lax.all_to_all(g_out, plane, split_axis=0, concat_axis=0, tiled=True)]
  transfers between devices with their start and end apart: 6 -> 4, of which waited for: 1 -> 0; matrix products, arithmetic and copies ran while one was open for 0% -> 0% of each run, Pallas kernels for 36% -> 58%
where the time goes in v3:
time: 302 us
  Pallas kernels  276 us (91%)
  between operations  13.9 us (5%)
  starting transfers between devices  8.01 us (3%)
    pallas_call x3, Pallas kernels, remote_call(): pl.pallas_call(wrapped, out_shape=list(outs), in_specs=[pl.BlockSpec(memo...  221 us
    pallas_call x1, Pallas kernels, attend_back(): local_call(attend_back_kernel, (shape((CHIP_ROWS, 128), F32), shape((TOKE...  33.9 us
    pallas_call x1, Pallas kernels, attend(): local_call(attend_kernel, (shape((CHIP_ROWS, 128), F32), shape((CHIP_ROWS...  17.9 us
    all_to_all x1, starting transfers between devices, body(): lax.all_to_all(y_out, plane, split_axis=0, concat_axis=0, tiled=True)  7.9 us
  transfers between devices with their start and end apart: 4, of which 0 were waited for; matrix products, arithmetic and copies ran while one was open for 0% of the time, Pallas kernels for 58%

profile of v3, /device:TPU:1, one launch (start us, length us, event | category | flops | bytes accessed | tf_op | source)
XLA Modules:
  0.0 301.7 jit_solution(5005831500333128267)
XLA Ops:
  7.2 0.0 all-gather.3.cloned.1.call-start
  7.2 0.7 all-gather.3.cloned.1.call-update
  7.9 0.0 all-gather.5.cloned.1.call-start
  8.0 66.9 %shard_map.310 = (bf16[2,1024,128]{2,1,0:T(8,128)(2,1)}, bf16[1024,128]{1,0:T(8,128)(2,1)}, f32[1,1024]{1,0:T(1,128)}, f32[1024,128]{1,0:T(8,128)}, f32[1024,128...) custom-call(s32[5]{0:T(128)} %refs_0_.1, ...), custom_call_target="tpu_custom_call" | custom-call | tf_op jit(solution)/shard_map/pallas_call | solution.py:128
  74.8 17.9 %shard_map.311 = (f32[1024,128]{1,0:T(8,128)}, f32[1024,128]{1,0:T(8,128)}, bf16[1024,128]{1,0:T(8,128)(2,1)}, bf16[4,512,256]{2,1,0:T(8,128)(2,1)}) custom-call(s32[16384]{0:T(1024)} %order_smem.3, s32[1]{0:T(128)} %bitcast.base_ref, bf16[16384,128]{1,0:T(8,128)(2,1)} %bitcast.22, bf16[16384,128]{1,0:T(8,128)(2,1)} %get-tuple-element.59.aux_hbm, ...), custom_call_target="tpu_custom_call" | custom-call | tf_op jit(solution)/shard_map/pallas_call | solution.py:721
  92.8 0.0 all-gather.3.cloned.1.call-done
  92.8 96.9 %shard_map.312 = (f32[128,1024]{1,0:T(8,128)}, bf16[128,1280]{1,0:T(8,128)(2,1)}, bf16[128,1280]{1,0:T(8,128)(2,1)}, f32[128,1024]{1,0:T(8,128)}, bf16[128,1024]...) custom-call(bf16[8,128,128]{2,1,0:T(8,128)(2,1)} %bitcast.29, ...), custom_call_target="tpu_custom_call" | custom-call | tf_op jit(solution)/shard_map/pallas_call | solution.py:128
  189.7 0.0 all-gather.5.cloned.1.call-update
  189.7 0.0 reduce-scatter.2.cloned.1.call-start
  189.8 0.7 reduce-scatter.2.cloned.1.call-update
  190.5 7.9 %all-to-all-start = ((bf16[32,40,1024]{2,1,0:T(8,128)(2,1)}), bf16[32,40,1024]{2,1,0:T(8,128)(2,1)S(1)}, u32[]{:S(2)}, u32[]{:S(2)}) async-start(bf16[32,40,1024]{2,1,0:T(8,128)(2,1)} %get-tuple-element.82), calls=%async_computation | async-start | bytes 5242880 | tf_op jit(solution)/shard_map/all_to_all | solution.py:1604
  198.4 33.9 %shard_map.313 = (f32[1024,128]{1,0:T(8,128)}, bf16[16384,128]{1,0:T(8,128)(2,1)}) custom-call(s32[16384]{0:T(1024)} %order_smem.3, s32[1]{0:T(128)} %bitcast.base_ref, bf16[16384,128]{1,0:T(8,128)(2,1)} %bitcast.23, bf16[16384,128]{1,0:T(8,128)(2,1)} %get-tuple-element.59.aux_hbm, bf16[1024,128]{1,0:T(8,128)(2,1)} %get-tuple-element.60.own_kv_ref, ...), custom_call_target="tpu_custom_call" | custom-call | tf_op jit(solution)/shard_map/pallas_call | solution.py:852
  232.3 0.0 all-to-all-done
  232.3 0.0 copy-start
  232.3 0.0 all-gather.5.cloned.1.call-done.refs_2_
  232.3 1.5 copy-done
  233.8 56.8 %shard_map.314 = (f32[128,1024]{1,0:T(8,128)}, bf16[128,1024]{1,0:T(8,128)(2,1)}, f32[8,8,256]{2,1,0:T(8,128)}, f32[8,1152]{1,0:T(8,128)}) custom-call(bf16[4,4,2,512,128]{4,3,2,1,0:T(8,128)(2,1)} %bitcast.28, bf16[1024,128]{1,0:T(8,128)(2,1)} %get-tuple-element.66.refs_1_, bf16[1024,1024]{1,0:T(8,128)(2,1)} %all-gather.5.cloned.1.call-done.refs_2_, ...), custom_call_target="tpu_custom_call" | custom-call | tf_op jit(solution)/shard_map/pallas_call | solution.py:128
  290.6 0.0 reduce-scatter.2.cloned.1.call-done.grads_ref
  290.7 3.3 %shard_map.315 = (f32[128,1024]{1,0:T(8,128)}, bf16[128,1024]{1,0:T(8,128)(2,1)}, f32[8,1024]{1,0:T(8,128)}, f32[8,512]{1,0:T(8,128)}, f32[8,512]{1,0:T(8,128)},...) custom-call(f32[128,1024]{1,0:T(8,128)} %get-tuple-element.86.dnorme, ...), custom_call_target="tpu_custom_call" | custom-call | tf_op jit(solution)/shard_map/pallas_call | solution.py:1626
  294.0 1.2 slice_bitcast_fusion
Async XLA Ops:
  7.2 85.6 %all-gather.3.cloned.1.call-start = ((), (), s32[]{:S(2)}) async-start(), calls=%async_computation.2 | async-start | bytes 8650752 | tf_op jit(solution)/shard_map/all_gather | solution.py:1570
  7.9 224.4 %all-gather.5.cloned.1.call-start = ((), (), s32[]{:S(2)}) async-start(), calls=%async_computation.3 | async-start | bytes 2359296 | tf_op jit(solution)/shard_map/all_gather | solution.py:1610
  189.7 100.9 %reduce-scatter.2.cloned.1.call-start = ((), (), s32[]{:S(2)}) async-start(), calls=%async_computation.4 | async-start | bytes 3932160 | tf_op jit(solution)/shard_map/reduce_scatter | solution.py:1607
  190.5 41.8 %all-to-all-start = ((bf16[32,40,1024]{2,1,0:T(8,128)(2,1)}), bf16[32,40,1024]{2,1,0:T(8,128)(2,1)S(1)}, u32[]{:S(2)}, u32[]{:S(2)}) async-start(bf16[32,40,1024]{2,1,0:T(8,128)(2,1)} %get-tuple-element.82), calls=%async_computation | async-start | bytes 5242880 | tf_op jit(solution)/shard_map/all_to_all | solution.py:1604
  232.3 1.5 copy-start
Sparse Core Ops, SparseCore 0:
  10.3 71.1 all-gather.2
  189.8 26.5 all-gather.4
  218.8 38.1 reduce-scatter.1

commit v4 on v3

--- a/solution.py
+++ b/solution.py
@@ -18,7 +18,7 @@
 EXPERTS = 32
 FF = 512
 CAP = 36
-SLOT = 40
+SLOT = CAP
 SLOTS = EXPERTS * SLOT
 ROWS = 128
 CHIP_ROWS = 1024
@@ -885,8 +885,8 @@
     return constant(SLOT_PLACE[:, None] == np.arange(128)[None, :])
 
 
-def pick_matrix(place):
-    return constant((SLOT_EXPERT[:, None] == np.arange(128)[None, :]) & (SLOT_PLACE[:, None] == place))
+def origin_matrix():
+    return constant((np.arange(8 * SLOT) // SLOT)[:, None] == np.arange(128)[None, :])
 
 
 def place_column():
@@ -900,13 +900,6 @@
 
 
 BLOCK = 8 * SLOT
-BLOCK_SOURCE = np.arange(BLOCK) // SLOT
-BLOCK_PLACE = np.arange(BLOCK) % SLOT
-
-
-def block_matrix(places):
-    hit = np.isin(BLOCK_PLACE, places)[None, :] & (BLOCK_SOURCE[:, None] == BLOCK_SOURCE[None, :])
-    return constant(hit)
 
 
 def packed_pairs(values):
@@ -920,7 +913,7 @@
 
 def moe_kernel(
     sent_ref, tok_ref, w_out_ref, router_ref, member_ref, put_ref, take_ref, expand_ref,
-    expand_t_ref, place_ref, place_t_ref, cot_ref, cots_hbm, gate_hbm, up_hbm, down_hbm,
+    expand_t_ref, place_ref, place_t_ref, origin_ref, block_place_ref, cot_ref, cots_hbm, gate_hbm, up_hbm, down_hbm,
     residual_ref, weigh_high_ref, weigh_low_ref, gmid_ref, branch_ref, gsent_in, side_in,
     y_hbm, grads_hbm,
     sent_in, x_out, x_in, y_v, back_out, back_in, gate_v, up_v, down_v,
@@ -998,11 +991,14 @@
     mixed_v[...] = mixed
     put = put_ref[...]
 
-    def slots(value):
-        return value.reshape(EXPERTS, SLOT, value.shape[1]).astype(BF16)
-
-    x_out[:, :, 0:512] = slots(mm(put, mixed[:, 0:512]))
-    x_out[:, :, 512:1024] = slots(mm(put, mixed[:, 512:1024]))
+    def tiles(value):
+        return value.reshape(8, SLOT, 8, 128).astype(BF16)
+
+    def rows_of(value):
+        return value.astype(F32).reshape(value.shape[0] * SLOT, D).astype(BF16)
+
+    for i in range(4):
+        x_out[i * 8 : (i + 1) * 8] = tiles(mm(put[i * BLOCK : (i + 1) * BLOCK], mixed))
 
     def x_copy(k):
         to = toward(k)
@@ -1062,8 +1058,12 @@
     def cot_of(at):
         return cots_v[number(at)]
 
-    slot_lane = lane_index((SLOT, 128))
-    own_lane = slot_lane == lax.broadcasted_iota(jnp.int32, (SLOT, 128), 0)
+    block_row = lax.broadcasted_iota(jnp.int32, (BLOCK, 1), 0)
+    block_start = jnp.zeros((BLOCK, 1), F32)
+    for i in range(1, 8):
+        block_start += jnp.where(block_row >= i * SLOT, 128.0, 0.0)
+    origin_ref.get()
+    block_place_ref.get()
 
     def answer_copy(k):
         return remote(answer_out.at[k], answer_in.at[expert], answer_send, answer_recv, k, source(k))
@@ -1085,15 +1085,18 @@
                 x_copy(k).wait_recv()
                 note_copy(k).wait_recv()
 
-        x = x_in[pl.ds(first, 8)].astype(F32).reshape(BLOCK, D).astype(BF16)
-        share, chosen = [], []
-        for i in range(8):
-            note = note_in[first + i]
-            share.append(jnp.sum(jnp.where(own_lane, note[0:1], 0.0), axis=1, keepdims=True))
-            row = jnp.sum(jnp.where(own_lane, note[1:2], 0.0), axis=1, keepdims=True)
-            chosen.append(jnp.where(slot_lane.astype(F32) == row, 1.0, 0.0).astype(BF16))
-        share = jnp.concatenate(share, axis=0)
-        g = jnp.concatenate([mm(chosen[i], cot_of(source(first + i))) for i in range(8)], axis=0)
+        x = rows_of(x_in[pl.ds(first, 8)])
+        origin, place = origin_ref[...], block_place_ref[...].astype(F32)
+        blank = jnp.zeros((120, 128), F32)
+        gates = [note_in[first + i][0:1] for i in range(8)]
+        gates_high, gates_low = halves(jnp.concatenate(gates + [blank], axis=0))
+        share = mm(origin, gates_high) + mm(origin, gates_low)
+        share = jnp.sum(share * place, axis=1, keepdims=True)
+        tokens = [note_in[first + i][1:2] for i in range(8)]
+        row = mm(origin, jnp.concatenate(tokens + [blank], axis=0).astype(BF16))
+        row = jnp.sum(row * place, axis=1, keepdims=True) + block_start
+        chosen = jnp.where(lane_index((BLOCK, D)).astype(F32) == row, 1.0, 0.0).astype(BF16)
+        g = mm(chosen, jnp.concatenate([cot_of(source(first + i)) for i in range(8)], axis=0))
         a = mm(x, gate_v[...])
         b = mm(x, up_v[...])
         s = 1.0 / (1.0 + jnp.exp(-a))
@@ -1101,25 +1104,25 @@
         hidden = (silu * b).astype(BF16)
         y = mm(hidden, down_v[...]).astype(BF16).astype(F32)
         dgate = jnp.sum(y * g, axis=1, keepdims=True)
+        dgate_high, dgate_low = halves(dgate * place)
+        answers = mm(origin, dgate_high, TN) + mm(origin, dgate_low, TN)
         for i in range(8):
             k = first + i
-            own = dgate[i * SLOT : (i + 1) * SLOT]
-            row = jnp.sum(jnp.where(own_lane, own, 0.0), axis=0, keepdims=True)
-            answer_out[k] = jnp.broadcast_to(row, (8, 128))
+            answer_out[k] = jnp.broadcast_to(answers[i : i + 1], (8, 128))
 
             @pl.when(k < 31)
             def _():
                 answer_copy(k).start()
 
-        y = y.reshape(8, SLOT, D)
+        y = tiles(y)
         for i in range(8):
-            y_v[number(source(first + i))] = y[i].astype(BF16)
+            y_v[number(source(first + i))] = y[i]
         gy = (g * share).astype(BF16)
         dhidden = mm(gy, down_v[...], NT)
         da = (dhidden * b * (s * (1.0 + a * (1.0 - s)))).astype(BF16)
         db = (dhidden * silu).astype(BF16)
         back = mm(da, gate_v[...], NT) + mm(db, up_v[...], NT)
-        back_out[pl.ds(first, 8)] = back.reshape(8, SLOT, D).astype(BF16)
+        back_out[pl.ds(first, 8)] = tiles(back)
         for i in range(8):
             k = first + i
 
@@ -1178,9 +1181,7 @@
     lax.fori_loop(0, 31, settle, 0)
     back_kept().wait()
 
-    for i in range(2):
-        rows = back_in[i * 16 : (i + 1) * 16].astype(F32).reshape(640, D).astype(BF16)
-        dmixed += mm(take[:, i * 640 : (i + 1) * 640], rows)
+    dmixed += mm(take, rows_of(back_in[...]))
     residual = residual_ref[...]
     scale = lax.rsqrt(jnp.mean(residual * residual, axis=-1, keepdims=True) + EPSILON)
     gain = router_ref[...].astype(F32).T[EXPERTS : EXPERTS + 1, :]
@@ -1229,13 +1230,13 @@
 
 
 def moe(inputs, cid):
-    slots = (EXPERTS, SLOT, D)
+    slots = (EXPERTS, SLOT, 8, 128)
     up, down = (D, FF), (FF, D)
     dma = pltpu.SemaphoreType.DMA
     return remote_call(
         moe_kernel,
         inputs,
-        ("h", "l", (0, D), (D, D + 128)) + ("l",) * 8 + ("h",) * 4,
+        ("h", "l", (0, D), (D, D + 128)) + ("l",) * 10 + ("h",) * 4,
         [
             shape((ROWS, D), F32),
             shape((ROWS, SLOTS), BF16),
@@ -1415,7 +1416,8 @@
         spread.append(go(share_out.at[:, to["y"] * 4 + to["z"]], share_in.at[mine], to))
     kept = pltpu.make_async_copy(share_out.at[:, mine], share_in.at[mine], local.at[0])
     kept.start()
-    mixed = mm(weigh_high_ref[...], y_ref[...]) + mm(weigh_low_ref[...], y_ref[...])
+    outs = y_ref[...].astype(F32).reshape(SLOTS, D).astype(BF16)
+    mixed = mm(weigh_high_ref[...], outs) + mm(weigh_low_ref[...], outs)
     mixed_out[...] = (residual_ref[...] + mixed).astype(BF16)
     mixed_out.store()
     for item in spread + [kept]:
@@ -1596,14 +1598,12 @@
     ) = moe(
         (
             sent.reshape(8, ROWS, 128), tokens, w_late, w_late, member, put, take, expand, expand_t,
-            place, place_t, cotangent,
+            place, place_t, origin_matrix(), place[:BLOCK], cotangent,
             cot_rows.reshape(EXPERTS, ROWS, D), w_gate[0], w_up[0], w_down[0],
         ),
         3,
     )
-    y_in = lax.all_to_all(
-        y_out, plane, split_axis=0, concat_axis=0, tiled=True
-    ).reshape(SLOTS, D)
+    y_in = lax.all_to_all(y_out, plane, split_axis=0, concat_axis=0, tiled=True)
     expert_grads = lax.psum_scatter(expert_grads, "x", scatter_dimension=0, tiled=True)
 
     gsent_own = gsent_own.reshape(CHIP_ROWS, 128)

time: 302 us -> 292 us (0.967)
  Pallas kernels: 276 us -> 269 us
  starting transfers between devices: 8.01 us -> 4.66 us
    pallas_call x3, Pallas kernels: 221 us -> 214 us  [remote_call(): pl.pallas_call(wrapped, out_shape=list(outs), in_specs=[pl.BlockSpec(memo...]
    all_to_all x1, starting transfers between devices: 7.9 us -> 4.55 us  [body(): y_in = lax.all_to_all(y_out, plane, split_axis=0, concat_axis=0, tiled=True)]
  transfers between devices with their start and end apart: 4 -> 4, of which waited for: 0 -> 0; matrix products, arithmetic and copies ran while one was open for 0% -> 0% of each run, Pallas kernels for 58% -> 60%
where the time goes in v4:
time: 292 us
  Pallas kernels  269 us (92%)
  between operations  13.9 us (5%)
  starting transfers between devices  4.66 us (2%)
    pallas_call x3, Pallas kernels, remote_call(): pl.pallas_call(wrapped, out_shape=list(outs), in_specs=[pl.BlockSpec(memo...  214 us
    pallas_call x1, Pallas kernels, attend_back(): local_call(attend_back_kernel, (shape((CHIP_ROWS, 128), F32), shape((TOKE...  33.9 us
    pallas_call x1, Pallas kernels, attend(): local_call(attend_kernel, (shape((CHIP_ROWS, 128), F32), shape((CHIP_ROWS...  17.9 us
  transfers between devices with their start and end apart: 4, of which 0 were waited for; matrix products, arithmetic and copies ran while one was open for 0% of the time, Pallas kernels for 60%

profile of v4, /device:TPU:1, one launch (start us, length us, event | category | flops | bytes accessed | tf_op | source)
XLA Modules:
  0.0 291.7 jit_solution(9040812245160829412)
XLA Ops:
  7.2 0.0 all-gather.3.cloned.1.call-start
  7.2 0.7 all-gather.3.cloned.1.call-update
  7.9 0.0 all-gather.5.cloned.1.call-start
  8.0 66.8 %shard_map.319 = (bf16[2,1024,128]{2,1,0:T(8,128)(2,1)}, bf16[1024,128]{1,0:T(8,128)(2,1)}, f32[1,1024]{1,0:T(1,128)}, f32[1024,128]{1,0:T(8,128)}, f32[1024,128...) custom-call(s32[5]{0:T(128)} %refs_0_.1, ...), custom_call_target="tpu_custom_call" | custom-call | tf_op jit(solution)/shard_map/pallas_call | solution.py:128
  74.7 17.9 %shard_map.320 = (f32[1024,128]{1,0:T(8,128)}, f32[1024,128]{1,0:T(8,128)}, bf16[1024,128]{1,0:T(8,128)(2,1)}, bf16[4,512,256]{2,1,0:T(8,128)(2,1)}) custom-call(s32[16384]{0:T(1024)} %order_smem.3, s32[1]{0:T(128)} %bitcast.base_ref, bf16[16384,128]{1,0:T(8,128)(2,1)} %bitcast.21, bf16[16384,128]{1,0:T(8,128)(2,1)} %get-tuple-element.59.aux_hbm, ...), custom_call_target="tpu_custom_call" | custom-call | tf_op jit(solution)/shard_map/pallas_call | solution.py:721
  92.7 0.0 all-gather.3.cloned.1.call-done
  92.7 91.4 %shard_map.321 = (f32[128,1024]{1,0:T(8,128)}, bf16[128,1152]{1,0:T(8,128)(2,1)}, bf16[128,1152]{1,0:T(8,128)(2,1)}, f32[128,1024]{1,0:T(8,128)}, bf16[128,1024]...) custom-call(bf16[8,128,128]{2,1,0:T(8,128)(2,1)} %bitcast.27, ...), custom_call_target="tpu_custom_call" | custom-call | tf_op jit(solution)/shard_map/pallas_call | solution.py:128
  184.1 0.0 all-gather.5.cloned.1.call-update
  184.1 0.0 reduce-scatter.2.cloned.1.call-start
  184.2 0.7 reduce-scatter.2.cloned.1.call-update
  184.9 4.5 %all-to-all-start = ((bf16[32,36,8,128]{3,2,1,0:T(8,128)(2,1)}), bf16[32,36,8,128]{3,2,1,0:T(8,128)(2,1)S(1)}, u32[]{:S(2)}, u32[]{:S(2)}) async-start(bf16[32,36,8,128]{3,2,1,0:T(8,128)(2,1)} %get-tuple-element.82), calls=%async_computation | async-start | bytes 4718592 | tf_op jit(solution)/shard_map/all_to_all | solution.py:1606
  189.4 33.9 %shard_map.322 = (f32[1024,128]{1,0:T(8,128)}, bf16[16384,128]{1,0:T(8,128)(2,1)}) custom-call(s32[16384]{0:T(1024)} %order_smem.3, s32[1]{0:T(128)} %bitcast.base_ref, bf16[16384,128]{1,0:T(8,128)(2,1)} %bitcast.22, bf16[16384,128]{1,0:T(8,128)(2,1)} %get-tuple-element.59.aux_hbm, bf16[1024,128]{1,0:T(8,128)(2,1)} %get-tuple-element.60.own_kv_ref, ...), custom_call_target="tpu_custom_call" | custom-call | tf_op jit(solution)/shard_map/pallas_call | solution.py:852
  223.3 0.0 all-to-all-done.refs_9_
  223.4 0.0 copy-start
  223.4 0.0 all-gather.5.cloned.1.call-done.refs_2_
  223.4 1.4 copy-done
  224.8 55.7 %shard_map.323 = (f32[128,1024]{1,0:T(8,128)}, bf16[128,1024]{1,0:T(8,128)(2,1)}, f32[8,8,256]{2,1,0:T(8,128)}, f32[8,1152]{1,0:T(8,128)}) custom-call(bf16[4,4,2,512,128]{4,3,2,1,0:T(8,128)(2,1)} %bitcast.26, bf16[1024,128]{1,0:T(8,128)(2,1)} %get-tuple-element.66.refs_1_, bf16[1024,1024]{1,0:T(8,128)(2,1)} %all-gather.5.cloned.1.call-done.refs_2_, ...), custom_call_target="tpu_custom_call" | custom-call | tf_op jit(solution)/shard_map/pallas_call | solution.py:128
  280.5 0.0 reduce-scatter.2.cloned.1.call-done.grads_ref
  280.5 3.3 %shard_map.324 = (f32[128,1024]{1,0:T(8,128)}, bf16[128,1024]{1,0:T(8,128)(2,1)}, f32[8,1024]{1,0:T(8,128)}, f32[8,512]{1,0:T(8,128)}, f32[8,512]{1,0:T(8,128)},...) custom-call(f32[128,1024]{1,0:T(8,128)} %get-tuple-element.86.dnorme, ...), custom_call_target="tpu_custom_call" | custom-call | tf_op jit(solution)/shard_map/pallas_call | solution.py:1626
  283.9 1.3 slice_bitcast_fusion
Async XLA Ops:
  7.2 85.5 %all-gather.3.cloned.1.call-start = ((), (), s32[]{:S(2)}) async-start(), calls=%async_computation.2 | async-start | bytes 8650752 | tf_op jit(solution)/shard_map/all_gather | solution.py:1572
  7.9 215.5 %all-gather.5.cloned.1.call-start = ((), (), s32[]{:S(2)}) async-start(), calls=%async_computation.3 | async-start | bytes 2359296 | tf_op jit(solution)/shard_map/all_gather | solution.py:1610
  184.1 96.4 %reduce-scatter.2.cloned.1.call-start = ((), (), s32[]{:S(2)}) async-start(), calls=%async_computation.4 | async-start | bytes 3932160 | tf_op jit(solution)/shard_map/reduce_scatter | solution.py:1607
  184.9 38.5 %all-to-all-start = ((bf16[32,36,8,128]{3,2,1,0:T(8,128)(2,1)}), bf16[32,36,8,128]{3,2,1,0:T(8,128)(2,1)S(1)}, u32[]{:S(2)}, u32[]{:S(2)}) async-start(bf16[32,36,8,128]{3,2,1,0:T(8,128)(2,1)} %get-tuple-element.82), calls=%async_computation | async-start | bytes 4718592 | tf_op jit(solution)/shard_map/all_to_all | solution.py:1606
  223.4 1.4 copy-start
Sparse Core Ops, SparseCore 0:
  10.3 71.1 all-gather.2
  184.3 22.1 all-gather.4
  208.8 38.1 reduce-scatter.1

commit v5 on v4

--- a/solution.py
+++ b/solution.py
@@ -70,10 +70,14 @@
 
 
 class Late:
-    def __init__(self, hbm, vmem, sem, columns):
+    def __init__(self, hbm, vmem, sem, columns, wait):
         self.hbm, self.vmem = hbm, vmem
         source = hbm if columns is None else hbm.at[:, columns[0] : columns[1]]
         self.copy, self.ready = pltpu.make_async_copy(source, vmem, sem), False
+        if not wait:
+            self.copy.start()
+
+    def begin(self):
         self.copy.start()
 
     def get(self):
@@ -100,13 +104,16 @@
         self.copy.start()
 
 
-def remote_call(kernel, inputs, kinds, outs, out_kinds, scratch, cid):
+DEFERRED_COLUMNS = (0, 256)
+
+
+def remote_call(kernel, inputs, kinds, outs, out_kinds, scratch, cid, room=VMEM_BYTES):
     spaces = {"s": pltpu.SMEM, "v": pltpu.VMEM}
     late = [(i, kind) for i, kind in enumerate(kinds) if kind not in ("s", "v", "h")]
     early = [i for i, kind in enumerate(out_kinds) if kind == "e"]
 
     def late_shape(i, kind):
-        dims = inputs[i].shape if kind == "l" else (inputs[i].shape[0], kind[1] - kind[0])
+        dims = inputs[i].shape if kind in ("l", "d") else (inputs[i].shape[0], kind[1] - kind[0])
         return pltpu.VMEM(dims, inputs[i].dtype)
 
     def wrapped(*refs):
@@ -116,7 +123,8 @@
         late_v, rest = rest[: len(late)], rest[len(late) :]
         early_v, (late_sem, early_sem) = rest[: len(early)], rest[len(early) :]
         for n, (i, kind) in enumerate(late):
-            ins[i] = Late(ins[i], late_v[n], late_sem.at[n], None if kind == "l" else kind)
+            columns = None if kind in ("l", "d") else kind
+            ins[i] = Late(ins[i], late_v[n], late_sem.at[n], columns, kind == "d" or kind == DEFERRED_COLUMNS)
         for n, i in enumerate(early):
             results[i] = Early(results[i], early_v[n], early_sem.at[n])
         kernel(*ins, *results, *own)
@@ -135,7 +143,7 @@
         + [pltpu.VMEM(outs[i].shape, outs[i].dtype) for i in early]
         + [pltpu.SemaphoreType.DMA((max(1, len(late)),)), pltpu.SemaphoreType.DMA((max(1, len(early)),))],
         compiler_params=pltpu.CompilerParams(
-            collective_id=cid, has_side_effects=True, vmem_limit_bytes=VMEM_BYTES
+            collective_id=cid, has_side_effects=True, vmem_limit_bytes=room
         ),
     )(*inputs)
 
@@ -190,7 +198,7 @@
     )
 
 
-def scatter_plane(me, p_ref, o_ref, far_a, near_a, out_a, sum_a, far_b, near_b, out_b, send, recv):
+def scatter_plane(me, begun, p_ref, o_ref, far_a, near_a, out_a, sum_a, far_b, near_b, out_b, send, recv):
     half = p_ref.vmem.shape[3] // 2
     lower, upper = pl.ds(0, half), pl.ds(half, half)
     axis = (("y", "z"), ("z", "y"))
@@ -218,6 +226,7 @@
                 go(part(t, 2, by, True).at[lower], far_a.at[t, k, 0], t, 0, 1),
                 go(part(t, 2, by, True).at[upper], far_a.at[t, k, 1], t, 0, 3),
             )
+    begun()
     for k, by in enumerate(turns):
         for t in both:
             ahead, behind = part(t, 1, by), part(t, 3, by)
@@ -352,7 +361,7 @@
     lengths_ref, tok_ref, wq_ref, wk_ref, wv_ref, wo_ref, router_ref, gain_one_ref, gain_two_ref,
     order_ref, routes_ref, expand_ref, expand_t_ref, col_ref, row_ref, turn_high_ref, turn_low_ref,
     q_ref, kv_own_ref, gain_ref, cos_ref, sin_ref, w_out_ref, member_ref, put_ref, take_ref,
-    own_aux_ref, order_rows_ref, key_norm_ref, kv_hbm, late_hbm, normed_v, aux_v,
+    own_aux_ref, order_rows_ref, key_norm_ref, heads_ref, kv_hbm, late_hbm, normed_v, aux_v,
     rows_v, w_v, kv_v, long_v, side_v, w_ref, late_ref, send, recv, local,
 ):
     me = position(AXES)
@@ -435,9 +444,8 @@
         low = table(turn_low_ref, jnp.where(lane == (wide & 127), 1.0, 0.0).astype(BF16))
         cos_ref[pl.ds(i * 128, 128), :] = high[:, :128] * low[:, :128] - high[:, 128:] * low[:, 128:]
         sin_ref[pl.ds(i * 128, 128), :] = high[:, 128:] * low[:, :128] + high[:, :128] * low[:, 128:]
-    for i in range(4):
-        order_rows_ref[i : i + 1, 0:128] = mine[2 * i : 2 * i + 1, :].astype(F32)
-        order_rows_ref[i : i + 1, 128:256] = mine[2 * i + 1 : 2 * i + 2, :].astype(F32)
+    heads_ref[...] = order_ref[pl.ds(0, 32, stride=4), :]
+    order_rows_ref[...] = mine.astype(F32)
 
     to_plus.wait()
     next_plus = go(rows_v.at[c, minus, lower], rows_v.at[c, minus, lower], {"x": plus})
@@ -454,7 +462,7 @@
     weights = w_v[...].astype(F32).reshape(D, 384)
     w_out_ref[...] = weights.astype(BF16)
     gain = weights[:, 256:384].T[0:1, :]
-    gain_ref[...] = gain
+    gain_ref[...] = jnp.broadcast_to(gain, (8, D))
     low_lanes = lane_index((256, 128)) < 64
 
     def project(block):
@@ -561,7 +569,7 @@
         [
             shape((2, CHIP_ROWS, 128), BF16),
             shape((CHIP_ROWS, 128), BF16),
-            shape((1, D), F32),
+            shape((8, D), F32),
             shape((CHIP_ROWS, 128), F32),
             shape((CHIP_ROWS, 128), F32),
             shape((D, 384), BF16),
@@ -569,14 +577,15 @@
             shape((SLOTS, ROWS), BF16),
             shape((ROWS, SLOTS), BF16),
             shape((CHIP_ROWS, 128), BF16),
-            shape((4, RUN), F32),
             shape((8, 128), F32),
+            shape((8, 128), F32),
+            shape((32, 128), jnp.int32),
             shape((4, 4, 2, 512, 128), BF16),
             shape((4, 4, 4, 2, 8, 1152), BF16),
             shape((CHIP_ROWS, D), BF16),
             shape((TOKENS, 128), BF16),
         ],
-        ("e", "e", "v", "e", "e", "e", "v", "e", "e", "e", "v", "v", "h", "h", "e", "e"),
+        ("e", "e", "v", "e", "e", "e", "v", "e", "e", "e", "v", "v", "v", "h", "h", "e", "e"),
         [
             pltpu.VMEM((2, 4, ROWS, D), BF16),
             pltpu.VMEM((4, 4, 4, 2, 8, 384), BF16),
@@ -606,7 +615,8 @@
 
 
 def order_pair(order_ref, index):
-    row = jnp.broadcast_to(order_ref[pl.ds(index, 1), :], (RUN, RUN))
+    row = jnp.concatenate([order_ref[pl.ds(2 * index, 1), :], order_ref[pl.ds(2 * index + 1, 1), :]], axis=1)
+    row = jnp.broadcast_to(row, (RUN, RUN))
     return row, row.T
 
 
@@ -616,7 +626,7 @@
 
 def run_lists(order_ref, base, first_ref):
     def note(block, carry):
-        run = lax.shift_right_logical(order_ref[block * 512], 8)
+        run = lax.shift_right_logical(order_ref[block, 0], 8)
         first_ref[run] = block * 512
         first_ref[63 - run] = block * 512 + RUN
         return carry
@@ -624,7 +634,7 @@
     lax.fori_loop(0, 32, note, 0)
 
     def count(part):
-        run = lax.shift_right_logical(order_ref[base + lax.div(part, 2) * 512], 8)
+        run = lax.shift_right_logical(order_ref[lax.div(base, 512) + lax.div(part, 2), 0], 8)
         return jnp.where(lax.rem(part, 2) == 0, run, 31 - run)
 
     return count
@@ -953,8 +963,6 @@
             ((cots_hbm, cots_v), (gate_hbm, gate_v), (up_hbm, up_v), (down_hbm, down_v))
         )
     ]
-    for item in loads:
-        item.start()
     barrier = pltpu.get_barrier_semaphore()
     for by in LINE_OFFSETS:
         pl.semaphore_signal(barrier, inc=1, device_id=moved(me, by), device_id_type=MESH)
@@ -979,6 +987,8 @@
         moves[-1].start()
     kept = pltpu.make_async_copy(sent_ref.at[c_at * 4 + x_at], sent_in.at[here_line], local.at[4])
     kept.start()
+    for item in loads:
+        item.start()
     for item in moves + [kept]:
         item.wait()
     sent = jnp.concatenate([sent_in[i] for i in range(8)], axis=1)
@@ -1324,8 +1334,14 @@
         side += side_rows_ref[i].astype(F32)
     side_ref[...] = side.reshape(16, 8, 128)
     pl.semaphore_wait(barrier, len(offsets) + 16 - alone)
+    def begun():
+        for item in (
+            dq_ref, cos_ref, sin_ref, w_ref, normed_ref, weigh_high_ref, weigh_low_ref, residual_ref
+        ):
+            item.begin()
+
     scatter_plane(
-        me, partial_ref, dkv_ref, far_a, near_a, out_a, sum_a, far_b, near_b, out_b, plane_send, plane_recv
+        me, begun, partial_ref, dkv_ref, far_a, near_a, out_a, sum_a, far_b, near_b, out_b, plane_send, plane_recv
     )
     used = [0]
 
@@ -1471,7 +1487,7 @@
     return remote_call(
         tail_kernel,
         inputs,
-        ("l",) * 8 + ((0, 256), "v", "l", "l", "l"),
+        ("l",) * 4 + ("d",) * 4 + (DEFERRED_COLUMNS, "v", "d", "d", "d"),
         [
             shape((ROWS, D), F32),
             shape((ROWS, D), BF16),
@@ -1509,6 +1525,7 @@
             pltpu.SemaphoreType.DMA((16,)),
         ],
         cid,
+        room=VMEM_BYTES,
     )
 
 
@@ -1520,7 +1537,7 @@
 ):
     tok = tok_ref[...].astype(F32)
     scale = lax.rsqrt(jnp.mean(tok * tok, axis=-1, keepdims=True) + EPSILON)
-    weighted = dnormed_ref[...] * gain_ref[...]
+    weighted = dnormed_ref[...] * gain_ref[0:1, :]
     inner = jnp.mean(weighted * tok, axis=-1, keepdims=True)
     tokens_out[...] = gmid_ref[...] + scale * weighted - tok * (scale * scale * scale) * inner
     mixed_out[...] = mixed_ref[...]
@@ -1536,11 +1553,16 @@
         + jnp.sum(key_out[...] * wk_ref[...].astype(F32), axis=1, keepdims=True)
         + jnp.sum(value_out[...] * wv_ref[...].astype(F32), axis=1, keepdims=True)
     )
-    gain_one = jnp.broadcast_to(total, (8, 128)).T[0:1, :]
+    row = jnp.broadcast_to(own_gain_ref[...].astype(F32), (8, 8))
+    diagonal = lax.broadcasted_iota(jnp.int32, (8, 8), 0) == lane_index((8, 8))
+    total = total / jnp.sum(jnp.where(diagonal, row, 0.0), axis=1, keepdims=True)
     side = early_ref[:, D : D + 128]
-    gain_two = side.T[EXPERTS : EXPERTS + 1, :]
-    gains_out[0:1, :] = gain_one[:, 0:8] / own_gain_ref[...].astype(F32)
-    gains_out[1:2, :] = gain_two[:, 0:8]
+    wide = jnp.broadcast_to(total, (8, 128))
+    blank = jnp.zeros((120, 128), F32)
+    gain_one = jnp.concatenate([wide, blank], axis=0).T[0:1, :]
+    gain_two = jnp.concatenate([side, blank], axis=0).T[EXPERTS : EXPERTS + 1, :]
+    top_row = lax.broadcasted_iota(jnp.int32, (8, 128), 0) == 0
+    gains_out[...] = jnp.where(top_row, jnp.broadcast_to(gain_one, (8, 128)), jnp.broadcast_to(gain_two, (8, 128)))
     grad_out[...] = early_ref[:, 0:D]
     router_out[...] = side[:, 0:EXPERTS]
     gate_out[...] = grads_ref[0:256].astype(F32)
@@ -1574,7 +1596,7 @@
     expand, expand_t = expand_matrix(), expand_matrix().T
     place, place_t = place_matrix(), place_matrix().T
     (
-        query, kv, gain_first, cos, sin, w_mine, member, put, take, own_aux, order_rows, key_norm,
+        query, kv, gain_first, cos, sin, w_mine, member, put, take, own_aux, order_rows, key_norm, heads,
         kv_all, w_late, normed, aux,
     ) = front(
         (
@@ -1590,7 +1612,7 @@
 
     base = first_row.reshape(1).astype(jnp.int32)
     att, norm, sent, query_ext = attend(
-        dealt_order, base, kv_all, aux, kv, own_aux, query, order_rows, key_norm
+        heads, base, kv_all, aux, kv, own_aux, query, order_rows, key_norm
     )
 
     (
@@ -1610,7 +1632,7 @@
     branch_rows = lax.all_gather(branch, ("c", "x"), axis=0, tiled=True)
 
     dq, dkv = attend_back(
-        dealt_order, base, kv_all, aux, kv, own_aux, query_ext, order_rows, gsent_own, att, norm
+        heads, base, kv_all, aux, kv, own_aux, query_ext, order_rows, gsent_own, att, norm
     )
 
     dnormed, mixed, qkv_rows, early = tail(
@@ -1631,7 +1653,7 @@
             shape((8, D), F32),
             shape((8, 512), F32),
             shape((8, 512), F32),
-            shape((2, 8), F32),
+            shape((8, 128), F32),
             shape((8, D), F32),
             shape((8, EXPERTS), F32),
             shape((256, FF), F32),
@@ -1642,7 +1664,7 @@
         dnormed, tokens, gain_first, gmid, mixed, qkv_rows, w_query, w_key, w_value,
         gain_one.reshape(1, 8), early, expert_grads,
     )
-    grad_gain_one, grad_gain_two = gains[0], gains[1]
+    grad_gain_one, grad_gain_two = gains[0, :8], gains[1, :8]
     grad_gate, grad_up, grad_down = grad_gate[None], grad_up[None], grad_down[None]
     return (
         mixed,

time: 292 us -> 292 us (level)
  no operation moved by 1% of the time
where the time goes in v5:
time: 292 us
  Pallas kernels  269 us (92%)
  between operations  13.9 us (5%)
  starting transfers between devices  4.84 us (2%)
    pallas_call x3, Pallas kernels, remote_call(): pl.pallas_call(wrapped, out_shape=list(outs), in_specs=[pl.BlockSpec(memo...  215 us
    pallas_call x1, Pallas kernels, attend_back(): local_call(attend_back_kernel, (shape((CHIP_ROWS, 128), F32), shape((TOKE...  33.9 us
    pallas_call x1, Pallas kernels, attend(): local_call(attend_kernel, (shape((CHIP_ROWS, 128), F32), shape((CHIP_ROWS...  17.2 us
  transfers between devices with their start and end apart: 4, of which 0 were waited for; matrix products, arithmetic and copies ran while one was open for 0% of the time, Pallas kernels for 60%

profile of v5, /device:TPU:1, one launch (start us, length us, event | category | flops | bytes accessed | tf_op | source)
XLA Modules:
  0.0 291.8 jit_solution(11966017481874389483)
XLA Ops:
  7.2 0.0 all-gather.3.cloned.1.call-start
  7.2 0.7 all-gather.3.cloned.1.call-update
  7.9 0.0 all-gather.5.cloned.1.call-start
  8.0 66.8 %shard_map.319 = (bf16[2,1024,128]{2,1,0:T(8,128)(2,1)}, bf16[1024,128]{1,0:T(8,128)(2,1)}, f32[8,1024]{1,0:T(8,128)}, f32[1024,128]{1,0:T(8,128)}, f32[1024,128...) custom-call(s32[5]{0:T(128)} %refs_0_.1, ...), custom_call_target="tpu_custom_call" | custom-call | tf_op jit(solution)/shard_map/pallas_call | solution.py:136
  74.7 17.2 %shard_map.320 = (f32[1024,128]{1,0:T(8,128)}, f32[1024,128]{1,0:T(8,128)}, bf16[1024,128]{1,0:T(8,128)(2,1)}, bf16[4,512,256]{2,1,0:T(8,128)(2,1)}) custom-call(s32[32,128]{1,0:T(8,128)} %get-tuple-element.59.order_smem, s32[1]{0:T(128)} %bitcast.4.base_ref, bf16[16384,128]{1,0:T(8,128)(2,1)} %bitcast.21, bf16[16384,128]{1,0:T(8,128)(2,1)} %get-tuple-element.61.aux_hbm, ...), custom_call_target="tpu_custom_call" | custom-call | tf_op jit(solution)/shard_map/pallas_call | solution.py:731
  91.9 0.0 all-gather.3.cloned.1.call-done
  92.0 91.4 %shard_map.321 = (f32[128,1024]{1,0:T(8,128)}, bf16[128,1152]{1,0:T(8,128)(2,1)}, bf16[128,1152]{1,0:T(8,128)(2,1)}, f32[128,1024]{1,0:T(8,128)}, bf16[128,1024]...) custom-call(bf16[8,128,128]{2,1,0:T(8,128)(2,1)} %bitcast.27, ...), custom_call_target="tpu_custom_call" | custom-call | tf_op jit(solution)/shard_map/pallas_call | solution.py:136
  183.4 0.0 all-gather.5.cloned.1.call-update
  183.4 0.0 reduce-scatter.2.cloned.1.call-start
  183.4 0.7 reduce-scatter.2.cloned.1.call-update
  184.1 4.7 %all-to-all-start = ((bf16[32,36,8,128]{3,2,1,0:T(8,128)(2,1)}), bf16[32,36,8,128]{3,2,1,0:T(8,128)(2,1)S(1)}, u32[]{:S(2)}, u32[]{:S(2)}) async-start(bf16[32,36,8,128]{3,2,1,0:T(8,128)(2,1)} %get-tuple-element.84), calls=%async_computation | async-start | bytes 4718592 | tf_op jit(solution)/shard_map/all_to_all | solution.py:1628
  188.8 33.9 %shard_map.322 = (f32[1024,128]{1,0:T(8,128)}, bf16[16384,128]{1,0:T(8,128)(2,1)}) custom-call(s32[32,128]{1,0:T(8,128)} %get-tuple-element.59.order_smem, s32[1]{0:T(128)} %bitcast.4.base_ref, bf16[16384,128]{1,0:T(8,128)(2,1)} %bitcast.22, bf16[16384,128]{1,0:T(8,128)(2,1)} %get-tuple-element.61.aux_hbm, bf16[1024,128]{1,0:T(8,128)(2,1)} %get-tuple-element.62.own_kv_ref, ...), custom_call_target="tpu_custom_call" | custom-call | tf_op jit(solution)/shard_map/pallas_call | solution.py:862
  222.8 0.0 all-to-all-done.refs_9_
  222.8 0.0 copy-start
  222.8 0.0 all-gather.5.cloned.1.call-done.refs_2_
  222.8 1.4 copy-done
  224.2 56.4 %shard_map.323 = (f32[128,1024]{1,0:T(8,128)}, bf16[128,1024]{1,0:T(8,128)(2,1)}, f32[8,8,256]{2,1,0:T(8,128)}, f32[8,1152]{1,0:T(8,128)}) custom-call(bf16[4,4,2,512,128]{4,3,2,1,0:T(8,128)(2,1)} %bitcast.26, bf16[1024,128]{1,0:T(8,128)(2,1)} %get-tuple-element.68.refs_1_, bf16[1024,1024]{1,0:T(8,128)(2,1)} %all-gather.5.cloned.1.call-done.refs_2_, ...), custom_call_target="tpu_custom_call" | custom-call | tf_op jit(solution)/shard_map/pallas_call | solution.py:136
  280.6 0.0 reduce-scatter.2.cloned.1.call-done.grads_ref
  280.7 3.4 %shard_map.324 = (f32[128,1024]{1,0:T(8,128)}, bf16[128,1024]{1,0:T(8,128)(2,1)}, f32[8,1024]{1,0:T(8,128)}, f32[8,512]{1,0:T(8,128)}, f32[8,512]{1,0:T(8,128)},...) custom-call(f32[128,1024]{1,0:T(8,128)} %get-tuple-element.88.dnorme, ...), custom_call_target="tpu_custom_call" | custom-call | tf_op jit(solution)/shard_map/pallas_call | solution.py:1648
  284.0 1.3 slice_bitcast_fusion
Async XLA Ops:
  7.2 84.8 %all-gather.3.cloned.1.call-start = ((), (), s32[]{:S(2)}) async-start(), calls=%async_computation.2 | async-start | bytes 8650752 | tf_op jit(solution)/shard_map/all_gather | solution.py:1594
  7.9 214.9 %all-gather.5.cloned.1.call-start = ((), (), s32[]{:S(2)}) async-start(), calls=%async_computation.3 | async-start | bytes 2359296 | tf_op jit(solution)/shard_map/all_gather | solution.py:1632
  183.4 97.3 %reduce-scatter.2.cloned.1.call-start = ((), (), s32[]{:S(2)}) async-start(), calls=%async_computation.4 | async-start | bytes 3932160 | tf_op jit(solution)/shard_map/reduce_scatter | solution.py:1629
  184.1 38.7 %all-to-all-start = ((bf16[32,36,8,128]{3,2,1,0:T(8,128)(2,1)}), bf16[32,36,8,128]{3,2,1,0:T(8,128)(2,1)S(1)}, u32[]{:S(2)}, u32[]{:S(2)}) async-start(bf16[32,36,8,128]{3,2,1,0:T(8,128)(2,1)} %get-tuple-element.84), calls=%async_computation | async-start | bytes 4718592 | tf_op jit(solution)/shard_map/all_to_all | solution.py:1628
  222.8 1.4 copy-start
Sparse Core Ops, SparseCore 0:
  10.3 71.2 all-gather.2
  183.5 23.1 all-gather.4
  209.1 38.1 reduce-scatter.1

commit v6 on v5

--- a/solution.py
+++ b/solution.py
@@ -999,16 +999,21 @@
     scale = lax.rsqrt(jnp.mean(residual * residual, axis=-1, keepdims=True) + EPSILON)
     mixed = (residual * scale * gain).astype(BF16)
     mixed_v[...] = mixed
-    put = put_ref[...]
-
     def tiles(value):
         return value.reshape(8, SLOT, 8, 128).astype(BF16)
 
     def rows_of(value):
         return value.astype(F32).reshape(value.shape[0] * SLOT, D).astype(BF16)
 
-    for i in range(4):
-        x_out[i * 8 : (i + 1) * 8] = tiles(mm(put[i * BLOCK : (i + 1) * BLOCK], mixed))
+    def plane_of(by):
+        plane = lax.rem(y_at + by, 4)
+        return pl.ds(plane * 8, 8), pl.ds(pl.multiple_of(plane * BLOCK, 32), BLOCK)
+
+    def build(by):
+        experts, rows = plane_of(by)
+        x_out[experts] = tiles(mm(put_ref[rows, :], mixed))
+
+    build(2)
 
     def x_copy(k):
         to = toward(k)
@@ -1022,7 +1027,10 @@
         x_copy(k).start()
         return carry
 
-    lax.fori_loop(0, 8, x_start, 0)
+    lax.fori_loop(0, 6, x_start, 0)
+    for by in (3, 1, 0):
+        build(by)
+    lax.fori_loop(6, 8, x_start, 0)
     kept = pltpu.make_async_copy(x_out.at[expert], x_in.at[31], local.at[4])
     kept.start()
     logits = mm(mixed, router_ref[...])
@@ -1188,10 +1196,19 @@
         back_copy(k).wait()
         return carry
 
-    lax.fori_loop(0, 31, settle, 0)
+    def add(by):
+        experts, rows = plane_of(by)
+        return mm(put_ref[rows, :], rows_of(back_in[experts]), TN)
+
+    lax.fori_loop(0, 6, settle, 0)
+    lax.fori_loop(12, 14, settle, 0)
+    dmixed += add(2)
+    lax.fori_loop(6, 12, settle, 0)
+    lax.fori_loop(14, 31, settle, 0)
     back_kept().wait()
-
-    dmixed += mm(take, rows_of(back_in[...]))
+    for by in (3, 1, 0):
+        dmixed += add(by)
+
     residual = residual_ref[...]
     scale = lax.rsqrt(jnp.mean(residual * residual, axis=-1, keepdims=True) + EPSILON)
     gain = router_ref[...].astype(F32).T[EXPERTS : EXPERTS + 1, :]

time: 292 us -> 292 us (level)
  Pallas kernels: 269 us -> 266 us
  starting transfers between devices: 4.84 us -> 7.79 us
    pallas_call x3, Pallas kernels: 215 us -> 211 us  [remote_call(): pl.pallas_call(wrapped, out_shape=list(outs), in_specs=[pl.BlockSpec(memo...]
    all_to_all x1, starting transfers between devices: 4.73 us -> 7.67 us  [body(): y_in = lax.all_to_all(y_out, plane, split_axis=0, concat_axis=0, tiled=True)]
where the time goes in v6:
time: 292 us; the launch traced here: 291 us
  Pallas kernels  266 us (91%)
  between operations  13.9 us (5%)
  starting transfers between devices  7.79 us (3%)
    pallas_call x3, Pallas kernels, remote_call(): pl.pallas_call(wrapped, out_shape=list(outs), in_specs=[pl.BlockSpec(memo...  211 us
    pallas_call x1, Pallas kernels, attend_back(): local_call(attend_back_kernel, (shape((CHIP_ROWS, 128), F32), shape((TOKE...  33.9 us
    pallas_call x1, Pallas kernels, attend(): local_call(attend_kernel, (shape((CHIP_ROWS, 128), F32), shape((CHIP_ROWS...  17.2 us
    all_to_all x1, starting transfers between devices, body(): y_in = lax.all_to_all(y_out, plane, split_axis=0, concat_axis=0, tiled=True)  7.67 us
  transfers between devices with their start and end apart: 4, of which 0 were waited for; matrix products, arithmetic and copies ran while one was open for 0% of the time, Pallas kernels for 60%

profile of v6, /device:TPU:1, one launch (start us, length us, event | category | flops | bytes accessed | tf_op | source)
XLA Modules:
  0.0 291.5 jit_solution(5160370458061391088)
XLA Ops:
  7.2 0.0 all-gather.3.cloned.1.call-start
  7.2 0.7 all-gather.3.cloned.1.call-update
  7.9 0.0 all-gather.5.cloned.1.call-start
  8.0 66.8 %shard_map.319 = (bf16[2,1024,128]{2,1,0:T(8,128)(2,1)}, bf16[1024,128]{1,0:T(8,128)(2,1)}, f32[8,1024]{1,0:T(8,128)}, f32[1024,128]{1,0:T(8,128)}, f32[1024,128...) custom-call(s32[5]{0:T(128)} %refs_0_.1, ...), custom_call_target="tpu_custom_call" | custom-call | tf_op jit(solution)/shard_map/pallas_call | solution.py:136
  74.7 17.2 %shard_map.320 = (f32[1024,128]{1,0:T(8,128)}, f32[1024,128]{1,0:T(8,128)}, bf16[1024,128]{1,0:T(8,128)(2,1)}, bf16[4,512,256]{2,1,0:T(8,128)(2,1)}) custom-call(s32[32,128]{1,0:T(8,128)} %get-tuple-element.59.order_smem, s32[1]{0:T(128)} %bitcast.4.base_ref, bf16[16384,128]{1,0:T(8,128)(2,1)} %bitcast.21, bf16[16384,128]{1,0:T(8,128)(2,1)} %get-tuple-element.61.aux_hbm, ...), custom_call_target="tpu_custom_call" | custom-call | tf_op jit(solution)/shard_map/pallas_call | solution.py:731
  91.9 0.0 all-gather.3.cloned.1.call-done
  92.0 88.0 %shard_map.321 = (f32[128,1024]{1,0:T(8,128)}, bf16[128,1152]{1,0:T(8,128)(2,1)}, bf16[128,1152]{1,0:T(8,128)(2,1)}, f32[128,1024]{1,0:T(8,128)}, bf16[128,1024]...) custom-call(bf16[8,128,128]{2,1,0:T(8,128)(2,1)} %bitcast.27, ...), custom_call_target="tpu_custom_call" | custom-call | tf_op jit(solution)/shard_map/pallas_call | solution.py:136
  180.0 0.0 all-gather.5.cloned.1.call-update
  180.0 0.0 reduce-scatter.2.cloned.1.call-start
  180.0 0.7 reduce-scatter.2.cloned.1.call-update
  180.7 7.7 %all-to-all-start = ((bf16[32,36,8,128]{3,2,1,0:T(8,128)(2,1)}), bf16[32,36,8,128]{3,2,1,0:T(8,128)(2,1)S(1)}, u32[]{:S(2)}, u32[]{:S(2)}) async-start(bf16[32,36,8,128]{3,2,1,0:T(8,128)(2,1)} %get-tuple-element.84), calls=%async_computation | async-start | bytes 4718592 | tf_op jit(solution)/shard_map/all_to_all | solution.py:1645
  188.4 33.9 %shard_map.322 = (f32[1024,128]{1,0:T(8,128)}, bf16[16384,128]{1,0:T(8,128)(2,1)}) custom-call(s32[32,128]{1,0:T(8,128)} %get-tuple-element.59.order_smem, s32[1]{0:T(128)} %bitcast.4.base_ref, bf16[16384,128]{1,0:T(8,128)(2,1)} %bitcast.22, bf16[16384,128]{1,0:T(8,128)(2,1)} %get-tuple-element.61.aux_hbm, bf16[1024,128]{1,0:T(8,128)(2,1)} %get-tuple-element.62.own_kv_ref, ...), custom_call_target="tpu_custom_call" | custom-call | tf_op jit(solution)/shard_map/pallas_call | solution.py:862
  222.3 0.0 all-to-all-done.refs_9_
  222.4 0.0 copy-start
  222.4 0.0 all-gather.5.cloned.1.call-done.refs_2_
  222.4 1.4 copy-done
  223.8 56.5 %shard_map.323 = (f32[128,1024]{1,0:T(8,128)}, bf16[128,1024]{1,0:T(8,128)(2,1)}, f32[8,8,256]{2,1,0:T(8,128)}, f32[8,1152]{1,0:T(8,128)}) custom-call(bf16[4,4,2,512,128]{4,3,2,1,0:T(8,128)(2,1)} %bitcast.26, bf16[1024,128]{1,0:T(8,128)(2,1)} %get-tuple-element.68.refs_1_, bf16[1024,1024]{1,0:T(8,128)(2,1)} %all-gather.5.cloned.1.call-done.refs_2_, ...), custom_call_target="tpu_custom_call" | custom-call | tf_op jit(solution)/shard_map/pallas_call | solution.py:136
  280.3 0.0 reduce-scatter.2.cloned.1.call-done.grads_ref
  280.3 3.4 %shard_map.324 = (f32[128,1024]{1,0:T(8,128)}, bf16[128,1024]{1,0:T(8,128)(2,1)}, f32[8,1024]{1,0:T(8,128)}, f32[8,512]{1,0:T(8,128)}, f32[8,512]{1,0:T(8,128)},...) custom-call(f32[128,1024]{1,0:T(8,128)} %get-tuple-element.88.dnorme, ...), custom_call_target="tpu_custom_call" | custom-call | tf_op jit(solution)/shard_map/pallas_call | solution.py:1665
  283.7 1.3 slice_bitcast_fusion
Async XLA Ops:
  7.2 84.8 %all-gather.3.cloned.1.call-start = ((), (), s32[]{:S(2)}) async-start(), calls=%async_computation.2 | async-start | bytes 8650752 | tf_op jit(solution)/shard_map/all_gather | solution.py:1611
  7.9 214.5 %all-gather.5.cloned.1.call-start = ((), (), s32[]{:S(2)}) async-start(), calls=%async_computation.3 | async-start | bytes 2359296 | tf_op jit(solution)/shard_map/all_gather | solution.py:1649
  180.0 100.3 %reduce-scatter.2.cloned.1.call-start = ((), (), s32[]{:S(2)}) async-start(), calls=%async_computation.4 | async-start | bytes 3932160 | tf_op jit(solution)/shard_map/reduce_scatter | solution.py:1646
  180.7 41.6 %all-to-all-start = ((bf16[32,36,8,128]{3,2,1,0:T(8,128)(2,1)}), bf16[32,36,8,128]{3,2,1,0:T(8,128)(2,1)S(1)}, u32[]{:S(2)}, u32[]{:S(2)}) async-start(bf16[32,36,8,128]{3,2,1,0:T(8,128)(2,1)} %get-tuple-element.84), calls=%async_computation | async-start | bytes 4718592 | tf_op jit(solution)/shard_map/all_to_all | solution.py:1645
  222.4 1.4 copy-start
Sparse Core Ops, SparseCore 0:
  10.3 71.2 all-gather.2
  180.1 26.1 all-gather.4
  208.7 38.1 reduce-scatter.1
